TPU v7x, 512 devices: a whole 4x8x8 slice. The times are simulated.
512 devices in a mesh: leaf: 128 (over z, y, core), sub: 4 (over x).
Axes of the slice: x: 4, y: 8, z: 8, core: 2. Of those that a mesh axis runs over, the one named last changes fastest.
Arguments:
- density: bfloat16 [2, 128, 524288], P(None, None, ('leaf', 'sub')), may hold values from -6 to 6
- coords: bfloat16 [3, 524288], P(None, ('leaf', 'sub')), may hold values from -3 to 3
- weights: bfloat16 [524288], P(('leaf', 'sub')), may hold values from 0.033935547 to 0.33984375
- counts: int32 [4096], P(('leaf', 'sub')), may hold values from 1 to 27, as said below
- neighbors: int32 [4096, 27], P(('leaf', 'sub')), may hold values from 0 to 11, as said below
- skeleton: int32 [512, 128], P(('leaf', 'sub')), may hold values from 0 to 1023
- compress: bfloat16 [2, 128, 524288], P(None, None, ('leaf', 'sub')), may hold values from -0.125 to 0.125
- mix: bfloat16 [512, 9, 2, 2, 128, 128], P(('leaf', 'sub')), may hold values from -0.25 to 0.25
- expand: bfloat16 [2, 128, 524288], P(None, None, ('leaf', 'sub')), may hold values from -0.375 to 0.375
Outputs:
- field: bfloat16 [2, 128, 524288], P(None, None, ('leaf', 'sub'))
Inputs may be any that keep to these rules, and one draw needn't show every extreme that they name: `counts`: each box's count of live near-field boxes; box 0 has exactly 27. `neighbors`: slot 0 of each device's last box is 10, slot 0 of each device's first box is 1.
All inputs are finite; a program needn't handle non-finite values.
Results may differ from a plain program's by a relative error of at most 0.024.
Values may be sent and summed in bfloat16 or wider, within the bound.
No kernel may reach another device: no remote copies, remote signals or barrier semaphores. Data moves between devices by JAX's collectives and lax.ppermute only.
A program may use at most 64 MiB of HBM per device.

v0:
```python
import math

import jax
import jax.numpy as jnp
from jax import lax
from jax.sharding import PartitionSpec as P

HB = 2


WAVE_NUMBER = 2.0 * math.pi
SOFTENING = 0.05
FOUR_PI = 4.0 * math.pi


def padded(cells, sides, width):
    for axis, dim in sides:
        count = lax.axis_size(axis)
        ends = count - 1
        head = lax.slice_in_dim(cells, 0, width, axis=dim)
        tail = lax.slice_in_dim(cells, cells.shape[dim] - width, cells.shape[dim], axis=dim)
        cells = jnp.concatenate(
            [
                lax.ppermute(tail, axis, [(i, (i + 1) % count) for i in range(ends)]),
                cells,
                lax.ppermute(head, axis, [((i + 1) % count, i) for i in range(ends)]),
            ],
            axis=dim,
        )
    return cells


def from_partner(value, axis, stride):
    mask = 2**stride
    pairs = [(source, source ^ mask) for source in range(lax.axis_size(axis))]
    return lax.ppermute(value, axis, pairs)


def kernel_tiles(target, source, src_weight, live):
    spread = target[:, :, :, None] - source[:, :, None, :]
    radius = jnp.sqrt(jnp.sum(spread * spread, axis=1) + SOFTENING * SOFTENING)
    amplitude = live[:, None, None] * src_weight[:, None, :] / (FOUR_PI * radius)
    return jnp.stack(
        [amplitude * jnp.cos(WAVE_NUMBER * radius), amplitude * jnp.sin(WAVE_NUMBER * radius)]
    ).astype(jnp.bfloat16)


def near_product(tiles, sources):
    parts = jnp.einsum("jkts,pcks->jpct", tiles, sources, preferred_element_type=jnp.float32)
    return jnp.stack([parts[0, 0] - parts[1, 1], parts[0, 1] + parts[1, 0]])


def pair_product(left, right):
    columns = left.shape[1]
    rank_rows = right.shape[1]
    product = lax.dot_general(
        left.reshape(2 * columns, -1),
        right.reshape(2 * rank_rows, -1),
        (((1,), (1,)), ((), ())),
        preferred_element_type=jnp.float32,
    )
    real = product[:columns, :rank_rows] - product[columns:, rank_rows:]
    imag = product[:columns, rank_rows:] + product[columns:, :rank_rows]
    return jnp.stack([real, imag])


def expand_product(left, right):
    columns = left.shape[1]
    product = lax.dot_general(
        left.reshape(2 * columns, -1),
        right,
        (((1,), (1,)), ((), ())),
        preferred_element_type=jnp.float32,
    )
    real = product[:columns, 0] - product[columns:, 1]
    imag = product[:columns, 1] + product[columns:, 0]
    return jnp.stack([real, imag])


def combine(own, other, matrices):
    return (pair_product(own, matrices[0]) + pair_product(other, matrices[1])).astype(jnp.bfloat16)


def per_device(density, coords, weights, counts, neighbors, skeleton, compress, mix, expand):
    columns = density.shape[1]
    panels = density.shape[2]
    box_count = counts.shape[0]
    box_size = panels // box_count
    slot_count = neighbors.shape[1]
    wide_boxes = box_count + 2 * HB
    geometry = jnp.concatenate(
        [density.reshape(2 * columns, panels), coords, weights[None, :]], axis=0
    )
    widened = padded(geometry, ((("leaf", "sub"), 1),), HB * box_size)
    wide_density = widened[: 2 * columns].reshape(2, columns, wide_boxes, box_size)
    wide_coords = (
        widened[2 * columns : 2 * columns + 3].astype(jnp.float32).reshape(3, wide_boxes, box_size)
    )
    wide_weight = widened[2 * columns + 3].astype(jnp.float32).reshape(wide_boxes, box_size)
    own_coords = coords.astype(jnp.float32).reshape(3, box_count, box_size)
    slot_ids = jnp.arange(slot_count, dtype=jnp.int32)
    picked = jnp.take(density, skeleton[0], axis=2).astype(jnp.float32)
    state = (picked + pair_product(density, compress)).astype(jnp.bfloat16)
    sub_levels = lax.axis_size("sub").bit_length() - 1
    leaf_levels = lax.axis_size("leaf").bit_length() - 1
    for level in range(sub_levels):
        other = from_partner(state, "sub", level)
        state = combine(state, other, mix[0, level])
    for level in range(leaf_levels):
        other = from_partner(state, "leaf", level)
        state = combine(state, other, mix[0, sub_levels + level])
    far = expand_product(state, expand)

    def box_term(local_box):
        slots = neighbors[local_box]
        live = (slot_ids < counts[local_box]).astype(jnp.float32)
        target = jnp.broadcast_to(own_coords[:, local_box][None], (slot_count, 3, box_size))
        source = jnp.transpose(wide_coords[:, slots], (1, 0, 2))
        tiles = kernel_tiles(target, source, wide_weight[slots], live)
        return near_product(tiles, jnp.take(wide_density, slots, axis=2))

    near = lax.map(box_term, jnp.arange(box_count, dtype=jnp.int32))
    near = jnp.transpose(near, (1, 2, 0, 3)).reshape(2, columns, panels)
    return (far + near).astype(jnp.bfloat16)


def solution(mesh):
    return jax.shard_map(
        per_device,
        mesh=mesh,
        in_specs=(
            P(None, None, ("leaf", "sub")),
            P(None, ("leaf", "sub")),
            P(("leaf", "sub")),
            P(("leaf", "sub")),
            P(("leaf", "sub"), None),
            P(("leaf", "sub"), None),
            P(None, None, ("leaf", "sub")),
            P(("leaf", "sub"), None, None, None, None, None),
            P(None, None, ("leaf", "sub")),
        ),
        out_specs=P(None, None, ("leaf", "sub")),
        check_vma=False,
    )
```

profile of v0, /device:TPU:2, one launch (start us, length us, event | category | flops | bytes accessed | tf_op | source)
XLA Modules:
  0.0 244.5 jit_solution(14274689452713318895)
XLA Ops:
  0.8 1.7 pad_maximum_fusion.3
  2.5 3.4 %collective-permute-start.9 = (bf16[260,256]{1,0:T(8,128)(2,1)}, bf16[260,256]{1,0:T(8,128)(2,1)S(1)}, u32[]{:S(2)}, u32[]{:S(2)}) collective-permute-start(bf16[260,256]{1,0:T(8,128)(2,1)} %get-tuple-element.145), channel_id=1, source_target_pairs={{0,1},{1,2},{2,3},{3,4},{4,5},{5,6},{6,7},{7,8},{8,9},{9,10},{10,1... | collective-permute-start | bytes 399368 | tf_op jit(solution)/shard_map/ppermute | solution.py:24
  5.9 5.7 %collective-permute-start.10 = (bf16[260,256]{1,0:T(8,128)(2,1)}, bf16[260,256]{1,0:T(8,128)(2,1)S(1)}, u32[]{:S(2)}, u32[]{:S(2)}) collective-permute-start(bf16[260,256]{1,0:T(8,128)(2,1)} %get-tuple-element.146), channel_id=1, source_target_pairs={{1,0},{2,1},{3,2},{4,3},{5,4},{6,5},{7,6},{8,7},{9,8},{10,9},{11,1... | collective-permute-start | bytes 399368 | tf_op jit(solution)/shard_map/ppermute | solution.py:26
  13.0 1.3 copy.36
  15.6 1.9 collective-permute-start
  17.5 2.1 fusion.71
  19.9 1.9 collective-permute-done
  22.0 1.9 collective-permute-start.1
  24.2 5.5 %collective-permute-done.1 = bf16[2,128,128]{2,1,0:T(8,128)(2,1)S(1)} collective-permute-done((bf16[2,128,128]{2,1,0:T(8,128)(2,1)S(1)}, bf16[2,128,128]{2,1,0:T(8,128)(2,1)S(1)}, u32[]{:S(2)}, u32[]{:S(2)}) %collective-permute-start.1) | collective-permute-done | bytes 65568 | tf_op jit(solution)/shard_map/ppermute | solution.py:36
  30.5 1.9 collective-permute-start.2
  32.5 1.0 fusion.77
  35.5 150.4 %while.11 = (s32[]{:T(128)}, f32[8,2,128,128]{3,2,1,0:T(8,128)}, s32[8]{0:T(128)S(1)}, s32[8,27]{1,0:T(8,128)}, bf16[2,128,12,128]{3,1,2,0:T(8,128)(2,1)S(1)}, /...) while((s32[]{:T(128)}, f32[8,2,128,128]{3,2,1,0:T(8,128)}, ...), condition=%wide.region_2.3_spmd.clone, body=%wide.region_0.0_spmd.clone.sunk | while | flops 464556704 | bytes 13507277 | solution.py:122
  42.6 8.0 %fusion.142 = (bf16[1,27,128,128]{3,2,1,0:T(8,128)(2,1)}, bf16[1,27,128,128]{3,2,1,0:T(8,128)(2,1)}) fusion(f32[27,128,128]{2,1,0:T(8,128)S(1)} %multiply_reduce_fusion.2, f32[27,128]{1,0:T(8,128)S(1)} %broadcast_multiply_fusion.2), kind=kLoop, calls=%fused_computation.13.clone.1 | loop fusion | flops 3538944 | bytes 3552768 | tf_op jit(solution)/shard_map/convert
  50.6 0.9 gather_fusion.2
  51.5 2.1 fusion.143
  61.4 8.0 %fusion.142 = (bf16[1,27,128,128]{3,2,1,0:T(8,128)(2,1)}, bf16[1,27,128,128]{3,2,1,0:T(8,128)(2,1)}) fusion(f32[27,128,128]{2,1,0:T(8,128)S(1)} %multiply_reduce_fusion.2, f32[27,128]{1,0:T(8,128)S(1)} %broadcast_multiply_fusion.2), kind=kLoop, calls=%fused_computation.13.clone.1 | loop fusion | flops 3538944 | bytes 3552768 | tf_op jit(solution)/shard_map/convert
  69.3 0.9 gather_fusion.2
  70.2 2.1 fusion.143
  80.2 8.0 %fusion.142 = (bf16[1,27,128,128]{3,2,1,0:T(8,128)(2,1)}, bf16[1,27,128,128]{3,2,1,0:T(8,128)(2,1)}) fusion(f32[27,128,128]{2,1,0:T(8,128)S(1)} %multiply_reduce_fusion.2, f32[27,128]{1,0:T(8,128)S(1)} %broadcast_multiply_fusion.2), kind=kLoop, calls=%fused_computation.13.clone.1 | loop fusion | flops 3538944 | bytes 3552768 | tf_op jit(solution)/shard_map/convert
  88.1 0.9 gather_fusion.2
  89.0 2.1 fusion.143
  99.0 8.0 %fusion.142 = (bf16[1,27,128,128]{3,2,1,0:T(8,128)(2,1)}, bf16[1,27,128,128]{3,2,1,0:T(8,128)(2,1)}) fusion(f32[27,128,128]{2,1,0:T(8,128)S(1)} %multiply_reduce_fusion.2, f32[27,128]{1,0:T(8,128)S(1)} %broadcast_multiply_fusion.2), kind=kLoop, calls=%fused_computation.13.clone.1 | loop fusion | flops 3538944 | bytes 3552768 | tf_op jit(solution)/shard_map/convert
  106.9 0.9 gather_fusion.2
  107.8 2.1 fusion.143
  117.8 8.0 %fusion.142 = (bf16[1,27,128,128]{3,2,1,0:T(8,128)(2,1)}, bf16[1,27,128,128]{3,2,1,0:T(8,128)(2,1)}) fusion(f32[27,128,128]{2,1,0:T(8,128)S(1)} %multiply_reduce_fusion.2, f32[27,128]{1,0:T(8,128)S(1)} %broadcast_multiply_fusion.2), kind=kLoop, calls=%fused_computation.13.clone.1 | loop fusion | flops 3538944 | bytes 3552768 | tf_op jit(solution)/shard_map/convert
  125.7 0.9 gather_fusion.2
  126.6 2.1 fusion.143
  136.6 8.0 %fusion.142 = (bf16[1,27,128,128]{3,2,1,0:T(8,128)(2,1)}, bf16[1,27,128,128]{3,2,1,0:T(8,128)(2,1)}) fusion(f32[27,128,128]{2,1,0:T(8,128)S(1)} %multiply_reduce_fusion.2, f32[27,128]{1,0:T(8,128)S(1)} %broadcast_multiply_fusion.2), kind=kLoop, calls=%fused_computation.13.clone.1 | loop fusion | flops 3538944 | bytes 3552768 | tf_op jit(solution)/shard_map/convert
  145.4 2.1 fusion.143
  155.4 8.0 %fusion.142 = (bf16[1,27,128,128]{3,2,1,0:T(8,128)(2,1)}, bf16[1,27,128,128]{3,2,1,0:T(8,128)(2,1)}) fusion(f32[27,128,128]{2,1,0:T(8,128)S(1)} %multiply_reduce_fusion.2, f32[27,128]{1,0:T(8,128)S(1)} %broadcast_multiply_fusion.2), kind=kLoop, calls=%fused_computation.13.clone.1 | loop fusion | flops 3538944 | bytes 3552768 | tf_op jit(solution)/shard_map/convert
  164.2 2.1 fusion.143
  174.2 8.0 %fusion.142 = (bf16[1,27,128,128]{3,2,1,0:T(8,128)(2,1)}, bf16[1,27,128,128]{3,2,1,0:T(8,128)(2,1)}) fusion(f32[27,128,128]{2,1,0:T(8,128)S(1)} %multiply_reduce_fusion.2, f32[27,128]{1,0:T(8,128)S(1)} %broadcast_multiply_fusion.2), kind=kLoop, calls=%fused_computation.13.clone.1 | loop fusion | flops 3538944 | bytes 3552768 | tf_op jit(solution)/shard_map/convert
  183.0 2.1 fusion.143
  185.9 1.1 fusion.78
  187.0 0.9 fusion.23
  187.9 1.9 collective-permute-start.3
  190.0 4.2 %collective-permute-done.3 = bf16[2,128,128]{2,1,0:T(8,128)(2,1)S(1)} collective-permute-done((bf16[2,128,128]{2,1,0:T(8,128)(2,1)S(1)}, bf16[2,128,128]{2,1,0:T(8,128)(2,1)S(1)}, u32[]{:S(2)}, u32[]{:S(2)}) %collective-permute-start.3) | collective-permute-done | bytes 65568 | tf_op jit(solution)/shard_map/ppermute | solution.py:36
  194.5 1.9 collective-permute-start.4
  196.7 5.7 %collective-permute-done.4 = bf16[2,128,128]{2,1,0:T(8,128)(2,1)S(1)} collective-permute-done((bf16[2,128,128]{2,1,0:T(8,128)(2,1)S(1)}, bf16[2,128,128]{2,1,0:T(8,128)(2,1)S(1)}, u32[]{:S(2)}, u32[]{:S(2)}) %collective-permute-start.4) | collective-permute-done | bytes 65568 | tf_op jit(solution)/shard_map/ppermute | solution.py:36
  202.6 6.2 %collective-permute-start.5 = (bf16[2,128,128]{2,1,0:T(8,128)(2,1)S(1)}, bf16[2,128,128]{2,1,0:T(8,128)(2,1)S(1)}, u32[]{:S(2)}, u32[]{:S(2)}) collective-permute-start(bf16[2,128,128]{2,1,0:T(8,128)(2,1)S(1)} %fusion.25), channel_id=1, source_target_pairs={{0,32},{4,36},{8,40},{12,44},{16,48},{20,52},{24,56},{28,60},{32,0... | collective-permute-start | bytes 196616 | tf_op jit(solution)/shard_map/ppermute | solution.py:36
  209.0 3.9 %collective-permute-done.5 = bf16[2,128,128]{2,1,0:T(8,128)(2,1)S(1)} collective-permute-done((bf16[2,128,128]{2,1,0:T(8,128)(2,1)S(1)}, bf16[2,128,128]{2,1,0:T(8,128)(2,1)S(1)}, u32[]{:S(2)}, u32[]{:S(2)}) %collective-permute-start.5) | collective-permute-done | bytes 65568 | tf_op jit(solution)/shard_map/ppermute | solution.py:36
  213.2 4.0 %collective-permute-start.6 = (bf16[2,128,128]{2,1,0:T(8,128)(2,1)S(1)}, bf16[2,128,128]{2,1,0:T(8,128)(2,1)S(1)}, u32[]{:S(2)}, u32[]{:S(2)}) collective-permute-start(bf16[2,128,128]{2,1,0:T(8,128)(2,1)S(1)} %fusion.26), channel_id=1, source_target_pairs={{0,64},{4,68},{8,72},{12,76},{16,80},{20,84},{24,88},{28,92},{32,9... | collective-permute-start | bytes 196616 | tf_op jit(solution)/shard_map/ppermute | solution.py:36
  217.5 2.0 collective-permute-done.6
  219.7 6.1 %collective-permute-start.7 = (bf16[2,128,128]{2,1,0:T(8,128)(2,1)S(1)}, bf16[2,128,128]{2,1,0:T(8,128)(2,1)S(1)}, u32[]{:S(2)}, u32[]{:S(2)}) collective-permute-start(bf16[2,128,128]{2,1,0:T(8,128)(2,1)S(1)} %fusion.27), channel_id=1, source_target_pairs={{0,128},{4,132},{8,136},{12,140},{16,144},{20,148},{24,152},{28,15... | collective-permute-start | bytes 196616 | tf_op jit(solution)/shard_map/ppermute | solution.py:36
  226.1 2.0 collective-permute-done.7
  228.3 10.9 %collective-permute-start.8 = (bf16[2,128,128]{2,1,0:T(8,128)(2,1)S(1)}, bf16[2,128,128]{2,1,0:T(8,128)(2,1)S(1)}, u32[]{:S(2)}, u32[]{:S(2)}) collective-permute-start(bf16[2,128,128]{2,1,0:T(8,128)(2,1)S(1)} %fusion.28), channel_id=1, source_target_pairs={{0,256},{4,260},{8,264},{12,268},{16,272},{20,276},{24,280},{28,28... | collective-permute-start | bytes 196616 | tf_op jit(solution)/shard_map/ppermute | solution.py:36
  239.4 2.0 collective-permute-done.8
  242.3 2.1 fusion.17
  (207 shorter events, 59.2 us)
Async XLA Ops:
  0.0 241.7 %copy-start = (bf16[2,128,1024]{2,1,0:T(8,128)(2,1)S(1)}, bf16[2,128,1024]{2,1,0:T(8,128)(2,1)}, u32[]{:S(2)}) copy-start(bf16[2,128,1024]{2,1,0:T(8,128)(2,1)} %param.19) | copy-start | bytes 1572868
  0.0 14.3 %copy-start.1 = (bf16[2,128,1024]{2,1,0:T(8,128)(2,1)S(1)}, bf16[2,128,1024]{2,1,0:T(8,128)(2,1)}, u32[]{:S(2)}) copy-start(bf16[2,128,1024]{2,1,0:T(8,128)(2,1)} %param.11) | copy-start | bytes 1572868
  0.0 14.3 %copy-start.2 = (bf16[2,128,1024]{2,1,0:T(8,128)(2,1)S(1)}, bf16[2,128,1024]{2,1,0:T(8,128)(2,1)}, u32[]{:S(2)}) copy-start(bf16[2,128,1024]{2,1,0:T(8,128)(2,1)} %param.17) | copy-start | bytes 1572868
  2.5 31.6 %collective-permute-start.9 = (bf16[260,256]{1,0:T(8,128)(2,1)}, bf16[260,256]{1,0:T(8,128)(2,1)S(1)}, u32[]{:S(2)}, u32[]{:S(2)}) collective-permute-start(bf16[260,256]{1,0:T(8,128)(2,1)} %get-tuple-element.145), channel_id=1, source_target_pairs={{0,1},{1,2},{2,3},{3,4},{4,5},{5,6},{6,7},{7,8},{8,9},{9,10},{10,1... | collective-permute-start | bytes 399368 | tf_op jit(solution)/shard_map/ppermute | solution.py:24
  5.9 28.2 %collective-permute-start.10 = (bf16[260,256]{1,0:T(8,128)(2,1)}, bf16[260,256]{1,0:T(8,128)(2,1)S(1)}, u32[]{:S(2)}, u32[]{:S(2)}) collective-permute-start(bf16[260,256]{1,0:T(8,128)(2,1)} %get-tuple-element.146), channel_id=1, source_target_pairs={{1,0},{2,1},{3,2},{4,3},{5,4},{6,5},{7,6},{8,7},{9,8},{10,9},{11,1... | collective-permute-start | bytes 399368 | tf_op jit(solution)/shard_map/ppermute | solution.py:26
  14.7 5.2 %copy-start.12 = (bf16[3,1024]{1,0:T(4,128)(2,1)S(1)}, bf16[3,1024]{1,0:T(4,128)(2,1)}, u32[]{:S(2)}) copy-start(bf16[3,1024]{1,0:T(4,128)(2,1)} %param.12) | copy-start | bytes 18436
  15.6 6.2 %collective-permute-start = (bf16[2,128,128]{2,1,0:T(8,128)(2,1)S(1)}, bf16[2,128,128]{2,1,0:T(8,128)(2,1)S(1)}, u32[]{:S(2)}, u32[]{:S(2)}) collective-permute-start(bf16[2,128,128]{2,1,0:T(8,128)(2,1)S(1)} %fusion.20), channel_id=1, source_target_pairs={{0,1},{1,0},{2,3},{3,2},{4,5},{5,4},{6,7},{7,6},{8,9},{9,8},{10,11... | collective-permute-start | bytes 196616 | tf_op jit(solution)/shard_map/ppermute | solution.py:36
  22.0 7.7 %collective-permute-start.1 = (bf16[2,128,128]{2,1,0:T(8,128)(2,1)S(1)}, bf16[2,128,128]{2,1,0:T(8,128)(2,1)S(1)}, u32[]{:S(2)}, u32[]{:S(2)}) collective-permute-start(bf16[2,128,128]{2,1,0:T(8,128)(2,1)S(1)} %fusion.21), channel_id=1, source_target_pairs={{0,2},{1,3},{2,0},{3,1},{4,6},{5,7},{6,4},{7,5},{8,10},{9,11},{10,... | collective-permute-start | bytes 196616 | tf_op jit(solution)/shard_map/ppermute | solution.py:36
  30.5 155.3 %collective-permute-start.2 = (bf16[2,128,128]{2,1,0:T(8,128)(2,1)}, bf16[2,128,128]{2,1,0:T(8,128)(2,1)}, u32[]{:S(2)}, u32[]{:S(2)}) collective-permute-start(bf16[2,128,128]{2,1,0:T(8,128)(2,1)} %fusion.22), channel_id=1, source_target_pairs={{0,4},{4,0},{8,12},{12,8},{16,20},{20,16},{24,28},{28,24},{32,36},... | collective-permute-start | bytes 196616 | tf_op jit(solution)/shard_map/ppermute | solution.py:36
  34.8 0.7 copy-start.13
  35.5 150.4 %copy-start.11 = (bf16[1,1,1,2,128,128]{5,4,3,2,1,0:T(8,128)(2,1)S(1)}, bf16[1,1,1,2,128,128]{5,4,3,2,1,0:T(8,128)(2,1)}, u32[]{:S(2)}) copy-start(bf16[1,1,1,2,128,128]{5,4,3,2,1,0:T(8,128)(2,1)} %get-tuple-element.138) | copy-start | bytes 196612
  35.5 154.3 %copy-start.10 = (bf16[1,1,1,2,128,128]{5,4,3,2,1,0:T(8,128)(2,1)S(1)}, bf16[1,1,1,2,128,128]{5,4,3,2,1,0:T(8,128)(2,1)}, u32[]{:S(2)}) copy-start(bf16[1,1,1,2,128,128]{5,4,3,2,1,0:T(8,128)(2,1)} %get-tuple-element.137) | copy-start | bytes 196612
  185.9 8.4 %copy-start.9 = (bf16[1,1,1,2,128,128]{5,4,3,2,1,0:T(8,128)(2,1)S(1)}, bf16[1,1,1,2,128,128]{5,4,3,2,1,0:T(8,128)(2,1)}, u32[]{:S(2)}) copy-start(bf16[1,1,1,2,128,128]{5,4,3,2,1,0:T(8,128)(2,1)} %get-tuple-element.136) | copy-start | bytes 196612
  185.9 10.6 %copy-start.8 = (bf16[1,1,1,2,128,128]{5,4,3,2,1,0:T(8,128)(2,1)S(1)}, bf16[1,1,1,2,128,128]{5,4,3,2,1,0:T(8,128)(2,1)}, u32[]{:S(2)}) copy-start(bf16[1,1,1,2,128,128]{5,4,3,2,1,0:T(8,128)(2,1)} %get-tuple-element.135) | copy-start | bytes 196612
  186.9 15.4 %copy-start.7 = (bf16[1,1,1,2,128,128]{5,4,3,2,1,0:T(8,128)(2,1)S(1)}, bf16[1,1,1,2,128,128]{5,4,3,2,1,0:T(8,128)(2,1)}, u32[]{:S(2)}) copy-start(bf16[1,1,1,2,128,128]{5,4,3,2,1,0:T(8,128)(2,1)} %get-tuple-element.134) | copy-start | bytes 196612
  187.9 6.4 %collective-permute-start.3 = (bf16[2,128,128]{2,1,0:T(8,128)(2,1)S(1)}, bf16[2,128,128]{2,1,0:T(8,128)(2,1)S(1)}, u32[]{:S(2)}, u32[]{:S(2)}) collective-permute-start(bf16[2,128,128]{2,1,0:T(8,128)(2,1)S(1)} %fusion.23), channel_id=1, source_target_pairs={{0,8},{4,12},{8,0},{12,4},{16,24},{20,28},{24,16},{28,20},{32,40},... | collective-permute-start | bytes 196616 | tf_op jit(solution)/shard_map/ppermute | solution.py:36
  190.0 18.8 %copy-start.6 = (bf16[1,1,1,2,128,128]{5,4,3,2,1,0:T(8,128)(2,1)S(1)}, bf16[1,1,1,2,128,128]{5,4,3,2,1,0:T(8,128)(2,1)}, u32[]{:S(2)}) copy-start(bf16[1,1,1,2,128,128]{5,4,3,2,1,0:T(8,128)(2,1)} %get-tuple-element.133) | copy-start | bytes 196612
  194.5 18.5 %copy-start.5 = (bf16[1,1,1,2,128,128]{5,4,3,2,1,0:T(8,128)(2,1)S(1)}, bf16[1,1,1,2,128,128]{5,4,3,2,1,0:T(8,128)(2,1)}, u32[]{:S(2)}) copy-start(bf16[1,1,1,2,128,128]{5,4,3,2,1,0:T(8,128)(2,1)} %get-tuple-element.132) | copy-start | bytes 196612
  194.5 7.8 %collective-permute-start.4 = (bf16[2,128,128]{2,1,0:T(8,128)(2,1)S(1)}, bf16[2,128,128]{2,1,0:T(8,128)(2,1)S(1)}, u32[]{:S(2)}, u32[]{:S(2)}) collective-permute-start(bf16[2,128,128]{2,1,0:T(8,128)(2,1)S(1)} %fusion.24), channel_id=1, source_target_pairs={{0,16},{4,20},{8,24},{12,28},{16,0},{20,4},{24,8},{28,12},{32,48},... | collective-permute-start | bytes 196616 | tf_op jit(solution)/shard_map/ppermute | solution.py:36
  196.7 20.6 %copy-start.4 = (bf16[1,1,1,2,128,128]{5,4,3,2,1,0:T(8,128)(2,1)S(1)}, bf16[1,1,1,2,128,128]{5,4,3,2,1,0:T(8,128)(2,1)}, u32[]{:S(2)}) copy-start(bf16[1,1,1,2,128,128]{5,4,3,2,1,0:T(8,128)(2,1)} %get-tuple-element.131) | copy-start | bytes 196612
  202.6 16.9 %copy-start.3 = (bf16[1,1,1,2,128,128]{5,4,3,2,1,0:T(8,128)(2,1)S(1)}, bf16[1,1,1,2,128,128]{5,4,3,2,1,0:T(8,128)(2,1)}, u32[]{:S(2)}) copy-start(bf16[1,1,1,2,128,128]{5,4,3,2,1,0:T(8,128)(2,1)} %get-tuple-element.130) | copy-start | bytes 196612
  202.6 10.3 %collective-permute-start.5 = (bf16[2,128,128]{2,1,0:T(8,128)(2,1)S(1)}, bf16[2,128,128]{2,1,0:T(8,128)(2,1)S(1)}, u32[]{:S(2)}, u32[]{:S(2)}) collective-permute-start(bf16[2,128,128]{2,1,0:T(8,128)(2,1)S(1)} %fusion.25), channel_id=1, source_target_pairs={{0,32},{4,36},{8,40},{12,44},{16,48},{20,52},{24,56},{28,60},{32,0... | collective-permute-start | bytes 196616 | tf_op jit(solution)/shard_map/ppermute | solution.py:36
  213.2 6.3 %collective-permute-start.6 = (bf16[2,128,128]{2,1,0:T(8,128)(2,1)S(1)}, bf16[2,128,128]{2,1,0:T(8,128)(2,1)S(1)}, u32[]{:S(2)}, u32[]{:S(2)}) collective-permute-start(bf16[2,128,128]{2,1,0:T(8,128)(2,1)S(1)} %fusion.26), channel_id=1, source_target_pairs={{0,64},{4,68},{8,72},{12,76},{16,80},{20,84},{24,88},{28,92},{32,9... | collective-permute-start | bytes 196616 | tf_op jit(solution)/shard_map/ppermute | solution.py:36
  219.7 8.4 %collective-permute-start.7 = (bf16[2,128,128]{2,1,0:T(8,128)(2,1)S(1)}, bf16[2,128,128]{2,1,0:T(8,128)(2,1)S(1)}, u32[]{:S(2)}, u32[]{:S(2)}) collective-permute-start(bf16[2,128,128]{2,1,0:T(8,128)(2,1)S(1)} %fusion.27), channel_id=1, source_target_pairs={{0,128},{4,132},{8,136},{12,140},{16,144},{20,148},{24,152},{28,15... | collective-permute-start | bytes 196616 | tf_op jit(solution)/shard_map/ppermute | solution.py:36
  228.3 13.2 %collective-permute-start.8 = (bf16[2,128,128]{2,1,0:T(8,128)(2,1)S(1)}, bf16[2,128,128]{2,1,0:T(8,128)(2,1)S(1)}, u32[]{:S(2)}, u32[]{:S(2)}) collective-permute-start(bf16[2,128,128]{2,1,0:T(8,128)(2,1)S(1)} %fusion.28), channel_id=1, source_target_pairs={{0,256},{4,260},{8,264},{12,268},{16,272},{20,276},{24,280},{28,28... | collective-permute-start | bytes 196616 | tf_op jit(solution)/shard_map/ppermute | solution.py:36
where the time goes:
time: 246 us; the launch traced here: 244 us
  other arithmetic  99.6 us (40%)
  starting transfers between devices  45.9 us (19%)
  local copies, waits for them, and re-layouts  32.2 us (13%)
  waiting for transfers between devices  27.3 us (11%)
  matrix products  22.8 us (9%)
  loops' own time  16 us (7%)
    another operation x8, other arithmetic  63.7 us
    ppermute x9, starting transfers between devices, from_partner(): return lax.ppermute(value, axis, pairs)  36.8 us
    ppermute x9, waiting for transfers between devices, from_partner(): return lax.ppermute(value, axis, pairs)  27.3 us
    dot_general x8, matrix products, near_product(): jnp.einsum('jkts,pcks->jpct', tiles, sources, preferred_element_type=jnp....  17 us
    another operation x1, loops' own time, per_device(): near = lax.map(box_term, jnp.arange(box_count, dtype=jnp.int32))  16 us
    gather x8, local copies, waits for them, and re-layouts, box_term(): return near_product(tiles, jnp.take(wide_density, slots, axis=2))  7.08 us
    ppermute x1, starting transfers between devices, padded(): lax.ppermute(head, axis, [((i + 1) % count, i) for i in range(ends)])  5.71 us
    and x8, other arithmetic, box_term(): return near_product(tiles, jnp.take(wide_density, slots, axis=2))  5.63 us
  transfers between devices with their start and end apart: 11, of which 8 were waited for; matrix products, arithmetic and copies ran while one was open for 60% of the time, Pallas kernels for 0%

commit v1 on v0

v1 whole, which is shorter than its diff:
```python
import functools
import math

import jax
import jax.numpy as jnp
from jax import lax
from jax.experimental import pallas as pl
from jax.experimental.pallas import tpu as pltpu
from jax.sharding import PartitionSpec as P

HB = 2
PACK = 16

SOFTENING = 0.05
FOUR_PI = 4.0 * math.pi

SIN_COEFFS = (4.442867902822206, -7.307443412968344, 3.5947879989545957, -0.7843738193353357)
COS_COEFFS = (1.4142134965639892, -6.978850988075765, 5.739461166775787, -1.8835629581956719, 0.3106981253821905)

NT = (((1,), (1,)), ((), ()))
NN = (((1,), (0,)), ((), ()))
TN = (((0,), (0,)), ((), ()))

VMEM_LIMIT = 16 * 1024 * 1024


def dot(left, right, dims):
    return lax.dot_general(left, right, dims, preferred_element_type=jnp.float32)


def horner(coeffs, x):
    total = coeffs[-1] * x + coeffs[-2]
    for c in reversed(coeffs[:-2]):
        total = total * x + c
    return total


def rows_of(values, rows, count):
    index = lax.broadcasted_iota(jnp.int32, (rows, count), 0)
    total = jnp.zeros((rows, count), jnp.float32)
    for i, value in enumerate(values):
        total = jnp.where(index == i, value, total)
    return total


def head_kernel(density, compress, skeleton, state):
    rank = skeleton.shape[1]
    panels = density.shape[1]
    columns = density.shape[0] // 2
    d = density[...]
    index = lax.broadcasted_iota(jnp.int32, (panels, rank), 0)
    onehot = (index == skeleton[...]).astype(jnp.float32).astype(jnp.bfloat16)
    picked = dot(d, onehot, NN)
    product = dot(d, compress[...], NT)
    real = product[:columns, :rank] - product[columns:, rank:] + picked[:columns]
    imag = product[:columns, rank:] + product[columns:, :rank] + picked[columns:]
    state[0] = real.astype(state.dtype)
    state[1] = imag.astype(state.dtype)


def pack_kernel(density, coords, weights, after, geometry, head, tail):
    del after
    panels = density.shape[1]
    width = head.shape[1]
    rows = density.shape[0]
    c = coords[...].astype(jnp.float32)
    w = weights[...].astype(jnp.float32)
    geo = rows_of([c[0:1], c[1:2], c[2:3], w], PACK, panels).astype(jnp.bfloat16)
    geometry[...] = geo
    head[0:rows, :] = density[:, 0:width]
    tail[0:rows, :] = density[:, panels - width : panels]
    head[rows : rows + PACK, :] = geo[:, 0:width]
    tail[rows : rows + PACK, :] = geo[:, panels - width : panels]


def near_kernel(first, counts, neighbors, density, geometry, left, right, after, out, tiles):
    del after
    rows, panels = density.shape
    columns = rows // 2
    halo = left.shape[1]
    wide = panels + 2 * halo
    box_count, slot_count = neighbors.shape
    size = panels // box_count
    wide_boxes = wide // size
    boxes = out.shape[2] // size

    geo = jnp.concatenate(
        [left[rows : rows + PACK, :], geometry[...], right[rows : rows + PACK, :]], axis=1
    ).astype(jnp.float32)
    x, y, z, w = geo[0:1], geo[1:2], geo[2:3], geo[3:4]
    square = x * x + y * y + z * z

    def split(value):
        one = value.astype(jnp.bfloat16).astype(jnp.float32)
        two = (value - one).astype(jnp.bfloat16).astype(jnp.float32)
        return [one, two, value - one - two]

    ones = jnp.ones_like(x)
    source = rows_of(
        [x, y, z] + split(square + SOFTENING * SOFTENING) + [ones] * 3, PACK, wide
    ).astype(jnp.bfloat16)

    slots = neighbors[...]
    live_count = jnp.zeros((box_count, 1), jnp.int32)
    box_id = lax.broadcasted_iota(jnp.int32, (box_count, 1), 0)
    for b in range(box_count):
        live_count = jnp.where(box_id == b, counts[b], live_count)
    slot_id = lax.broadcasted_iota(jnp.int32, (box_count, slot_count), 1)
    slots = jnp.where(slot_id < live_count, slots, -1)
    times = [
        jnp.sum(jnp.where(slots == g, 1.0, 0.0), axis=1, keepdims=True) for g in range(wide_boxes)
    ]

    for i in range(boxes):
        b = first + i
        start = halo + b * size
        at = slice(start, start + size)
        target = rows_of(
            [-2.0 * x[:, at], -2.0 * y[:, at], -2.0 * z[:, at]] + [ones[:, at]] * 3 + split(square[:, at]),
            PACK,
            size,
        ).astype(jnp.bfloat16)
        for g in range(0, wide_boxes, 2):
            span = slice(g * size, (g + 2) * size)
            r2 = dot(target, source[:, span], TN)
            inverse = lax.rsqrt(r2)
            radius = r2 * inverse
            f = radius - jnp.round(radius)
            q = f * f
            u = f * horner(SIN_COEFFS, q)
            v = horner(COS_COEFFS, q)
            factor = w[:, span] * (1.0 / FOUR_PI)
            many = jnp.concatenate(
                [jnp.broadcast_to(times[g + j][b : b + 1], (1, size)) for j in range(2)], axis=1
            )
            a = inverse * (factor * many)
            au = a * u
            tiles[i, 0:size, span] = (a - au * u).astype(jnp.bfloat16)
            tiles[i, size : 2 * size, span] = (au * v).astype(jnp.bfloat16)
        total = dot(density[...], tiles[i, :, halo : halo + panels], NT)
        total += dot(left[0:rows, :], tiles[i, :, 0:halo], NT)
        total += dot(right[0:rows, :], tiles[i, :, halo + panels : wide], NT)
        place = slice(i * size, (i + 1) * size)
        out[0, :, place] = total[:columns, :size] - total[columns:, size:]
        out[1, :, place] = total[:columns, size:] + total[columns:, :size]


def tail_kernel(state, expand, near, out):
    columns = state.shape[1]
    rank = state.shape[2]
    s = state[...].reshape(2 * columns, rank)
    first = dot(s, expand[0], NN)
    second = dot(s, expand[1], NN)
    real = first[:columns] - second[columns:]
    imag = second[:columns] + first[columns:]
    out[0] = (real + near[0]).astype(out.dtype)
    out[1] = (imag + near[1]).astype(out.dtype)


def params():
    return pltpu.CompilerParams(vmem_limit_bytes=VMEM_LIMIT)


def in_vmem():
    return pl.BlockSpec(memory_space=pltpu.VMEM)


def anywhere():
    return pl.BlockSpec(memory_space=pl.ANY)


def exchange(value, axis, stride):
    mask = 2**stride
    pairs = [(source, source ^ mask) for source in range(lax.axis_size(axis))]
    return lax.ppermute(value, axis, pairs)


def shift(value, step):
    axes = ("leaf", "sub")
    count = lax.axis_size(axes)
    if step > 0:
        pairs = [(i, i + 1) for i in range(count - 1)]
    else:
        pairs = [(i + 1, i) for i in range(count - 1)]
    return lax.ppermute(value, axes, pairs)


def pair_product(left, right):
    columns = left.shape[1]
    rank_rows = right.shape[1]
    product = dot(left.reshape(2 * columns, -1), right.reshape(2 * rank_rows, -1), NT)
    real = product[:columns, :rank_rows] - product[columns:, rank_rows:]
    imag = product[:columns, rank_rows:] + product[columns:, :rank_rows]
    return jnp.stack([real, imag])


def combine(own, other, matrices):
    return (pair_product(own, matrices[0]) + pair_product(other, matrices[1])).astype(jnp.bfloat16)


def per_device(density, coords, weights, counts, neighbors, skeleton, compress, mix, expand):
    columns, panels = density.shape[1:]
    rank = compress.shape[1]
    box_count = counts.shape[0]
    size = panels // box_count
    halo = HB * size
    rows = 2 * columns
    flat = density.reshape(rows, panels)
    basis = compress.reshape(2 * rank, panels)

    state = pl.pallas_call(
        head_kernel,
        out_shape=jax.ShapeDtypeStruct((2, columns, rank), jnp.bfloat16),
        in_specs=[in_vmem()] * 3,
        out_specs=in_vmem(),
        compiler_params=params(),
        cost_estimate=pl.CostEstimate(flops=2 * rows * panels * 3 * rank, bytes_accessed=2**20, transcendentals=0),
        name="compress_density",
    )(flat, basis, skeleton)

    strip = jax.ShapeDtypeStruct((rows + PACK, halo), jnp.bfloat16)
    geometry, head, tail = pl.pallas_call(
        pack_kernel,
        out_shape=(jax.ShapeDtypeStruct((PACK, panels), jnp.bfloat16), strip, strip),
        in_specs=[in_vmem()] * 3 + [anywhere()],
        out_specs=(in_vmem(),) * 3,
        compiler_params=params(),
        cost_estimate=pl.CostEstimate(flops=2**20, bytes_accessed=2**20, transcendentals=0),
        name="pack_halo",
    )(flat, coords, weights[None, :], state)
    left = shift(tail, 1)
    right = shift(head, -1)

    sub_levels = lax.axis_size("sub").bit_length() - 1
    leaf_levels = lax.axis_size("leaf").bit_length() - 1
    steps = [("sub", i) for i in range(sub_levels)] + [("leaf", i) for i in range(leaf_levels)]
    per_call = 2
    calls = box_count // per_call
    begin = 3
    near = []

    def near_boxes(after):
        call = pl.pallas_call(
            functools.partial(near_kernel, len(near) * per_call),
            out_shape=jax.ShapeDtypeStruct((2, columns, per_call * size), jnp.float32),
            in_specs=[pl.BlockSpec(memory_space=pltpu.SMEM)] + [in_vmem()] * 5 + [anywhere()],
            out_specs=in_vmem(),
            scratch_shapes=[pltpu.VMEM((per_call, 2 * size, panels + 2 * halo), jnp.bfloat16)],
            compiler_params=params(),
            cost_estimate=pl.CostEstimate(
                flops=2 * per_call * rows * (panels + 2 * halo) * 2 * size,
                bytes_accessed=2**21,
                transcendentals=per_call * size * (panels + 2 * halo),
            ),
            name="near_boxes",
        )
        near.append(call(counts, neighbors, flat, geometry, left, right, after))

    for level, (axis, stride) in enumerate(steps):
        other = exchange(state, axis, stride)
        if level >= begin and len(near) < calls:
            near_boxes(state)
        state = combine(state, other, mix[0, level])
    while len(near) < calls:
        near_boxes(state)

    near = jnp.concatenate(near, axis=2)
    block = 2 * size
    return pl.pallas_call(
        tail_kernel,
        grid=(panels // block,),
        out_shape=jax.ShapeDtypeStruct((2, columns, panels), jnp.bfloat16),
        in_specs=[
            pl.BlockSpec((2, columns, rank), lambda i: (0, 0, 0)),
            pl.BlockSpec((2, rank, block), lambda i: (0, 0, i)),
            pl.BlockSpec((2, columns, block), lambda i: (0, 0, i)),
        ],
        out_specs=pl.BlockSpec((2, columns, block), lambda i: (0, 0, i)),
        compiler_params=params(),
        cost_estimate=pl.CostEstimate(flops=4 * rows * rank * panels, bytes_accessed=2**21, transcendentals=0),
        name="expand_state",
    )(state, expand, near)


def solution(mesh):
    return jax.shard_map(
        per_device,
        mesh=mesh,
        in_specs=(
            P(None, None, ("leaf", "sub")),
            P(None, ("leaf", "sub")),
            P(("leaf", "sub")),
            P(("leaf", "sub")),
            P(("leaf", "sub"), None),
            P(("leaf", "sub"), None),
            P(None, None, ("leaf", "sub")),
            P(("leaf", "sub"), None, None, None, None, None),
            P(None, None, ("leaf", "sub")),
        ),
        out_specs=P(None, None, ("leaf", "sub")),
        check_vma=False,
    )
```

time: 246 us -> 85.9 us (0.35)
  the two profiles are of different devices: /device:TPU:2 before, /device:TPU:8 now
where the time goes in v1:
time: 85.9 us; the launch traced here: 85.2 us
  starting transfers between devices  53.2 us (62%)
  Pallas kernels  12 us (14%)
  waiting for transfers between devices  10.1 us (12%)
  local copies, waits for them, and re-layouts  5.51 us (6%)
  matrix products  3.24 us (4%)
    ppermute x9, starting transfers between devices, exchange(): return lax.ppermute(value, axis, pairs)  45.6 us
    ppermute x9, waiting for transfers between devices, exchange(): return lax.ppermute(value, axis, pairs)  10.1 us
    pallas_call x4, Pallas kernels, near_boxes(): near.append(call(counts, neighbors, flat, geometry, left, right, after))  9.4 us
    ppermute x2, starting transfers between devices, shift(): return lax.ppermute(value, axes, pairs)  7.67 us
    unnamed x14, local copies, waits for them, and re-layouts  3.45 us
    dot_general x18, matrix products, dot(): lax.dot_general(left, right, dims, preferred_element_type=jnp.float32)  3.24 us
    pallas_call x1, Pallas kernels, per_device(): pl.pallas_call(tail_kernel, grid=(panels // block,), out_shape=jax.ShapeD...  2.11 us
  transfers between devices with their start and end apart: 11, of which 5 were waited for; matrix products, arithmetic and copies ran while one was open for 5% of the time, Pallas kernels for 11%

profile of v1, /device:TPU:8, one launch (start us, length us, event | category | flops | bytes accessed | tf_op | source)
XLA Modules:
  0.0 85.2 jit_solution(3874102150568793684)
XLA Ops:
  0.0 1.0 %copy-done = bf16[2,128,1024]{2,1,0:T(8,128)(2,1)S(1)} copy-done((bf16[2,128,1024]{2,1,0:T(8,128)(2,1)S(1)}, bf16[2,128,1024]{2,1,0:T(8,128)(2,1)}, u32[]{:S(2)}) %copy-start) | copy-done | bytes 524312
  1.0 1.0 %copy-done.1 = bf16[2,128,1024]{2,1,0:T(8,128)(2,1)S(1)} copy-done((bf16[2,128,1024]{2,1,0:T(8,128)(2,1)S(1)}, bf16[2,128,1024]{2,1,0:T(8,128)(2,1)}, u32[]{:S(2)}) %copy-start.1) | copy-done | bytes 524312
  2.1 0.7 copy-done.4
  2.7 0.4 compress_density.1.after
  3.2 3.4 %collective-permute-start = (bf16[2,128,128]{2,1,0:T(8,128)(2,1)S(1)}, bf16[2,128,128]{2,1,0:T(8,128)(2,1)S(1)}, u32[]{:S(2)}, u32[]{:S(2)}) collective-permute-start(bf16[2,128,128]{2,1,0:T(8,128)(2,1)S(1)} %compress_density.1.after), channel_id=1, source_target_pairs={{0,1},{1,0},{2,3},{3,2},{4,5},{5,4},{6,7},{7,6},{8,9},{9,8},{10,11... | collective-permute-start | bytes 196616 | tf_op jit(solution)/shard_map/ppermute | solution.py:175
  6.6 0.7 broadcast_in_dim.3.weights
  7.3 0.7 copy-done.3
  8.0 2.4 %collective-permute-start.9 = (bf16[272,256]{1,0:T(8,128)(2,1)S(1)}, bf16[272,256]{1,0:T(8,128)(2,1)S(1)}, u32[]{:S(2)}, u32[]{:S(2)}) collective-permute-start(bf16[272,256]{1,0:T(8,128)(2,1)S(1)} %get-tuple-element.9), channel_id=1, source_target_pairs={{0,1},{1,2},{2,3},{3,4},{4,5},{5,6},{6,7},{7,8},{8,9},{9,10},{10,1... | collective-permute-start | bytes 417800 | tf_op jit(solution)/shard_map/ppermute | solution.py:185
  10.5 5.2 %collective-permute-start.10 = (bf16[272,256]{1,0:T(8,128)(2,1)S(1)}, bf16[272,256]{1,0:T(8,128)(2,1)S(1)}, u32[]{:S(2)}, u32[]{:S(2)}) collective-permute-start(bf16[272,256]{1,0:T(8,128)(2,1)S(1)} %get-tuple-element.10), channel_id=1, source_target_pairs={{1,0},{2,1},{3,2},{4,3},{5,4},{6,5},{7,6},{8,7},{9,8},{10,9},{11,1... | collective-permute-start | bytes 417800 | tf_op jit(solution)/shard_map/ppermute | solution.py:185
  15.7 1.4 %fusion.45 = (bf16[1,1,1,2,128,128]{5,4,3,2,1,0:T(8,128)(2,1)S(1)}, bf16[1,1,1,2,128,128]{5,4,3,2,1,0:T(8,128)(2,1)S(1)}, bf16[1,1,1,2,128,128]{5,4,3,2,1,0:T(8,...) fusion(bf16[1,9,2,2,128,128]{5,4,3,2,1,0:T(8,128)(2,1)} %param.16), kind=kLoop, calls=%fused_computation.91 | loop fusion | bytes 2359296 | tf_op jit(solution)/shard_map/slice | solution.py:198
  17.1 0.2 fusion.46
  17.3 0.2 fusion.47
  17.5 2.8 %collective-permute-start.1 = (bf16[2,128,128]{2,1,0:T(8,128)(2,1)S(1)}, bf16[2,128,128]{2,1,0:T(8,128)(2,1)S(1)}, u32[]{:S(2)}, u32[]{:S(2)}) collective-permute-start(bf16[2,128,128]{2,1,0:T(8,128)(2,1)S(1)} %fusion), channel_id=1, source_target_pairs={{0,2},{1,3},{2,0},{3,1},{4,6},{5,7},{6,4},{7,5},{8,10},{9,11},{10,... | collective-permute-start | bytes 196616 | tf_op jit(solution)/shard_map/ppermute | solution.py:175
  20.3 0.2 fusion.48
  20.6 4.6 %collective-permute-done.1 = bf16[2,128,128]{2,1,0:T(8,128)(2,1)S(1)} collective-permute-done((bf16[2,128,128]{2,1,0:T(8,128)(2,1)S(1)}, bf16[2,128,128]{2,1,0:T(8,128)(2,1)S(1)}, u32[]{:S(2)}, u32[]{:S(2)}) %collective-permute-start.1) | collective-permute-done | bytes 65568 | tf_op jit(solution)/shard_map/ppermute | solution.py:175
  25.2 0.2 fusion.49
  25.4 1.9 %collective-permute-start.2 = (bf16[2,128,128]{2,1,0:T(8,128)(2,1)S(1)}, bf16[2,128,128]{2,1,0:T(8,128)(2,1)S(1)}, u32[]{:S(2)}, u32[]{:S(2)}) collective-permute-start(bf16[2,128,128]{2,1,0:T(8,128)(2,1)S(1)} %fusion.1), channel_id=1, source_target_pairs={{0,4},{4,0},{8,12},{12,8},{16,20},{20,16},{24,28},{28,24},{32,36},... | collective-permute-start | bytes 196616 | tf_op jit(solution)/shard_map/ppermute | solution.py:175
  27.4 0.2 fusion.50
  27.6 0.0 copy-start.5
  27.6 1.0 %collective-permute-done.2 = bf16[2,128,128]{2,1,0:T(8,128)(2,1)S(1)} collective-permute-done((bf16[2,128,128]{2,1,0:T(8,128)(2,1)S(1)}, bf16[2,128,128]{2,1,0:T(8,128)(2,1)S(1)}, u32[]{:S(2)}, u32[]{:S(2)}) %collective-permute-start.2) | collective-permute-done | bytes 65568 | tf_op jit(solution)/shard_map/ppermute | solution.py:175
  28.6 0.2 fusion.51
  28.8 3.8 %collective-permute-start.3 = (bf16[2,128,128]{2,1,0:T(8,128)(2,1)S(1)}, bf16[2,128,128]{2,1,0:T(8,128)(2,1)S(1)}, u32[]{:S(2)}, u32[]{:S(2)}) collective-permute-start(bf16[2,128,128]{2,1,0:T(8,128)(2,1)S(1)} %fusion.2.after), channel_id=1, source_target_pairs={{0,8},{4,12},{8,0},{12,4},{16,24},{20,28},{24,16},{28,20},{32,40},... | collective-permute-start | bytes 196616 | tf_op jit(solution)/shard_map/ppermute | solution.py:175
  32.6 0.2 fusion.52
  32.9 2.4 %near_boxes.4 = f32[2,128,256]{2,1,0:T(8,128)S(1)} custom-call(s32[8]{0:T(128)S(1)} %copy-done.6, s32[8,27]{1,0:T(8,128)S(1)} %copy-done.5, bf16[256,1024]{1,0:T(8,128)(2,1)S(1)} %bitcast.148, bf16[16,1024]{1,0:T(8,128)(2,1)S(1)} %get-tuple-element.8.geometry, bf16[272,256]{1,0:T(8,128)(2,1)S(1)} %collective-permute-done.9.left, ...), custom_call_target="tpu_custom_call" | custom-call | flops 402653184 | bytes 2097152 | tf_op jit(solution)/shard_map/near_boxes/pallas_call | solution.py:257
  35.2 0.2 fusion.53
  35.5 4.2 %collective-permute-start.4 = (bf16[2,128,128]{2,1,0:T(8,128)(2,1)S(1)}, bf16[2,128,128]{2,1,0:T(8,128)(2,1)S(1)}, u32[]{:S(2)}, u32[]{:S(2)}) collective-permute-start(bf16[2,128,128]{2,1,0:T(8,128)(2,1)S(1)} %fusion.3.after), channel_id=1, source_target_pairs={{0,16},{4,20},{8,24},{12,28},{16,0},{20,4},{24,8},{28,12},{32,48},... | collective-permute-start | bytes 196616 | tf_op jit(solution)/shard_map/ppermute | solution.py:175
  39.7 0.2 fusion.54
  39.9 2.3 %near_boxes.5 = f32[2,128,256]{2,1,0:T(8,128)S(1)} custom-call(s32[8]{0:T(128)S(1)} %copy-done.6, s32[8,27]{1,0:T(8,128)S(1)} %copy-done.5, bf16[256,1024]{1,0:T(8,128)(2,1)S(1)} %bitcast.149, bf16[16,1024]{1,0:T(8,128)(2,1)S(1)} %get-tuple-element.8.geometry, bf16[272,256]{1,0:T(8,128)(2,1)S(1)} %collective-permute-done.9.left, ...), custom_call_target="tpu_custom_call" | custom-call | flops 402653184 | bytes 2097152 | tf_op jit(solution)/shard_map/near_boxes/pallas_call | solution.py:257
  42.3 0.3 collective-permute-done.4
  42.6 0.2 fusion.55
  42.8 7.5 %collective-permute-start.5 = (bf16[2,128,128]{2,1,0:T(8,128)(2,1)S(1)}, bf16[2,128,128]{2,1,0:T(8,128)(2,1)S(1)}, u32[]{:S(2)}, u32[]{:S(2)}) collective-permute-start(bf16[2,128,128]{2,1,0:T(8,128)(2,1)S(1)} %fusion.4.after), channel_id=1, source_target_pairs={{0,32},{4,36},{8,40},{12,44},{16,48},{20,52},{24,56},{28,60},{32,0... | collective-permute-start | bytes 196616 | tf_op jit(solution)/shard_map/ppermute | solution.py:175
  50.3 0.2 fusion.56
  50.6 2.4 %near_boxes.6 = f32[2,128,256]{2,1,0:T(8,128)S(1)} custom-call(s32[8]{0:T(128)S(1)} %copy-done.6, s32[8,27]{1,0:T(8,128)S(1)} %copy-done.5, bf16[256,1024]{1,0:T(8,128)(2,1)S(1)} %bitcast.150, bf16[16,1024]{1,0:T(8,128)(2,1)S(1)} %get-tuple-element.8.geometry, bf16[272,256]{1,0:T(8,128)(2,1)S(1)} %collective-permute-done.9.left, ...), custom_call_target="tpu_custom_call" | custom-call | flops 402653184 | bytes 2097152 | tf_op jit(solution)/shard_map/near_boxes/pallas_call | solution.py:257
  52.9 0.2 fusion.57
  53.2 5.0 %collective-permute-start.6 = (bf16[2,128,128]{2,1,0:T(8,128)(2,1)S(1)}, bf16[2,128,128]{2,1,0:T(8,128)(2,1)S(1)}, u32[]{:S(2)}, u32[]{:S(2)}) collective-permute-start(bf16[2,128,128]{2,1,0:T(8,128)(2,1)S(1)} %fusion.5.after), channel_id=1, source_target_pairs={{0,64},{4,68},{8,72},{12,76},{16,80},{20,84},{24,88},{28,92},{32,9... | collective-permute-start | bytes 196616 | tf_op jit(solution)/shard_map/ppermute | solution.py:175
  58.1 0.2 fusion.58
  58.4 2.4 %near_boxes.7 = f32[2,128,256]{2,1,0:T(8,128)S(1)} custom-call(s32[8]{0:T(128)S(1)} %copy-done.6, s32[8,27]{1,0:T(8,128)S(1)} %copy-done.5, bf16[256,1024]{1,0:T(8,128)(2,1)S(1)} %bitcast.151, bf16[16,1024]{1,0:T(8,128)(2,1)S(1)} %get-tuple-element.8.geometry, bf16[272,256]{1,0:T(8,128)(2,1)S(1)} %collective-permute-done.9.left, ...), custom_call_target="tpu_custom_call" | custom-call | flops 402653184 | bytes 2097152 | tf_op jit(solution)/shard_map/near_boxes/pallas_call | solution.py:257
  60.7 0.1 pad_maximum_fusion.near
  60.9 0.2 fusion.59
  61.1 6.1 %collective-permute-start.7 = (bf16[2,128,128]{2,1,0:T(8,128)(2,1)S(1)}, bf16[2,128,128]{2,1,0:T(8,128)(2,1)S(1)}, u32[]{:S(2)}, u32[]{:S(2)}) collective-permute-start(bf16[2,128,128]{2,1,0:T(8,128)(2,1)S(1)} %fusion.6), channel_id=1, source_target_pairs={{0,128},{4,132},{8,136},{12,140},{16,144},{20,148},{24,152},{28,15... | collective-permute-start | bytes 196616 | tf_op jit(solution)/shard_map/ppermute | solution.py:175
  67.2 0.2 fusion.60
  67.4 2.0 %collective-permute-done.7 = bf16[2,128,128]{2,1,0:T(8,128)(2,1)S(1)} collective-permute-done((bf16[2,128,128]{2,1,0:T(8,128)(2,1)S(1)}, bf16[2,128,128]{2,1,0:T(8,128)(2,1)S(1)}, u32[]{:S(2)}, u32[]{:S(2)}) %collective-permute-start.7) | collective-permute-done | bytes 65568 | tf_op jit(solution)/shard_map/ppermute | solution.py:175
  69.4 0.2 fusion.61
  69.7 10.8 %collective-permute-start.8 = (bf16[2,128,128]{2,1,0:T(8,128)(2,1)S(1)}, bf16[2,128,128]{2,1,0:T(8,128)(2,1)S(1)}, u32[]{:S(2)}, u32[]{:S(2)}) collective-permute-start(bf16[2,128,128]{2,1,0:T(8,128)(2,1)S(1)} %fusion.7), channel_id=1, source_target_pairs={{0,256},{4,260},{8,264},{12,268},{16,272},{20,276},{24,280},{28,28... | collective-permute-start | bytes 196616 | tf_op jit(solution)/shard_map/ppermute | solution.py:175
  80.5 0.2 fusion.62
  80.7 2.2 %collective-permute-done.8 = bf16[2,128,128]{2,1,0:T(8,128)(2,1)S(1)} collective-permute-done((bf16[2,128,128]{2,1,0:T(8,128)(2,1)S(1)}, bf16[2,128,128]{2,1,0:T(8,128)(2,1)S(1)}, u32[]{:S(2)}, u32[]{:S(2)}) %collective-permute-start.8) | collective-permute-done | bytes 65568 | tf_op jit(solution)/shard_map/ppermute | solution.py:175
  82.9 0.2 fusion.63
  83.1 2.1 %expand_state.1 = bf16[2,128,1024]{2,1,0:T(8,128)(2,1)} custom-call(bf16[2,128,128]{2,1,0:T(8,128)(2,1)S(1)} %fusion.8.state, bf16[2,128,1024]{2,1,0:T(8,128)(2,1)S(1)} %copy-done.2, f32[2,128,1024]{2,1,0:T(8,128)S(1)} %pad_maximum_fusion.near), custom_call_target="tpu_custom_call" | custom-call | flops 134217728 | bytes 2097152 | tf_op jit(solution)/shard_map/expand_state/pallas_call | solution.py:269
  (42 shorter events, 0.5 us)
Async XLA Ops:
  0.0 1.0 %copy-start = (bf16[2,128,1024]{2,1,0:T(8,128)(2,1)S(1)}, bf16[2,128,1024]{2,1,0:T(8,128)(2,1)}, u32[]{:S(2)}) copy-start(bf16[2,128,1024]{2,1,0:T(8,128)(2,1)} %param.9) | copy-start | bytes 1572868
  1.0 1.0 %copy-start.1 = (bf16[2,128,1024]{2,1,0:T(8,128)(2,1)S(1)}, bf16[2,128,1024]{2,1,0:T(8,128)(2,1)}, u32[]{:S(2)}) copy-start(bf16[2,128,1024]{2,1,0:T(8,128)(2,1)} %param.15) | copy-start | bytes 1572868
  2.1 0.7 copy-start.4
  3.2 14.1 %collective-permute-start = (bf16[2,128,128]{2,1,0:T(8,128)(2,1)S(1)}, bf16[2,128,128]{2,1,0:T(8,128)(2,1)S(1)}, u32[]{:S(2)}, u32[]{:S(2)}) collective-permute-start(bf16[2,128,128]{2,1,0:T(8,128)(2,1)S(1)} %compress_density.1.after), channel_id=1, source_target_pairs={{0,1},{1,0},{2,3},{3,2},{4,5},{5,4},{6,7},{7,6},{8,9},{9,8},{10,11... | collective-permute-start | bytes 196616 | tf_op jit(solution)/shard_map/ppermute | solution.py:175
  7.3 0.7 copy-start.3
  8.0 24.8 %collective-permute-start.9 = (bf16[272,256]{1,0:T(8,128)(2,1)S(1)}, bf16[272,256]{1,0:T(8,128)(2,1)S(1)}, u32[]{:S(2)}, u32[]{:S(2)}) collective-permute-start(bf16[272,256]{1,0:T(8,128)(2,1)S(1)} %get-tuple-element.9), channel_id=1, source_target_pairs={{0,1},{1,2},{2,3},{3,4},{4,5},{5,6},{6,7},{7,8},{8,9},{9,10},{10,1... | collective-permute-start | bytes 417800 | tf_op jit(solution)/shard_map/ppermute | solution.py:185
  10.5 22.4 %collective-permute-start.10 = (bf16[272,256]{1,0:T(8,128)(2,1)S(1)}, bf16[272,256]{1,0:T(8,128)(2,1)S(1)}, u32[]{:S(2)}, u32[]{:S(2)}) collective-permute-start(bf16[272,256]{1,0:T(8,128)(2,1)S(1)} %get-tuple-element.10), channel_id=1, source_target_pairs={{1,0},{2,1},{3,2},{4,3},{5,4},{6,5},{7,6},{8,7},{9,8},{10,9},{11,1... | collective-permute-start | bytes 417800 | tf_op jit(solution)/shard_map/ppermute | solution.py:185
  17.5 7.7 %collective-permute-start.1 = (bf16[2,128,128]{2,1,0:T(8,128)(2,1)S(1)}, bf16[2,128,128]{2,1,0:T(8,128)(2,1)S(1)}, u32[]{:S(2)}, u32[]{:S(2)}) collective-permute-start(bf16[2,128,128]{2,1,0:T(8,128)(2,1)S(1)} %fusion), channel_id=1, source_target_pairs={{0,2},{1,3},{2,0},{3,1},{4,6},{5,7},{6,4},{7,5},{8,10},{9,11},{10,... | collective-permute-start | bytes 196616 | tf_op jit(solution)/shard_map/ppermute | solution.py:175
  25.4 3.1 %collective-permute-start.2 = (bf16[2,128,128]{2,1,0:T(8,128)(2,1)S(1)}, bf16[2,128,128]{2,1,0:T(8,128)(2,1)S(1)}, u32[]{:S(2)}, u32[]{:S(2)}) collective-permute-start(bf16[2,128,128]{2,1,0:T(8,128)(2,1)S(1)} %fusion.1), channel_id=1, source_target_pairs={{0,4},{4,0},{8,12},{12,8},{16,20},{20,16},{24,28},{28,24},{32,36},... | collective-permute-start | bytes 196616 | tf_op jit(solution)/shard_map/ppermute | solution.py:175
  27.6 5.3 %copy-start.5 = (s32[8,27]{1,0:T(8,128)S(1)}, s32[8,27]{1,0:T(8,128)}, u32[]{:S(2)}) copy-start(s32[8,27]{1,0:T(8,128)} %neighbors.7) | copy-start | bytes 2596
  27.6 5.3 %copy-start.6 = (s32[8]{0:T(128)S(1)}, s32[8]{0:T(128)}, u32[]{:S(2)}) copy-start(s32[8]{0:T(128)} %counts.7) | copy-start | bytes 100
  28.8 6.4 %collective-permute-start.3 = (bf16[2,128,128]{2,1,0:T(8,128)(2,1)S(1)}, bf16[2,128,128]{2,1,0:T(8,128)(2,1)S(1)}, u32[]{:S(2)}, u32[]{:S(2)}) collective-permute-start(bf16[2,128,128]{2,1,0:T(8,128)(2,1)S(1)} %fusion.2.after), channel_id=1, source_target_pairs={{0,8},{4,12},{8,0},{12,4},{16,24},{20,28},{24,16},{28,20},{32,40},... | collective-permute-start | bytes 196616 | tf_op jit(solution)/shard_map/ppermute | solution.py:175
  35.5 7.1 %collective-permute-start.4 = (bf16[2,128,128]{2,1,0:T(8,128)(2,1)S(1)}, bf16[2,128,128]{2,1,0:T(8,128)(2,1)S(1)}, u32[]{:S(2)}, u32[]{:S(2)}) collective-permute-start(bf16[2,128,128]{2,1,0:T(8,128)(2,1)S(1)} %fusion.3.after), channel_id=1, source_target_pairs={{0,16},{4,20},{8,24},{12,28},{16,0},{20,4},{24,8},{28,12},{32,48},... | collective-permute-start | bytes 196616 | tf_op jit(solution)/shard_map/ppermute | solution.py:175
  42.8 10.1 %collective-permute-start.5 = (bf16[2,128,128]{2,1,0:T(8,128)(2,1)S(1)}, bf16[2,128,128]{2,1,0:T(8,128)(2,1)S(1)}, u32[]{:S(2)}, u32[]{:S(2)}) collective-permute-start(bf16[2,128,128]{2,1,0:T(8,128)(2,1)S(1)} %fusion.4.after), channel_id=1, source_target_pairs={{0,32},{4,36},{8,40},{12,44},{16,48},{20,52},{24,56},{28,60},{32,0... | collective-permute-start | bytes 196616 | tf_op jit(solution)/shard_map/ppermute | solution.py:175
  53.2 7.7 %collective-permute-start.6 = (bf16[2,128,128]{2,1,0:T(8,128)(2,1)S(1)}, bf16[2,128,128]{2,1,0:T(8,128)(2,1)S(1)}, u32[]{:S(2)}, u32[]{:S(2)}) collective-permute-start(bf16[2,128,128]{2,1,0:T(8,128)(2,1)S(1)} %fusion.5.after), channel_id=1, source_target_pairs={{0,64},{4,68},{8,72},{12,76},{16,80},{20,84},{24,88},{28,92},{32,9... | collective-permute-start | bytes 196616 | tf_op jit(solution)/shard_map/ppermute | solution.py:175
  61.1 8.3 %collective-permute-start.7 = (bf16[2,128,128]{2,1,0:T(8,128)(2,1)S(1)}, bf16[2,128,128]{2,1,0:T(8,128)(2,1)S(1)}, u32[]{:S(2)}, u32[]{:S(2)}) collective-permute-start(bf16[2,128,128]{2,1,0:T(8,128)(2,1)S(1)} %fusion.6), channel_id=1, source_target_pairs={{0,128},{4,132},{8,136},{12,140},{16,144},{20,148},{24,152},{28,15... | collective-permute-start | bytes 196616 | tf_op jit(solution)/shard_map/ppermute | solution.py:175
  69.6 13.5 %copy-start.2 = (bf16[2,128,1024]{2,1,0:T(8,128)(2,1)S(1)}, bf16[2,128,1024]{2,1,0:T(8,128)(2,1)}, u32[]{:S(2)}) copy-start(bf16[2,128,1024]{2,1,0:T(8,128)(2,1)} %expand.1) | copy-start | bytes 1572868
  69.7 13.2 %collective-permute-start.8 = (bf16[2,128,128]{2,1,0:T(8,128)(2,1)S(1)}, bf16[2,128,128]{2,1,0:T(8,128)(2,1)S(1)}, u32[]{:S(2)}, u32[]{:S(2)}) collective-permute-start(bf16[2,128,128]{2,1,0:T(8,128)(2,1)S(1)} %fusion.7), channel_id=1, source_target_pairs={{0,256},{4,260},{8,264},{12,268},{16,272},{20,276},{24,280},{28,28... | collective-permute-start | bytes 196616 | tf_op jit(solution)/shard_map/ppermute | solution.py:175

commit v2 on v1

--- a/solution.py
+++ b/solution.py
@@ -22,6 +22,7 @@
 TN = (((0,), (0,)), ((), ()))
 
 VMEM_LIMIT = 16 * 1024 * 1024
+WHOLE_VMEM = 63 * 1024 * 1024
 
 
 def dot(left, right, dims):
@@ -43,14 +44,24 @@
     return total
 
 
-def head_kernel(density, compress, skeleton, state):
+def head_kernel(skeleton_hbm, density_hbm, compress_hbm, state, skeleton, density, compress, sems):
+    copies = [
+        pltpu.make_async_copy(skeleton_hbm, skeleton, sems.at[0]),
+        pltpu.make_async_copy(density_hbm, density, sems.at[1]),
+        pltpu.make_async_copy(compress_hbm, compress, sems.at[2]),
+    ]
+    for copy in copies:
+        copy.start()
     rank = skeleton.shape[1]
     panels = density.shape[1]
     columns = density.shape[0] // 2
+    index = lax.broadcasted_iota(jnp.int32, (panels, rank), 0)
+    copies[0].wait()
+    onehot = (index == skeleton[...]).astype(jnp.float32).astype(jnp.bfloat16)
+    copies[1].wait()
     d = density[...]
-    index = lax.broadcasted_iota(jnp.int32, (panels, rank), 0)
-    onehot = (index == skeleton[...]).astype(jnp.float32).astype(jnp.bfloat16)
     picked = dot(d, onehot, NN)
+    copies[2].wait()
     product = dot(d, compress[...], NT)
     real = product[:columns, :rank] - product[columns:, rank:] + picked[:columns]
     imag = product[:columns, rank:] + product[columns:, :rank] + picked[columns:]
@@ -58,19 +69,28 @@
     state[1] = imag.astype(state.dtype)
 
 
-def pack_kernel(density, coords, weights, after, geometry, head, tail):
+def geometry_rows(coords, weights, count):
+    c = coords.astype(jnp.float32)
+    w = weights.astype(jnp.float32)
+    return rows_of([c[0:1], c[1:2], c[2:3], w], PACK, count).astype(jnp.bfloat16)
+
+
+def tail_strip_kernel(density, coords, weights, after, geometry, strip):
     del after
-    panels = density.shape[1]
-    width = head.shape[1]
+    rows, panels = density.shape
+    width = strip.shape[1]
+    geo = geometry_rows(coords[...], weights[...], panels)
+    geometry[...] = geo
+    strip[0:rows, :] = density[:, panels - width : panels]
+    strip[rows : rows + PACK, :] = geo[:, panels - width : panels]
+
+
+def head_strip_kernel(density, geometry, after, strip):
+    del after
     rows = density.shape[0]
-    c = coords[...].astype(jnp.float32)
-    w = weights[...].astype(jnp.float32)
-    geo = rows_of([c[0:1], c[1:2], c[2:3], w], PACK, panels).astype(jnp.bfloat16)
-    geometry[...] = geo
-    head[0:rows, :] = density[:, 0:width]
-    tail[0:rows, :] = density[:, panels - width : panels]
-    head[rows : rows + PACK, :] = geo[:, 0:width]
-    tail[rows : rows + PACK, :] = geo[:, panels - width : panels]
+    width = strip.shape[1]
+    strip[0:rows, :] = density[:, 0:width]
+    strip[rows : rows + PACK, :] = geometry[:, 0:width]
 
 
 def near_kernel(first, counts, neighbors, density, geometry, left, right, after, out, tiles):
@@ -145,20 +165,28 @@
         out[1, :, place] = total[:columns, size:] + total[columns:, :size]
 
 
-def tail_kernel(state, expand, near, out):
-    columns = state.shape[1]
-    rank = state.shape[2]
+def tail_kernel(state, expand, near, out, block, sems):
+    columns, rank = state.shape[1:]
+    panels = expand.shape[2]
+    step = panels // sems.shape[0]
     s = state[...].reshape(2 * columns, rank)
-    first = dot(s, expand[0], NN)
-    second = dot(s, expand[1], NN)
-    real = first[:columns] - second[columns:]
-    imag = second[:columns] + first[columns:]
-    out[0] = (real + near[0]).astype(out.dtype)
-    out[1] = (imag + near[1]).astype(out.dtype)
-
-
-def params():
-    return pltpu.CompilerParams(vmem_limit_bytes=VMEM_LIMIT)
+    copies = []
+    for i in range(sems.shape[0]):
+        at = slice(i * step, (i + 1) * step)
+        first = dot(s, expand[0, :, at], NN)
+        second = dot(s, expand[1, :, at], NN)
+        real = first[:columns] - second[columns:]
+        imag = second[:columns] + first[columns:]
+        block[0, :, at] = (real + near[0, :, at]).astype(block.dtype)
+        block[1, :, at] = (imag + near[1, :, at]).astype(block.dtype)
+        copies.append(pltpu.make_async_copy(block.at[:, :, at], out.at[:, :, at], sems.at[i]))
+        copies[-1].start()
+    for copy in copies:
+        copy.wait()
+
+
+def params(limit=VMEM_LIMIT):
+    return pltpu.CompilerParams(vmem_limit_bytes=limit)
 
 
 def in_vmem():
@@ -211,32 +239,49 @@
     state = pl.pallas_call(
         head_kernel,
         out_shape=jax.ShapeDtypeStruct((2, columns, rank), jnp.bfloat16),
-        in_specs=[in_vmem()] * 3,
+        in_specs=[pl.BlockSpec(memory_space=pltpu.HBM)] * 3,
         out_specs=in_vmem(),
-        compiler_params=params(),
+        scratch_shapes=[
+            pltpu.VMEM(skeleton.shape, skeleton.dtype),
+            pltpu.VMEM(flat.shape, flat.dtype),
+            pltpu.VMEM(basis.shape, basis.dtype),
+            pltpu.SemaphoreType.DMA((3,)),
+        ],
+        compiler_params=params(WHOLE_VMEM),
         cost_estimate=pl.CostEstimate(flops=2 * rows * panels * 3 * rank, bytes_accessed=2**20, transcendentals=0),
         name="compress_density",
-    )(flat, basis, skeleton)
+    )(skeleton, flat, basis)
 
     strip = jax.ShapeDtypeStruct((rows + PACK, halo), jnp.bfloat16)
-    geometry, head, tail = pl.pallas_call(
-        pack_kernel,
-        out_shape=(jax.ShapeDtypeStruct((PACK, panels), jnp.bfloat16), strip, strip),
-        in_specs=[in_vmem()] * 3 + [anywhere()],
-        out_specs=(in_vmem(),) * 3,
-        compiler_params=params(),
-        cost_estimate=pl.CostEstimate(flops=2**20, bytes_accessed=2**20, transcendentals=0),
-        name="pack_halo",
-    )(flat, coords, weights[None, :], state)
-    left = shift(tail, 1)
-    right = shift(head, -1)
+    cheap = pl.CostEstimate(flops=2**20, bytes_accessed=2**18, transcendentals=0)
+
+    def tail_strip(after):
+        return pl.pallas_call(
+            tail_strip_kernel,
+            out_shape=(jax.ShapeDtypeStruct((PACK, panels), jnp.bfloat16), strip),
+            in_specs=[in_vmem()] * 3 + [anywhere()],
+            out_specs=(in_vmem(),) * 2,
+            compiler_params=params(),
+            cost_estimate=cheap,
+            name="tail_strip",
+        )(flat, coords, weights[None, :], after)
+
+    def head_strip(after):
+        return pl.pallas_call(
+            head_strip_kernel,
+            out_shape=strip,
+            in_specs=[in_vmem()] * 2 + [anywhere()],
+            out_specs=in_vmem(),
+            compiler_params=params(),
+            cost_estimate=cheap,
+            name="head_strip",
+        )(flat, geometry, after)
 
     sub_levels = lax.axis_size("sub").bit_length() - 1
     leaf_levels = lax.axis_size("leaf").bit_length() - 1
     steps = [("sub", i) for i in range(sub_levels)] + [("leaf", i) for i in range(leaf_levels)]
     per_call = 2
     calls = box_count // per_call
-    begin = 3
     near = []
 
     def near_boxes(after):
@@ -258,24 +303,25 @@
 
     for level, (axis, stride) in enumerate(steps):
         other = exchange(state, axis, stride)
-        if level >= begin and len(near) < calls:
+        if level == 1:
+            geometry, strip_out = tail_strip(state)
+            left = shift(strip_out, 1)
+        if level == 2:
+            right = shift(head_strip(state), -1)
+        if level in (4, 5):
+            near_boxes(state)
             near_boxes(state)
         state = combine(state, other, mix[0, level])
     while len(near) < calls:
         near_boxes(state)
 
     near = jnp.concatenate(near, axis=2)
-    block = 2 * size
     return pl.pallas_call(
         tail_kernel,
-        grid=(panels // block,),
         out_shape=jax.ShapeDtypeStruct((2, columns, panels), jnp.bfloat16),
-        in_specs=[
-            pl.BlockSpec((2, columns, rank), lambda i: (0, 0, 0)),
-            pl.BlockSpec((2, rank, block), lambda i: (0, 0, i)),
-            pl.BlockSpec((2, columns, block), lambda i: (0, 0, i)),
-        ],
-        out_specs=pl.BlockSpec((2, columns, block), lambda i: (0, 0, i)),
+        in_specs=[in_vmem()] * 3,
+        out_specs=anywhere(),
+        scratch_shapes=[pltpu.VMEM((2, columns, panels), jnp.bfloat16), pltpu.SemaphoreType.DMA((4,))],
         compiler_params=params(),
         cost_estimate=pl.CostEstimate(flops=4 * rows * rank * panels, bytes_accessed=2**21, transcendentals=0),
         name="expand_state",

time: 85.9 us -> 82.1 us (0.956)
  the two profiles are of different devices: /device:TPU:8 before, /device:TPU:16 now
where the time goes in v2:
time: 82.1 us; the launch traced here: 81.6 us
  starting transfers between devices  52.6 us (64%)
  Pallas kernels  13.1 us (16%)
  waiting for transfers between devices  10 us (12%)
  matrix products  3.25 us (4%)
  local copies, waits for them, and re-layouts  1.45 us (2%)
    ppermute x9, starting transfers between devices, exchange(): return lax.ppermute(value, axis, pairs)  44.9 us
    ppermute x9, waiting for transfers between devices, exchange(): return lax.ppermute(value, axis, pairs)  10 us
    pallas_call x4, Pallas kernels, near_boxes(): near.append(call(counts, neighbors, flat, geometry, left, right, after))  9.4 us
    ppermute x2, starting transfers between devices, shift(): return lax.ppermute(value, axes, pairs)  7.68 us
    dot_general x18, matrix products, dot(): lax.dot_general(left, right, dims, preferred_element_type=jnp.float32)  3.25 us
    pallas_call x1, Pallas kernels, per_device(): pl.pallas_call(head_kernel, out_shape=jax.ShapeDtypeStruct((2, columns, r...  2.45 us
  transfers between devices with their start and end apart: 11, of which 5 were waited for; matrix products, arithmetic and copies ran while one was open for 5% of the time, Pallas kernels for 12%

profile of v2, /device:TPU:16, one launch (start us, length us, event | category | flops | bytes accessed | tf_op | source)
XLA Modules:
  0.0 81.6 jit_solution(1080419335314444507)
XLA Ops:
  0.0 2.4 %compress_density.1 = bf16[2,128,128]{2,1,0:T(8,128)(2,1)} custom-call(s32[1,128]{1,0:T(1,128)} %skeleton_hbm.1, bf16[256,1024]{1,0:T(8,128)(2,1)} %bitcast.146, bf16[256,1024]{1,0:T(8,128)(2,1)} %bitcast.157), custom_call_target="tpu_custom_call" | custom-call | flops 201326592 | bytes 1048576 | tf_op jit(solution)/shard_map/compress_density/pallas_call | solution.py:239
  2.5 0.0 copy-start.5
  2.5 0.0 copy-start.6
  2.5 3.5 %collective-permute-start = (bf16[2,128,128]{2,1,0:T(8,128)(2,1)}, bf16[2,128,128]{2,1,0:T(8,128)(2,1)S(1)}, u32[]{:S(2)}, u32[]{:S(2)}) collective-permute-start(bf16[2,128,128]{2,1,0:T(8,128)(2,1)} %compress_density.1), channel_id=1, source_target_pairs={{0,1},{1,0},{2,3},{3,2},{4,5},{5,4},{6,7},{7,6},{8,9},{9,8},{10,11... | collective-permute-start | bytes 196616 | tf_op jit(solution)/shard_map/ppermute | solution.py:203
  6.0 1.4 %fusion.45 = (bf16[1,1,1,2,128,128]{5,4,3,2,1,0:T(8,128)(2,1)S(1)}, bf16[1,1,1,2,128,128]{5,4,3,2,1,0:T(8,128)(2,1)S(1)}, bf16[1,1,1,2,128,128]{5,4,3,2,1,0:T(8,...) fusion(bf16[1,9,2,2,128,128]{5,4,3,2,1,0:T(8,128)(2,1)} %param.16), kind=kLoop, calls=%fused_computation.91 | loop fusion | bytes 2359296 | tf_op jit(solution)/shard_map/slice | solution.py:226
  7.4 0.0 copy-start
  7.4 0.0 copy-start.2
  7.5 0.2 fusion.46
  7.7 1.3 %collective-permute-done = bf16[2,128,128]{2,1,0:T(8,128)(2,1)S(1)} collective-permute-done((bf16[2,128,128]{2,1,0:T(8,128)(2,1)}, bf16[2,128,128]{2,1,0:T(8,128)(2,1)S(1)}, u32[]{:S(2)}, u32[]{:S(2)}) %collective-permute-start) | collective-permute-done | bytes 65568 | tf_op jit(solution)/shard_map/ppermute | solution.py:203
  9.0 0.2 fusion.47
  9.2 4.9 %collective-permute-start.1 = (bf16[2,128,128]{2,1,0:T(8,128)(2,1)S(1)}, bf16[2,128,128]{2,1,0:T(8,128)(2,1)S(1)}, u32[]{:S(2)}, u32[]{:S(2)}) collective-permute-start(bf16[2,128,128]{2,1,0:T(8,128)(2,1)S(1)} %fusion.after), channel_id=1, source_target_pairs={{0,2},{1,3},{2,0},{3,1},{4,6},{5,7},{6,4},{7,5},{8,10},{9,11},{10,... | collective-permute-start | bytes 196616 | tf_op jit(solution)/shard_map/ppermute | solution.py:203
  14.2 2.5 %collective-permute-start.9 = (bf16[272,256]{1,0:T(8,128)(2,1)S(1)}, bf16[272,256]{1,0:T(8,128)(2,1)S(1)}, u32[]{:S(2)}, u32[]{:S(2)}) collective-permute-start(bf16[272,256]{1,0:T(8,128)(2,1)S(1)} %get-tuple-element.8), channel_id=1, source_target_pairs={{0,1},{1,2},{2,3},{3,4},{4,5},{5,6},{6,7},{7,8},{8,9},{9,10},{10,1... | collective-permute-start | bytes 417800 | tf_op jit(solution)/shard_map/ppermute | solution.py:213
  16.7 0.2 fusion.48
  17.0 0.2 fusion.49
  17.2 1.9 %collective-permute-start.2 = (bf16[2,128,128]{2,1,0:T(8,128)(2,1)S(1)}, bf16[2,128,128]{2,1,0:T(8,128)(2,1)S(1)}, u32[]{:S(2)}, u32[]{:S(2)}) collective-permute-start(bf16[2,128,128]{2,1,0:T(8,128)(2,1)S(1)} %fusion.1.after), channel_id=1, source_target_pairs={{0,4},{4,0},{8,12},{12,8},{16,20},{20,16},{24,28},{28,24},{32,36},... | collective-permute-start | bytes 196616 | tf_op jit(solution)/shard_map/ppermute | solution.py:203
  19.2 5.2 %collective-permute-start.10 = (bf16[272,256]{1,0:T(8,128)(2,1)S(1)}, bf16[272,256]{1,0:T(8,128)(2,1)S(1)}, u32[]{:S(2)}, u32[]{:S(2)}) collective-permute-start(bf16[272,256]{1,0:T(8,128)(2,1)S(1)} %head_strip.1), channel_id=1, source_target_pairs={{1,0},{2,1},{3,2},{4,3},{5,4},{6,5},{7,6},{8,7},{9,8},{10,9},{11,1... | collective-permute-start | bytes 417800 | tf_op jit(solution)/shard_map/ppermute | solution.py:213
  24.3 0.2 fusion.50
  24.6 0.2 fusion.51
  24.8 3.5 %collective-permute-start.3 = (bf16[2,128,128]{2,1,0:T(8,128)(2,1)S(1)}, bf16[2,128,128]{2,1,0:T(8,128)(2,1)S(1)}, u32[]{:S(2)}, u32[]{:S(2)}) collective-permute-start(bf16[2,128,128]{2,1,0:T(8,128)(2,1)S(1)} %fusion.2), channel_id=1, source_target_pairs={{0,8},{4,12},{8,0},{12,4},{16,24},{20,28},{24,16},{28,20},{32,40},... | collective-permute-start | bytes 196616 | tf_op jit(solution)/shard_map/ppermute | solution.py:203
  28.3 0.2 fusion.52
  28.5 0.0 copy-start.3
  28.5 0.0 copy-start.4
  28.5 2.5 %collective-permute-done.3 = bf16[2,128,128]{2,1,0:T(8,128)(2,1)S(1)} collective-permute-done((bf16[2,128,128]{2,1,0:T(8,128)(2,1)S(1)}, bf16[2,128,128]{2,1,0:T(8,128)(2,1)S(1)}, u32[]{:S(2)}, u32[]{:S(2)}) %collective-permute-start.3) | collective-permute-done | bytes 65568 | tf_op jit(solution)/shard_map/ppermute | solution.py:203
  31.0 0.2 fusion.53
  31.3 4.5 %collective-permute-start.4 = (bf16[2,128,128]{2,1,0:T(8,128)(2,1)S(1)}, bf16[2,128,128]{2,1,0:T(8,128)(2,1)S(1)}, u32[]{:S(2)}, u32[]{:S(2)}) collective-permute-start(bf16[2,128,128]{2,1,0:T(8,128)(2,1)S(1)} %fusion.3.after), channel_id=1, source_target_pairs={{0,16},{4,20},{8,24},{12,28},{16,0},{20,4},{24,8},{28,12},{32,48},... | collective-permute-start | bytes 196616 | tf_op jit(solution)/shard_map/ppermute | solution.py:203
  35.8 0.2 fusion.54
  36.0 2.3 %near_boxes.5 = f32[2,128,256]{2,1,0:T(8,128)S(1)} custom-call(s32[8]{0:T(128)S(1)} %copy-done.4, s32[8,27]{1,0:T(8,128)S(1)} %copy-done.3, bf16[256,1024]{1,0:T(8,128)(2,1)S(1)} %bitcast.149, bf16[16,1024]{1,0:T(8,128)(2,1)S(1)} %get-tuple-element.7.geometry, bf16[272,256]{1,0:T(8,128)(2,1)S(1)} %collective-permute-done.9.left, ...), custom_call_target="tpu_custom_call" | custom-call | flops 402653184 | bytes 2097152 | tf_op jit(solution)/shard_map/near_boxes/pallas_call | solution.py:302
  38.4 2.4 %near_boxes.4 = f32[2,128,256]{2,1,0:T(8,128)S(1)} custom-call(s32[8]{0:T(128)S(1)} %copy-done.4, s32[8,27]{1,0:T(8,128)S(1)} %copy-done.3, bf16[256,1024]{1,0:T(8,128)(2,1)S(1)} %bitcast.150, bf16[16,1024]{1,0:T(8,128)(2,1)S(1)} %get-tuple-element.7.geometry, bf16[272,256]{1,0:T(8,128)(2,1)S(1)} %collective-permute-done.9.left, ...), custom_call_target="tpu_custom_call" | custom-call | flops 402653184 | bytes 2097152 | tf_op jit(solution)/shard_map/near_boxes/pallas_call | solution.py:302
  40.8 0.2 fusion.55
  41.0 6.6 %collective-permute-start.5 = (bf16[2,128,128]{2,1,0:T(8,128)(2,1)S(1)}, bf16[2,128,128]{2,1,0:T(8,128)(2,1)S(1)}, u32[]{:S(2)}, u32[]{:S(2)}) collective-permute-start(bf16[2,128,128]{2,1,0:T(8,128)(2,1)S(1)} %fusion.4.after), channel_id=1, source_target_pairs={{0,32},{4,36},{8,40},{12,44},{16,48},{20,52},{24,56},{28,60},{32,0... | collective-permute-start | bytes 196616 | tf_op jit(solution)/shard_map/ppermute | solution.py:203
  47.6 0.2 fusion.56
  47.8 2.3 %near_boxes.7 = f32[2,128,256]{2,1,0:T(8,128)S(1)} custom-call(s32[8]{0:T(128)S(1)} %copy-done.4, s32[8,27]{1,0:T(8,128)S(1)} %copy-done.3, bf16[256,1024]{1,0:T(8,128)(2,1)S(1)} %bitcast.151, bf16[16,1024]{1,0:T(8,128)(2,1)S(1)} %get-tuple-element.7.geometry, bf16[272,256]{1,0:T(8,128)(2,1)S(1)} %collective-permute-done.9.left, ...), custom_call_target="tpu_custom_call" | custom-call | flops 402653184 | bytes 2097152 | tf_op jit(solution)/shard_map/near_boxes/pallas_call | solution.py:302
  50.2 2.4 %near_boxes.6 = f32[2,128,256]{2,1,0:T(8,128)S(1)} custom-call(s32[8]{0:T(128)S(1)} %copy-done.4, s32[8,27]{1,0:T(8,128)S(1)} %copy-done.3, bf16[256,1024]{1,0:T(8,128)(2,1)S(1)} %bitcast.152, bf16[16,1024]{1,0:T(8,128)(2,1)S(1)} %get-tuple-element.7.geometry, bf16[272,256]{1,0:T(8,128)(2,1)S(1)} %collective-permute-done.9.left, ...), custom_call_target="tpu_custom_call" | custom-call | flops 402653184 | bytes 2097152 | tf_op jit(solution)/shard_map/near_boxes/pallas_call | solution.py:302
  52.6 0.1 pad_maximum_fusion.near
  52.7 0.2 fusion.57
  52.9 4.3 %collective-permute-start.6 = (bf16[2,128,128]{2,1,0:T(8,128)(2,1)S(1)}, bf16[2,128,128]{2,1,0:T(8,128)(2,1)S(1)}, u32[]{:S(2)}, u32[]{:S(2)}) collective-permute-start(bf16[2,128,128]{2,1,0:T(8,128)(2,1)S(1)} %fusion.5), channel_id=1, source_target_pairs={{0,64},{4,68},{8,72},{12,76},{16,80},{20,84},{24,88},{28,92},{32,9... | collective-permute-start | bytes 196616 | tf_op jit(solution)/shard_map/ppermute | solution.py:203
  57.2 0.2 fusion.58
  57.5 2.0 %collective-permute-done.6 = bf16[2,128,128]{2,1,0:T(8,128)(2,1)S(1)} collective-permute-done((bf16[2,128,128]{2,1,0:T(8,128)(2,1)S(1)}, bf16[2,128,128]{2,1,0:T(8,128)(2,1)S(1)}, u32[]{:S(2)}, u32[]{:S(2)}) %collective-permute-start.6) | collective-permute-done | bytes 65568 | tf_op jit(solution)/shard_map/ppermute | solution.py:203
  59.5 0.2 fusion.59
  59.7 6.1 %collective-permute-start.7 = (bf16[2,128,128]{2,1,0:T(8,128)(2,1)S(1)}, bf16[2,128,128]{2,1,0:T(8,128)(2,1)S(1)}, u32[]{:S(2)}, u32[]{:S(2)}) collective-permute-start(bf16[2,128,128]{2,1,0:T(8,128)(2,1)S(1)} %fusion.6), channel_id=1, source_target_pairs={{0,128},{4,132},{8,136},{12,140},{16,144},{20,148},{24,152},{28,15... | collective-permute-start | bytes 196616 | tf_op jit(solution)/shard_map/ppermute | solution.py:203
  65.8 0.2 fusion.60
  66.0 2.0 %collective-permute-done.7 = bf16[2,128,128]{2,1,0:T(8,128)(2,1)S(1)} collective-permute-done((bf16[2,128,128]{2,1,0:T(8,128)(2,1)S(1)}, bf16[2,128,128]{2,1,0:T(8,128)(2,1)S(1)}, u32[]{:S(2)}, u32[]{:S(2)}) %collective-permute-start.7) | collective-permute-done | bytes 65568 | tf_op jit(solution)/shard_map/ppermute | solution.py:203
  68.0 0.2 fusion.61
  68.3 9.5 %collective-permute-start.8 = (bf16[2,128,128]{2,1,0:T(8,128)(2,1)S(1)}, bf16[2,128,128]{2,1,0:T(8,128)(2,1)S(1)}, u32[]{:S(2)}, u32[]{:S(2)}) collective-permute-start(bf16[2,128,128]{2,1,0:T(8,128)(2,1)S(1)} %fusion.7), channel_id=1, source_target_pairs={{0,256},{4,260},{8,264},{12,268},{16,272},{20,276},{24,280},{28,28... | collective-permute-start | bytes 196616 | tf_op jit(solution)/shard_map/ppermute | solution.py:203
  77.8 0.2 fusion.62
  78.0 2.2 %collective-permute-done.8 = bf16[2,128,128]{2,1,0:T(8,128)(2,1)S(1)} collective-permute-done((bf16[2,128,128]{2,1,0:T(8,128)(2,1)S(1)}, bf16[2,128,128]{2,1,0:T(8,128)(2,1)S(1)}, u32[]{:S(2)}, u32[]{:S(2)}) %collective-permute-start.8) | collective-permute-done | bytes 65568 | tf_op jit(solution)/shard_map/ppermute | solution.py:203
  80.2 0.2 fusion.63
  80.4 1.2 %expand_state.1 = bf16[2,128,1024]{2,1,0:T(8,128)(2,1)} custom-call(bf16[2,128,128]{2,1,0:T(8,128)(2,1)S(1)} %fusion.8.state, bf16[2,128,1024]{2,1,0:T(8,128)(2,1)S(1)} %copy-done.1, f32[2,128,1024]{2,1,0:T(8,128)S(1)} %pad_maximum_fusion.near), custom_call_target="tpu_custom_call" | custom-call | flops 134217728 | bytes 2097152 | tf_op jit(solution)/shard_map/expand_state/pallas_call | solution.py:319
  (43 shorter events, 0.6 us)
Async XLA Ops:
  2.5 5.0 %copy-start.5 = (bf16[2,128,128]{2,1,0:T(8,128)(2,1)S(1)}, bf16[2,128,128]{2,1,0:T(8,128)(2,1)}, u32[]{:S(2)}) copy-start(bf16[2,128,128]{2,1,0:T(8,128)(2,1)} %compress_density.1) | copy-start | bytes 196612
  2.5 5.2 %copy-start.6 = (bf16[1024]{0:T(1024)(128)(2,1)S(1)}, bf16[1024]{0:T(1024)(128)(2,1)}, u32[]{:S(2)}) copy-start(bf16[1024]{0:T(1024)(128)(2,1)} %param.11) | copy-start | bytes 6148
  2.5 6.5 %collective-permute-start = (bf16[2,128,128]{2,1,0:T(8,128)(2,1)}, bf16[2,128,128]{2,1,0:T(8,128)(2,1)S(1)}, u32[]{:S(2)}, u32[]{:S(2)}) collective-permute-start(bf16[2,128,128]{2,1,0:T(8,128)(2,1)} %compress_density.1), channel_id=1, source_target_pairs={{0,1},{1,0},{2,3},{3,2},{4,5},{5,4},{6,7},{7,6},{8,9},{9,8},{10,11... | collective-permute-start | bytes 196616 | tf_op jit(solution)/shard_map/ppermute | solution.py:203
  7.4 6.7 %copy-start = (bf16[2,128,1024]{2,1,0:T(8,128)(2,1)S(1)}, bf16[2,128,1024]{2,1,0:T(8,128)(2,1)}, u32[]{:S(2)}) copy-start(bf16[2,128,1024]{2,1,0:T(8,128)(2,1)} %param.9) | copy-start | bytes 1572868
  7.4 6.7 %copy-start.2 = (bf16[3,1024]{1,0:T(4,128)(2,1)S(1)}, bf16[3,1024]{1,0:T(4,128)(2,1)}, u32[]{:S(2)}) copy-start(bf16[3,1024]{1,0:T(4,128)(2,1)} %coords.1) | copy-start | bytes 18436
  9.2 7.7 %collective-permute-start.1 = (bf16[2,128,128]{2,1,0:T(8,128)(2,1)S(1)}, bf16[2,128,128]{2,1,0:T(8,128)(2,1)S(1)}, u32[]{:S(2)}, u32[]{:S(2)}) collective-permute-start(bf16[2,128,128]{2,1,0:T(8,128)(2,1)S(1)} %fusion.after), channel_id=1, source_target_pairs={{0,2},{1,3},{2,0},{3,1},{4,6},{5,7},{6,4},{7,5},{8,10},{9,11},{10,... | collective-permute-start | bytes 196616 | tf_op jit(solution)/shard_map/ppermute | solution.py:203
  14.2 21.8 %collective-permute-start.9 = (bf16[272,256]{1,0:T(8,128)(2,1)S(1)}, bf16[272,256]{1,0:T(8,128)(2,1)S(1)}, u32[]{:S(2)}, u32[]{:S(2)}) collective-permute-start(bf16[272,256]{1,0:T(8,128)(2,1)S(1)} %get-tuple-element.8), channel_id=1, source_target_pairs={{0,1},{1,2},{2,3},{3,4},{4,5},{5,6},{6,7},{7,8},{8,9},{9,10},{10,1... | collective-permute-start | bytes 417800 | tf_op jit(solution)/shard_map/ppermute | solution.py:213
  17.2 7.4 %collective-permute-start.2 = (bf16[2,128,128]{2,1,0:T(8,128)(2,1)S(1)}, bf16[2,128,128]{2,1,0:T(8,128)(2,1)S(1)}, u32[]{:S(2)}, u32[]{:S(2)}) collective-permute-start(bf16[2,128,128]{2,1,0:T(8,128)(2,1)S(1)} %fusion.1.after), channel_id=1, source_target_pairs={{0,4},{4,0},{8,12},{12,8},{16,20},{20,16},{24,28},{28,24},{32,36},... | collective-permute-start | bytes 196616 | tf_op jit(solution)/shard_map/ppermute | solution.py:203
  19.2 16.9 %collective-permute-start.10 = (bf16[272,256]{1,0:T(8,128)(2,1)S(1)}, bf16[272,256]{1,0:T(8,128)(2,1)S(1)}, u32[]{:S(2)}, u32[]{:S(2)}) collective-permute-start(bf16[272,256]{1,0:T(8,128)(2,1)S(1)} %head_strip.1), channel_id=1, source_target_pairs={{1,0},{2,1},{3,2},{4,3},{5,4},{6,5},{7,6},{8,7},{9,8},{10,9},{11,1... | collective-permute-start | bytes 417800 | tf_op jit(solution)/shard_map/ppermute | solution.py:213
  24.8 6.2 %collective-permute-start.3 = (bf16[2,128,128]{2,1,0:T(8,128)(2,1)S(1)}, bf16[2,128,128]{2,1,0:T(8,128)(2,1)S(1)}, u32[]{:S(2)}, u32[]{:S(2)}) collective-permute-start(bf16[2,128,128]{2,1,0:T(8,128)(2,1)S(1)} %fusion.2), channel_id=1, source_target_pairs={{0,8},{4,12},{8,0},{12,4},{16,24},{20,28},{24,16},{28,20},{32,40},... | collective-permute-start | bytes 196616 | tf_op jit(solution)/shard_map/ppermute | solution.py:203
  28.5 7.5 %copy-start.3 = (s32[8,27]{1,0:T(8,128)S(1)}, s32[8,27]{1,0:T(8,128)}, u32[]{:S(2)}) copy-start(s32[8,27]{1,0:T(8,128)} %neighbors.7) | copy-start | bytes 2596
  28.5 7.5 %copy-start.4 = (s32[8]{0:T(128)S(1)}, s32[8]{0:T(128)}, u32[]{:S(2)}) copy-start(s32[8]{0:T(128)} %counts.7) | copy-start | bytes 100
  31.3 9.5 %collective-permute-start.4 = (bf16[2,128,128]{2,1,0:T(8,128)(2,1)S(1)}, bf16[2,128,128]{2,1,0:T(8,128)(2,1)S(1)}, u32[]{:S(2)}, u32[]{:S(2)}) collective-permute-start(bf16[2,128,128]{2,1,0:T(8,128)(2,1)S(1)} %fusion.3.after), channel_id=1, source_target_pairs={{0,16},{4,20},{8,24},{12,28},{16,0},{20,4},{24,8},{28,12},{32,48},... | collective-permute-start | bytes 196616 | tf_op jit(solution)/shard_map/ppermute | solution.py:203
  41.0 11.7 %collective-permute-start.5 = (bf16[2,128,128]{2,1,0:T(8,128)(2,1)S(1)}, bf16[2,128,128]{2,1,0:T(8,128)(2,1)S(1)}, u32[]{:S(2)}, u32[]{:S(2)}) collective-permute-start(bf16[2,128,128]{2,1,0:T(8,128)(2,1)S(1)} %fusion.4.after), channel_id=1, source_target_pairs={{0,32},{4,36},{8,40},{12,44},{16,48},{20,52},{24,56},{28,60},{32,0... | collective-permute-start | bytes 196616 | tf_op jit(solution)/shard_map/ppermute | solution.py:203
  52.9 6.5 %collective-permute-start.6 = (bf16[2,128,128]{2,1,0:T(8,128)(2,1)S(1)}, bf16[2,128,128]{2,1,0:T(8,128)(2,1)S(1)}, u32[]{:S(2)}, u32[]{:S(2)}) collective-permute-start(bf16[2,128,128]{2,1,0:T(8,128)(2,1)S(1)} %fusion.5), channel_id=1, source_target_pairs={{0,64},{4,68},{8,72},{12,76},{16,80},{20,84},{24,88},{28,92},{32,9... | collective-permute-start | bytes 196616 | tf_op jit(solution)/shard_map/ppermute | solution.py:203
  59.7 8.3 %collective-permute-start.7 = (bf16[2,128,128]{2,1,0:T(8,128)(2,1)S(1)}, bf16[2,128,128]{2,1,0:T(8,128)(2,1)S(1)}, u32[]{:S(2)}, u32[]{:S(2)}) collective-permute-start(bf16[2,128,128]{2,1,0:T(8,128)(2,1)S(1)} %fusion.6), channel_id=1, source_target_pairs={{0,128},{4,132},{8,136},{12,140},{16,144},{20,148},{24,152},{28,15... | collective-permute-start | bytes 196616 | tf_op jit(solution)/shard_map/ppermute | solution.py:203
  68.2 12.2 %copy-start.1 = (bf16[2,128,1024]{2,1,0:T(8,128)(2,1)S(1)}, bf16[2,128,1024]{2,1,0:T(8,128)(2,1)}, u32[]{:S(2)}) copy-start(bf16[2,128,1024]{2,1,0:T(8,128)(2,1)} %expand.1) | copy-start | bytes 1572868
  68.3 11.9 %collective-permute-start.8 = (bf16[2,128,128]{2,1,0:T(8,128)(2,1)S(1)}, bf16[2,128,128]{2,1,0:T(8,128)(2,1)S(1)}, u32[]{:S(2)}, u32[]{:S(2)}) collective-permute-start(bf16[2,128,128]{2,1,0:T(8,128)(2,1)S(1)} %fusion.7), channel_id=1, source_target_pairs={{0,256},{4,260},{8,264},{12,268},{16,272},{20,276},{24,280},{28,28... | collective-permute-start | bytes 196616 | tf_op jit(solution)/shard_map/ppermute | solution.py:203

commit v3 on v2

--- a/solution.py
+++ b/solution.py
@@ -20,6 +20,9 @@
 NT = (((1,), (1,)), ((), ()))
 NN = (((1,), (0,)), ((), ()))
 TN = (((0,), (0,)), ((), ()))
+
+NEAR_PLAN = {4: 1, 5: 2, 6: 1, 7: 2}
+SECOND_HALO = 3
 
 VMEM_LIMIT = 16 * 1024 * 1024
 WHOLE_VMEM = 63 * 1024 * 1024
@@ -93,16 +96,13 @@
     strip[rows : rows + PACK, :] = geometry[:, 0:width]
 
 
-def near_kernel(first, counts, neighbors, density, geometry, left, right, after, out, tiles):
-    del after
-    rows, panels = density.shape
-    columns = rows // 2
+def prepare_kernel(counts, neighbors, geometry, left, right, source, target, factor):
+    rows = left.shape[0] - PACK
+    panels = geometry.shape[1]
     halo = left.shape[1]
     wide = panels + 2 * halo
     box_count, slot_count = neighbors.shape
     size = panels // box_count
-    wide_boxes = wide // size
-    boxes = out.shape[2] // size
 
     geo = jnp.concatenate(
         [left[rows : rows + PACK, :], geometry[...], right[rows : rows + PACK, :]], axis=1
@@ -116,8 +116,14 @@
         return [one, two, value - one - two]
 
     ones = jnp.ones_like(x)
-    source = rows_of(
+    source[...] = rows_of(
         [x, y, z] + split(square + SOFTENING * SOFTENING) + [ones] * 3, PACK, wide
+    ).astype(jnp.bfloat16)
+    at = slice(halo, halo + panels)
+    target[...] = rows_of(
+        [-2.0 * x[:, at], -2.0 * y[:, at], -2.0 * z[:, at]] + [ones[:, at]] * 3 + split(square[:, at]),
+        PACK,
+        panels,
     ).astype(jnp.bfloat16)
 
     slots = neighbors[...]
@@ -127,33 +133,34 @@
         live_count = jnp.where(box_id == b, counts[b], live_count)
     slot_id = lax.broadcasted_iota(jnp.int32, (box_count, slot_count), 1)
     slots = jnp.where(slot_id < live_count, slots, -1)
-    times = [
-        jnp.sum(jnp.where(slots == g, 1.0, 0.0), axis=1, keepdims=True) for g in range(wide_boxes)
-    ]
-
-    for i in range(boxes):
+    for g in range(wide // size):
+        times = jnp.sum(jnp.where(slots == g, 1.0 / FOUR_PI, 0.0), axis=1, keepdims=True)
+        span = slice(g * size, (g + 1) * size)
+        factor[:, span] = times * w[:, span]
+
+
+def near_kernel(first, density, left, right, source, target, factor, after, out, tiles):
+    del after
+    rows, panels = density.shape
+    columns = rows // 2
+    halo = left.shape[1]
+    wide = panels + 2 * halo
+    size = panels // factor.shape[0]
+    chunk = 2 * size
+
+    for i in range(out.shape[2] // size):
         b = first + i
-        start = halo + b * size
-        at = slice(start, start + size)
-        target = rows_of(
-            [-2.0 * x[:, at], -2.0 * y[:, at], -2.0 * z[:, at]] + [ones[:, at]] * 3 + split(square[:, at]),
-            PACK,
-            size,
-        ).astype(jnp.bfloat16)
-        for g in range(0, wide_boxes, 2):
-            span = slice(g * size, (g + 2) * size)
-            r2 = dot(target, source[:, span], TN)
+        mine = target[:, b * size : (b + 1) * size]
+        for begin in range(0, wide, chunk):
+            span = slice(begin, begin + chunk)
+            r2 = dot(mine, source[:, span], TN)
             inverse = lax.rsqrt(r2)
             radius = r2 * inverse
             f = radius - jnp.round(radius)
             q = f * f
             u = f * horner(SIN_COEFFS, q)
             v = horner(COS_COEFFS, q)
-            factor = w[:, span] * (1.0 / FOUR_PI)
-            many = jnp.concatenate(
-                [jnp.broadcast_to(times[g + j][b : b + 1], (1, size)) for j in range(2)], axis=1
-            )
-            a = inverse * (factor * many)
+            a = inverse * factor[b : b + 1, span]
             au = a * u
             tiles[i, 0:size, span] = (a - au * u).astype(jnp.bfloat16)
             tiles[i, size : 2 * size, span] = (au * v).astype(jnp.bfloat16)
@@ -165,20 +172,38 @@
         out[1, :, place] = total[:columns, size:] + total[columns:, :size]
 
 
-def tail_kernel(state, expand, near, out, block, sems):
-    columns, rank = state.shape[1:]
-    panels = expand.shape[2]
-    step = panels // sems.shape[0]
-    s = state[...].reshape(2 * columns, rank)
+def flatten(pair):
+    return pair.reshape(2 * pair.shape[1], pair.shape[2])
+
+
+def add_level(level, own, other, mix):
+    columns, rank = own.shape[1:]
+    product = dot(flatten(other[...]), flatten(mix[level, 1]), NT)
+    real = own[0] + product[:columns, :rank] - product[columns:, rank:]
+    imag = own[1] + product[:columns, rank:] + product[columns:, :rank]
+    return real.astype(jnp.bfloat16), imag.astype(jnp.bfloat16)
+
+
+def level_kernel(level, own, other, mix, *rest):
+    out = rest[-1]
+    out[0], out[1] = add_level(level, own, other, mix)
+
+
+def tail_kernel(level, own, other, mix, expand, *rest):
+    near, (out, block, sems) = rest[:-3], rest[-3:]
+    columns = own.shape[1]
+    s = jnp.concatenate(add_level(level, own, other, mix), axis=0)
     copies = []
-    for i in range(sems.shape[0]):
-        at = slice(i * step, (i + 1) * step)
+    start = 0
+    for i, piece in enumerate(near):
+        at = slice(start, start + piece.shape[2])
+        start += piece.shape[2]
         first = dot(s, expand[0, :, at], NN)
         second = dot(s, expand[1, :, at], NN)
         real = first[:columns] - second[columns:]
         imag = second[:columns] + first[columns:]
-        block[0, :, at] = (real + near[0, :, at]).astype(block.dtype)
-        block[1, :, at] = (imag + near[1, :, at]).astype(block.dtype)
+        block[0, :, at] = (real + piece[0]).astype(block.dtype)
+        block[1, :, at] = (imag + piece[1]).astype(block.dtype)
         copies.append(pltpu.make_async_copy(block.at[:, :, at], out.at[:, :, at], sems.at[i]))
         copies[-1].start()
     for copy in copies:
@@ -220,10 +245,6 @@
     real = product[:columns, :rank_rows] - product[columns:, rank_rows:]
     imag = product[:columns, rank_rows:] + product[columns:, :rank_rows]
     return jnp.stack([real, imag])
-
-
-def combine(own, other, matrices):
-    return (pair_product(own, matrices[0]) + pair_product(other, matrices[1])).astype(jnp.bfloat16)
 
 
 def per_device(density, coords, weights, counts, neighbors, skeleton, compress, mix, expand):
@@ -280,52 +301,87 @@
     sub_levels = lax.axis_size("sub").bit_length() - 1
     leaf_levels = lax.axis_size("leaf").bit_length() - 1
     steps = [("sub", i) for i in range(sub_levels)] + [("leaf", i) for i in range(leaf_levels)]
-    per_call = 2
-    calls = box_count // per_call
+    mixes = mix[0]
+    wide = panels + 2 * halo
+
+    def kernel(body, out_shape, operands, after=(), scratch=(), cost=cheap, name=None):
+        one = not isinstance(out_shape, tuple)
+        return pl.pallas_call(
+            body,
+            out_shape=out_shape,
+            in_specs=[in_vmem()] * len(operands) + [anywhere()] * len(after),
+            out_specs=in_vmem() if one else (in_vmem(),) * len(out_shape),
+            scratch_shapes=list(scratch),
+            compiler_params=params(),
+            cost_estimate=cost,
+            name=name,
+        )(*operands, *after)
+
+    def prepare():
+        return pl.pallas_call(
+            prepare_kernel,
+            out_shape=(
+                jax.ShapeDtypeStruct((PACK, wide), jnp.bfloat16),
+                jax.ShapeDtypeStruct((PACK, panels), jnp.bfloat16),
+                jax.ShapeDtypeStruct((box_count, wide), jnp.float32),
+            ),
+            in_specs=[pl.BlockSpec(memory_space=pltpu.SMEM)] + [in_vmem()] * 4,
+            out_specs=(in_vmem(),) * 3,
+            compiler_params=params(),
+            cost_estimate=cheap,
+            name="prepare_near",
+        )(counts, neighbors, geometry, left, right)
+
+    def near_boxes(first, boxes, after):
+        return kernel(
+            functools.partial(near_kernel, first),
+            jax.ShapeDtypeStruct((2, columns, boxes * size), jnp.float32),
+            [flat, left, right, source, target, factor],
+            [after],
+            [pltpu.VMEM((boxes, 2 * size, wide), jnp.bfloat16)],
+            pl.CostEstimate(
+                flops=2 * boxes * rows * wide * 2 * size, bytes_accessed=2**21, transcendentals=boxes * size * wide
+            ),
+            "near_boxes",
+        )
+
     near = []
-
-    def near_boxes(after):
-        call = pl.pallas_call(
-            functools.partial(near_kernel, len(near) * per_call),
-            out_shape=jax.ShapeDtypeStruct((2, columns, per_call * size), jnp.float32),
-            in_specs=[pl.BlockSpec(memory_space=pltpu.SMEM)] + [in_vmem()] * 5 + [anywhere()],
-            out_specs=in_vmem(),
-            scratch_shapes=[pltpu.VMEM((per_call, 2 * size, panels + 2 * halo), jnp.bfloat16)],
-            compiler_params=params(),
-            cost_estimate=pl.CostEstimate(
-                flops=2 * per_call * rows * (panels + 2 * halo) * 2 * size,
-                bytes_accessed=2**21,
-                transcendentals=per_call * size * (panels + 2 * halo),
-            ),
-            name="near_boxes",
-        )
-        near.append(call(counts, neighbors, flat, geometry, left, right, after))
-
+    done = 0
+    last = len(steps) - 1
     for level, (axis, stride) in enumerate(steps):
         other = exchange(state, axis, stride)
+        own = pair_product(state, mixes[level, 0])
+        ties = []
         if level == 1:
             geometry, strip_out = tail_strip(state)
             left = shift(strip_out, 1)
-        if level == 2:
+        if level == min(SECOND_HALO, last):
             right = shift(head_strip(state), -1)
-        if level in (4, 5):
-            near_boxes(state)
-            near_boxes(state)
-        state = combine(state, other, mix[0, level])
-    while len(near) < calls:
-        near_boxes(state)
-
-    near = jnp.concatenate(near, axis=2)
+        boxes = box_count - done if level == last else NEAR_PLAN.get(level, 0)
+        if boxes:
+            if not near:
+                source, target, factor = prepare()
+            near.append(near_boxes(done, boxes, state))
+            done += boxes
+            ties = near[-1:]
+        if level < last:
+            state = kernel(
+                functools.partial(level_kernel, level),
+                jax.ShapeDtypeStruct(state.shape, state.dtype),
+                [own, other, mixes],
+                ties,
+                name="level_state",
+            )
     return pl.pallas_call(
-        tail_kernel,
+        functools.partial(tail_kernel, last),
         out_shape=jax.ShapeDtypeStruct((2, columns, panels), jnp.bfloat16),
-        in_specs=[in_vmem()] * 3,
+        in_specs=[in_vmem()] * (4 + len(near)),
         out_specs=anywhere(),
-        scratch_shapes=[pltpu.VMEM((2, columns, panels), jnp.bfloat16), pltpu.SemaphoreType.DMA((4,))],
+        scratch_shapes=[pltpu.VMEM((2, columns, panels), jnp.bfloat16), pltpu.SemaphoreType.DMA((len(near),))],
         compiler_params=params(),
         cost_estimate=pl.CostEstimate(flops=4 * rows * rank * panels, bytes_accessed=2**21, transcendentals=0),
         name="expand_state",
-    )(state, expand, near)
+    )(own, other, mixes, expand, *near)
 
 
 def solution(mesh):

time: 82.1 us -> 78.8 us (0.960)
  the two profiles are of different devices: /device:TPU:16 before, /device:TPU:32 now
where the time goes in v3:
time: 78.8 us; the launch traced here: 78.3 us
  starting transfers between devices  51.6 us (65%)
  Pallas kernels  13.6 us (17%)
  waiting for transfers between devices  7.95 us (10%)
  matrix products  2.52 us (3%)
  local copies, waits for them, and re-layouts  1.86 us (2%)
    ppermute x9, starting transfers between devices, exchange(): return lax.ppermute(value, axis, pairs)  43.4 us
    pallas_call x13, Pallas kernels, kernel(): pl.pallas_call(body, out_shape=out_shape, in_specs=[in_vmem()] * len(oper...  9.04 us
    ppermute x2, starting transfers between devices, shift(): return lax.ppermute(value, axes, pairs)  8.22 us
    ppermute x9, waiting for transfers between devices, exchange(): return lax.ppermute(value, axis, pairs)  7.94 us
    dot_general x9, matrix products, dot(): lax.dot_general(left, right, dims, preferred_element_type=jnp.float32)  2.52 us
    pallas_call x1, Pallas kernels, per_device(): pl.pallas_call(head_kernel, out_shape=jax.ShapeDtypeStruct((2, columns, r...  2.45 us
  transfers between devices with their start and end apart: 11, of which 6 were waited for; matrix products, arithmetic and copies ran while one was open for 6% of the time, Pallas kernels for 11%

profile of v3, /device:TPU:32, one launch (start us, length us, event | category | flops | bytes accessed | tf_op | source)
XLA Modules:
  0.0 78.3 jit_solution(706862744915470776)
XLA Ops:
  0.0 2.4 %compress_density.1 = bf16[2,128,128]{2,1,0:T(8,128)(2,1)} custom-call(s32[1,128]{1,0:T(1,128)} %skeleton_hbm.1, bf16[256,1024]{1,0:T(8,128)(2,1)} %bitcast.85, bf16[256,1024]{1,0:T(8,128)(2,1)} %bitcast.101), custom_call_target="tpu_custom_call" | custom-call | flops 201326592 | bytes 1048576 | tf_op jit(solution)/shard_map/compress_density/pallas_call | solution.py:260
  2.5 0.0 copy-start
  2.5 3.5 %collective-permute-start = (bf16[2,128,128]{2,1,0:T(8,128)(2,1)}, bf16[2,128,128]{2,1,0:T(8,128)(2,1)S(1)}, u32[]{:S(2)}, u32[]{:S(2)}) collective-permute-start(bf16[2,128,128]{2,1,0:T(8,128)(2,1)} %compress_density.1), channel_id=1, source_target_pairs={{0,1},{1,0},{2,3},{3,2},{4,5},{5,4},{6,7},{7,6},{8,9},{9,8},{10,11... | collective-permute-start | bytes 196616 | tf_op jit(solution)/shard_map/ppermute | solution.py:228
  6.0 0.7 broadcast_in_dim.3.weights
  6.7 1.1 %fusion.18 = (bf16[1,1,2,128,128]{4,3,2,1,0:T(8,128)(2,1)S(1)}, bf16[1,1,2,128,128]{4,3,2,1,0:T(8,128)(2,1)S(1)}, bf16[1,1,2,128,128]{4,3,2,1,0:T(8,128)(2,1)S(1...) fusion(bf16[9,2,2,128,128]{4,3,2,1,0:T(8,128)(2,1)} %bitcast.75), kind=kLoop, calls=%fused_computation.45 | loop fusion | bytes 1179648 | tf_op jit(solution)/shard_map/slice | solution.py:353
  7.8 0.0 copy-start.1
  7.8 0.0 copy-start.3
  7.9 1.1 %fusion.19 = f32[256,256]{1,0:T(8,128)S(1)} fusion(bf16[256,128]{1,0:T(8,128)(2,1)} %bitcast.110, bf16[256,128]{1,0:T(8,128)(2,1)S(1)} %bitcast.111), kind=kOutput, calls=%fused_computation.46 | convolution fusion | flops 16777216 | bytes 393216 | tf_op jit(solution)/shard_map/dot_general | solution.py:32
  9.0 0.2 level_state.8.after
  9.2 4.9 %collective-permute-start.1 = (bf16[2,128,128]{2,1,0:T(8,128)(2,1)S(1)}, bf16[2,128,128]{2,1,0:T(8,128)(2,1)S(1)}, u32[]{:S(2)}, u32[]{:S(2)}) collective-permute-start(bf16[2,128,128]{2,1,0:T(8,128)(2,1)S(1)} %level_state.8.after), channel_id=1, source_target_pairs={{0,2},{1,3},{2,0},{3,1},{4,6},{5,7},{6,4},{7,5},{8,10},{9,11},{10,... | collective-permute-start | bytes 196616 | tf_op jit(solution)/shard_map/ppermute | solution.py:228
  14.2 2.5 %collective-permute-start.5 = (bf16[272,256]{1,0:T(8,128)(2,1)S(1)}, bf16[272,256]{1,0:T(8,128)(2,1)S(1)}, u32[]{:S(2)}, u32[]{:S(2)}) collective-permute-start(bf16[272,256]{1,0:T(8,128)(2,1)S(1)} %get-tuple-element.10), channel_id=1, source_target_pairs={{0,1},{1,2},{2,3},{3,4},{4,5},{5,6},{6,7},{7,8},{8,9},{9,10},{10,1... | collective-permute-start | bytes 417800 | tf_op jit(solution)/shard_map/ppermute | solution.py:238
  16.7 0.2 fusion.20
  16.9 0.2 level_state.9
  17.1 1.9 %collective-permute-start.2 = (bf16[2,128,128]{2,1,0:T(8,128)(2,1)S(1)}, bf16[2,128,128]{2,1,0:T(8,128)(2,1)S(1)}, u32[]{:S(2)}, u32[]{:S(2)}) collective-permute-start(bf16[2,128,128]{2,1,0:T(8,128)(2,1)S(1)} %level_state.9), channel_id=1, source_target_pairs={{0,4},{4,0},{8,12},{12,8},{16,20},{20,16},{24,28},{28,24},{32,36},... | collective-permute-start | bytes 196616 | tf_op jit(solution)/shard_map/ppermute | solution.py:228
  19.0 0.2 fusion.21
  19.3 1.0 %collective-permute-done.2.other = bf16[2,128,128]{2,1,0:T(8,128)(2,1)S(1)} collective-permute-done((bf16[2,128,128]{2,1,0:T(8,128)(2,1)S(1)}, bf16[2,128,128]{2,1,0:T(8,128)(2,1)S(1)}, u32[]{:S(2)}, u32[]{:S(2)}) %collective-permute-start.2) | collective-permute-done | bytes 65568 | tf_op jit(solution)/shard_map/ppermute | solution.py:228
  20.3 0.2 level_state.10.after
  20.5 2.6 %collective-permute-start.3 = (bf16[2,128,128]{2,1,0:T(8,128)(2,1)S(1)}, bf16[2,128,128]{2,1,0:T(8,128)(2,1)S(1)}, u32[]{:S(2)}, u32[]{:S(2)}) collective-permute-start(bf16[2,128,128]{2,1,0:T(8,128)(2,1)S(1)} %level_state.10.after), channel_id=1, source_target_pairs={{0,8},{4,12},{8,0},{12,4},{16,24},{20,28},{24,16},{28,20},{32,40},... | collective-permute-start | bytes 196616 | tf_op jit(solution)/shard_map/ppermute | solution.py:228
  23.1 5.7 %collective-permute-start.6 = (bf16[272,256]{1,0:T(8,128)(2,1)S(1)}, bf16[272,256]{1,0:T(8,128)(2,1)S(1)}, u32[]{:S(2)}, u32[]{:S(2)}) collective-permute-start(bf16[272,256]{1,0:T(8,128)(2,1)S(1)} %head_strip.1), channel_id=1, source_target_pairs={{1,0},{2,1},{3,2},{4,3},{5,4},{6,5},{7,6},{8,7},{9,8},{10,9},{11,1... | collective-permute-start | bytes 417800 | tf_op jit(solution)/shard_map/ppermute | solution.py:238
  28.8 0.2 fusion.22
  29.0 0.0 copy-start.4
  29.1 0.2 level_state.11.after
  29.3 2.5 %collective-permute-start.4 = (bf16[2,128,128]{2,1,0:T(8,128)(2,1)S(1)}, bf16[2,128,128]{2,1,0:T(8,128)(2,1)S(1)}, u32[]{:S(2)}, u32[]{:S(2)}) collective-permute-start(bf16[2,128,128]{2,1,0:T(8,128)(2,1)S(1)} %level_state.11.after), channel_id=1, source_target_pairs={{0,16},{4,20},{8,24},{12,28},{16,0},{20,4},{24,8},{28,12},{32,48},... | collective-permute-start | bytes 196616 | tf_op jit(solution)/shard_map/ppermute | solution.py:228
  31.8 0.2 fusion.23
  32.1 0.6 prepare_near.1
  32.7 1.1 %near_boxes.5.rest_0_ = f32[2,128,128]{2,1,0:T(8,128)S(1)} custom-call(bf16[256,1024]{1,0:T(8,128)(2,1)S(1)} %bitcast.88, bf16[272,256]{1,0:T(8,128)(2,1)S(1)} %collective-permute-done.5.left, bf16[272,256]{1,0:T(8,128)(2,1)S(1)} %collective-permute-done.6.right, bf16[16,1536]{1,0:T(8,128)(2,1)S(1)} %get-tuple-element.12.source, ...), custom_call_target="tpu_custom_call" | custom-call | flops 201326592 | bytes 2097152 | tf_op jit(solution)/shard_map/near_boxes/pallas_call | solution.py:309
  33.8 2.7 %collective-permute-done.4.other = bf16[2,128,128]{2,1,0:T(8,128)(2,1)S(1)} collective-permute-done((bf16[2,128,128]{2,1,0:T(8,128)(2,1)S(1)}, bf16[2,128,128]{2,1,0:T(8,128)(2,1)S(1)}, u32[]{:S(2)}, u32[]{:S(2)}) %collective-permute-start.4) | collective-permute-done | bytes 65568 | tf_op jit(solution)/shard_map/ppermute | solution.py:228
  36.5 0.2 level_state.12.after
  36.7 5.2 %collective-permute-start.7 = (bf16[2,128,128]{2,1,0:T(8,128)(2,1)S(1)}, bf16[2,128,128]{2,1,0:T(8,128)(2,1)S(1)}, u32[]{:S(2)}, u32[]{:S(2)}) collective-permute-start(bf16[2,128,128]{2,1,0:T(8,128)(2,1)S(1)} %level_state.12.after), channel_id=1, source_target_pairs={{0,32},{4,36},{8,40},{12,44},{16,48},{20,52},{24,56},{28,60},{32,0... | collective-permute-start | bytes 196616 | tf_op jit(solution)/shard_map/ppermute | solution.py:228
  41.9 0.2 fusion.24
  42.2 1.8 %near_boxes.6.rest_0_.rest_1_ = f32[2,128,256]{2,1,0:T(8,128)S(1)} custom-call(bf16[256,1024]{1,0:T(8,128)(2,1)S(1)} %bitcast.89, bf16[272,256]{1,0:T(8,128)(2,1)S(1)} %collective-permute-done.5.left, bf16[272,256]{1,0:T(8,128)(2,1)S(1)} %collective-permute-done.6.right, bf16[16,1536]{1,0:T(8,128)(2,1)S(1)} %get-tuple-element.12.source, ...), custom_call_target="tpu_custom_call" | custom-call | flops 402653184 | bytes 2097152 | tf_op jit(solution)/shard_map/near_boxes/pallas_call | solution.py:309
  44.0 2.9 %collective-permute-done.7.other = bf16[2,128,128]{2,1,0:T(8,128)(2,1)S(1)} collective-permute-done((bf16[2,128,128]{2,1,0:T(8,128)(2,1)S(1)}, bf16[2,128,128]{2,1,0:T(8,128)(2,1)S(1)}, u32[]{:S(2)}, u32[]{:S(2)}) %collective-permute-start.7) | collective-permute-done | bytes 65568 | tf_op jit(solution)/shard_map/ppermute | solution.py:228
  46.9 0.2 level_state.13.after
  47.1 4.8 %collective-permute-start.8 = (bf16[2,128,128]{2,1,0:T(8,128)(2,1)S(1)}, bf16[2,128,128]{2,1,0:T(8,128)(2,1)S(1)}, u32[]{:S(2)}, u32[]{:S(2)}) collective-permute-start(bf16[2,128,128]{2,1,0:T(8,128)(2,1)S(1)} %level_state.13.after), channel_id=1, source_target_pairs={{0,64},{4,68},{8,72},{12,76},{16,80},{20,84},{24,88},{28,92},{32,9... | collective-permute-start | bytes 196616 | tf_op jit(solution)/shard_map/ppermute | solution.py:228
  51.9 0.2 fusion.25
  52.1 1.1 %near_boxes.7.rest_0_.rest_2_ = f32[2,128,128]{2,1,0:T(8,128)S(1)} custom-call(bf16[256,1024]{1,0:T(8,128)(2,1)S(1)} %bitcast.90, bf16[272,256]{1,0:T(8,128)(2,1)S(1)} %collective-permute-done.5.left, bf16[272,256]{1,0:T(8,128)(2,1)S(1)} %collective-permute-done.6.right, bf16[16,1536]{1,0:T(8,128)(2,1)S(1)} %get-tuple-element.12.source, ...), custom_call_target="tpu_custom_call" | custom-call | flops 201326592 | bytes 2097152 | tf_op jit(solution)/shard_map/near_boxes/pallas_call | solution.py:309
  53.2 0.9 %collective-permute-done.8.other = bf16[2,128,128]{2,1,0:T(8,128)(2,1)S(1)} collective-permute-done((bf16[2,128,128]{2,1,0:T(8,128)(2,1)S(1)}, bf16[2,128,128]{2,1,0:T(8,128)(2,1)S(1)}, u32[]{:S(2)}, u32[]{:S(2)}) %collective-permute-start.8) | collective-permute-done | bytes 65568 | tf_op jit(solution)/shard_map/ppermute | solution.py:228
  54.1 0.2 level_state.14.after
  54.3 6.1 %collective-permute-start.9 = (bf16[2,128,128]{2,1,0:T(8,128)(2,1)S(1)}, bf16[2,128,128]{2,1,0:T(8,128)(2,1)S(1)}, u32[]{:S(2)}, u32[]{:S(2)}) collective-permute-start(bf16[2,128,128]{2,1,0:T(8,128)(2,1)S(1)} %level_state.14.after), channel_id=1, source_target_pairs={{0,128},{4,132},{8,136},{12,140},{16,144},{20,148},{24,152},{28,15... | collective-permute-start | bytes 196616 | tf_op jit(solution)/shard_map/ppermute | solution.py:228
  60.4 0.2 fusion.26
  60.6 1.8 %near_boxes.8.rest_0_.rest_3_ = f32[2,128,256]{2,1,0:T(8,128)S(1)} custom-call(bf16[256,1024]{1,0:T(8,128)(2,1)S(1)} %bitcast.91, bf16[272,256]{1,0:T(8,128)(2,1)S(1)} %collective-permute-done.5.left, bf16[272,256]{1,0:T(8,128)(2,1)S(1)} %collective-permute-done.6.right, bf16[16,1536]{1,0:T(8,128)(2,1)S(1)} %get-tuple-element.12.source, ...), custom_call_target="tpu_custom_call" | custom-call | flops 402653184 | bytes 2097152 | tf_op jit(solution)/shard_map/near_boxes/pallas_call | solution.py:309
  62.4 0.2 collective-permute-done.9.other
  62.6 0.2 level_state.15.after
  62.8 11.9 %collective-permute-start.10 = (bf16[2,128,128]{2,1,0:T(8,128)(2,1)S(1)}, bf16[2,128,128]{2,1,0:T(8,128)(2,1)S(1)}, u32[]{:S(2)}, u32[]{:S(2)}) collective-permute-start(bf16[2,128,128]{2,1,0:T(8,128)(2,1)S(1)} %level_state.15.after), channel_id=1, source_target_pairs={{0,256},{4,260},{8,264},{12,268},{16,272},{20,276},{24,280},{28,28... | collective-permute-start | bytes 196616 | tf_op jit(solution)/shard_map/ppermute | solution.py:228
  74.7 0.2 fusion.27
  75.0 1.8 %near_boxes.9.rest_4_ = f32[2,128,256]{2,1,0:T(8,128)S(1)} custom-call(bf16[256,1024]{1,0:T(8,128)(2,1)S(1)} %bitcast.92, bf16[272,256]{1,0:T(8,128)(2,1)S(1)} %collective-permute-done.5.left, bf16[272,256]{1,0:T(8,128)(2,1)S(1)} %collective-permute-done.6.right, bf16[16,1536]{1,0:T(8,128)(2,1)S(1)} %get-tuple-element.12.source, ...), custom_call_target="tpu_custom_call" | custom-call | flops 402653184 | bytes 2097152 | tf_op jit(solution)/shard_map/near_boxes/pallas_call | solution.py:309
  76.8 0.2 collective-permute-done.10.other
  76.9 1.4 %expand_state.1 = bf16[2,128,1024]{2,1,0:T(8,128)(2,1)} custom-call(f32[2,128,128]{2,1,0:T(8,128)S(1)} %pad_maximum_fusion.8.own, bf16[2,128,128]{2,1,0:T(8,128)(2,1)S(1)} %collective-permute-done.10.other, bf16[9,2,2,128,128]{4,3,2,1,0:T(8,128)(2,1)S(1)} %bitcast.84, bf16[2,128,1024]{2,1,0:T(8,128)(2,1)S(1)} %copy-done.2, ...), custom_call_target="tpu_custom_call" | custom-call | flops 134217728 | bytes 2097152 | tf_op jit(solution)/shard_map/expand_state/pallas_call | solution.py:375
  (33 shorter events, 0.3 us)
Async XLA Ops:
  2.5 6.5 %copy-start = (bf16[1,9,2,2,128,128]{5,4,3,2,1,0:T(8,128)(2,1)S(1)}, bf16[1,9,2,2,128,128]{5,4,3,2,1,0:T(8,128)(2,1)}, u32[]{:S(2)}) copy-start(bf16[1,9,2,2,128,128]{5,4,3,2,1,0:T(8,128)(2,1)} %param.16) | copy-start | bytes 3538948
  2.5 6.5 %collective-permute-start = (bf16[2,128,128]{2,1,0:T(8,128)(2,1)}, bf16[2,128,128]{2,1,0:T(8,128)(2,1)S(1)}, u32[]{:S(2)}, u32[]{:S(2)}) collective-permute-start(bf16[2,128,128]{2,1,0:T(8,128)(2,1)} %compress_density.1), channel_id=1, source_target_pairs={{0,1},{1,0},{2,3},{3,2},{4,5},{5,4},{6,7},{7,6},{8,9},{9,8},{10,11... | collective-permute-start | bytes 196616 | tf_op jit(solution)/shard_map/ppermute | solution.py:228
  7.8 6.3 %copy-start.1 = (bf16[2,128,1024]{2,1,0:T(8,128)(2,1)S(1)}, bf16[2,128,1024]{2,1,0:T(8,128)(2,1)}, u32[]{:S(2)}) copy-start(bf16[2,128,1024]{2,1,0:T(8,128)(2,1)} %param.9) | copy-start | bytes 1572868
  7.8 6.3 %copy-start.3 = (bf16[3,1024]{1,0:T(4,128)(2,1)S(1)}, bf16[3,1024]{1,0:T(4,128)(2,1)}, u32[]{:S(2)}) copy-start(bf16[3,1024]{1,0:T(4,128)(2,1)} %coords.1) | copy-start | bytes 18436
  9.2 7.7 %collective-permute-start.1 = (bf16[2,128,128]{2,1,0:T(8,128)(2,1)S(1)}, bf16[2,128,128]{2,1,0:T(8,128)(2,1)S(1)}, u32[]{:S(2)}, u32[]{:S(2)}) collective-permute-start(bf16[2,128,128]{2,1,0:T(8,128)(2,1)S(1)} %level_state.8.after), channel_id=1, source_target_pairs={{0,2},{1,3},{2,0},{3,1},{4,6},{5,7},{6,4},{7,5},{8,10},{9,11},{10,... | collective-permute-start | bytes 196616 | tf_op jit(solution)/shard_map/ppermute | solution.py:228
  14.2 17.9 %collective-permute-start.5 = (bf16[272,256]{1,0:T(8,128)(2,1)S(1)}, bf16[272,256]{1,0:T(8,128)(2,1)S(1)}, u32[]{:S(2)}, u32[]{:S(2)}) collective-permute-start(bf16[272,256]{1,0:T(8,128)(2,1)S(1)} %get-tuple-element.10), channel_id=1, source_target_pairs={{0,1},{1,2},{2,3},{3,4},{4,5},{5,6},{6,7},{7,8},{8,9},{9,10},{10,1... | collective-permute-start | bytes 417800 | tf_op jit(solution)/shard_map/ppermute | solution.py:238
  17.1 3.1 %collective-permute-start.2 = (bf16[2,128,128]{2,1,0:T(8,128)(2,1)S(1)}, bf16[2,128,128]{2,1,0:T(8,128)(2,1)S(1)}, u32[]{:S(2)}, u32[]{:S(2)}) collective-permute-start(bf16[2,128,128]{2,1,0:T(8,128)(2,1)S(1)} %level_state.9), channel_id=1, source_target_pairs={{0,4},{4,0},{8,12},{12,8},{16,20},{20,16},{24,28},{28,24},{32,36},... | collective-permute-start | bytes 196616 | tf_op jit(solution)/shard_map/ppermute | solution.py:228
  20.5 8.6 %collective-permute-start.3 = (bf16[2,128,128]{2,1,0:T(8,128)(2,1)S(1)}, bf16[2,128,128]{2,1,0:T(8,128)(2,1)S(1)}, u32[]{:S(2)}, u32[]{:S(2)}) collective-permute-start(bf16[2,128,128]{2,1,0:T(8,128)(2,1)S(1)} %level_state.10.after), channel_id=1, source_target_pairs={{0,8},{4,12},{8,0},{12,4},{16,24},{20,28},{24,16},{28,20},{32,40},... | collective-permute-start | bytes 196616 | tf_op jit(solution)/shard_map/ppermute | solution.py:228
  23.1 9.0 %collective-permute-start.6 = (bf16[272,256]{1,0:T(8,128)(2,1)S(1)}, bf16[272,256]{1,0:T(8,128)(2,1)S(1)}, u32[]{:S(2)}, u32[]{:S(2)}) collective-permute-start(bf16[272,256]{1,0:T(8,128)(2,1)S(1)} %head_strip.1), channel_id=1, source_target_pairs={{1,0},{2,1},{3,2},{4,3},{5,4},{6,5},{7,6},{8,7},{9,8},{10,9},{11,1... | collective-permute-start | bytes 417800 | tf_op jit(solution)/shard_map/ppermute | solution.py:238
  29.0 3.0 %copy-start.4 = (s32[8,27]{1,0:T(8,128)S(1)}, s32[8,27]{1,0:T(8,128)}, u32[]{:S(2)}) copy-start(s32[8,27]{1,0:T(8,128)} %neighbors.1) | copy-start | bytes 2596
  29.0 3.0 %copy-start.5 = (s32[8]{0:T(128)S(1)}, s32[8]{0:T(128)}, u32[]{:S(2)}) copy-start(s32[8]{0:T(128)} %counts.1) | copy-start | bytes 100
  29.3 7.3 %collective-permute-start.4 = (bf16[2,128,128]{2,1,0:T(8,128)(2,1)S(1)}, bf16[2,128,128]{2,1,0:T(8,128)(2,1)S(1)}, u32[]{:S(2)}, u32[]{:S(2)}) collective-permute-start(bf16[2,128,128]{2,1,0:T(8,128)(2,1)S(1)} %level_state.11.after), channel_id=1, source_target_pairs={{0,16},{4,20},{8,24},{12,28},{16,0},{20,4},{24,8},{28,12},{32,48},... | collective-permute-start | bytes 196616 | tf_op jit(solution)/shard_map/ppermute | solution.py:228
  36.7 10.2 %collective-permute-start.7 = (bf16[2,128,128]{2,1,0:T(8,128)(2,1)S(1)}, bf16[2,128,128]{2,1,0:T(8,128)(2,1)S(1)}, u32[]{:S(2)}, u32[]{:S(2)}) collective-permute-start(bf16[2,128,128]{2,1,0:T(8,128)(2,1)S(1)} %level_state.12.after), channel_id=1, source_target_pairs={{0,32},{4,36},{8,40},{12,44},{16,48},{20,52},{24,56},{28,60},{32,0... | collective-permute-start | bytes 196616 | tf_op jit(solution)/shard_map/ppermute | solution.py:228
  47.1 7.0 %collective-permute-start.8 = (bf16[2,128,128]{2,1,0:T(8,128)(2,1)S(1)}, bf16[2,128,128]{2,1,0:T(8,128)(2,1)S(1)}, u32[]{:S(2)}, u32[]{:S(2)}) collective-permute-start(bf16[2,128,128]{2,1,0:T(8,128)(2,1)S(1)} %level_state.13.after), channel_id=1, source_target_pairs={{0,64},{4,68},{8,72},{12,76},{16,80},{20,84},{24,88},{28,92},{32,9... | collective-permute-start | bytes 196616 | tf_op jit(solution)/shard_map/ppermute | solution.py:228
  54.3 8.3 %collective-permute-start.9 = (bf16[2,128,128]{2,1,0:T(8,128)(2,1)S(1)}, bf16[2,128,128]{2,1,0:T(8,128)(2,1)S(1)}, u32[]{:S(2)}, u32[]{:S(2)}) collective-permute-start(bf16[2,128,128]{2,1,0:T(8,128)(2,1)S(1)} %level_state.14.after), channel_id=1, source_target_pairs={{0,128},{4,132},{8,136},{12,140},{16,144},{20,148},{24,152},{28,15... | collective-permute-start | bytes 196616 | tf_op jit(solution)/shard_map/ppermute | solution.py:228
  62.8 14.1 %collective-permute-start.10 = (bf16[2,128,128]{2,1,0:T(8,128)(2,1)S(1)}, bf16[2,128,128]{2,1,0:T(8,128)(2,1)S(1)}, u32[]{:S(2)}, u32[]{:S(2)}) collective-permute-start(bf16[2,128,128]{2,1,0:T(8,128)(2,1)S(1)} %level_state.15.after), channel_id=1, source_target_pairs={{0,256},{4,260},{8,264},{12,268},{16,272},{20,276},{24,280},{28,28... | collective-permute-start | bytes 196616 | tf_op jit(solution)/shard_map/ppermute | solution.py:228
  74.7 2.2 %copy-start.2 = (bf16[2,128,1024]{2,1,0:T(8,128)(2,1)S(1)}, bf16[2,128,1024]{2,1,0:T(8,128)(2,1)}, u32[]{:S(2)}) copy-start(bf16[2,128,1024]{2,1,0:T(8,128)(2,1)} %expand.1) | copy-start | bytes 1572868

commit v4 on v3

--- a/solution.py
+++ b/solution.py
@@ -21,8 +21,9 @@
 NN = (((1,), (0,)), ((), ()))
 TN = (((0,), (0,)), ((), ()))
 
-NEAR_PLAN = {4: 1, 5: 2, 6: 1, 7: 2}
-SECOND_HALO = 3
+NEAR_PLAN = {5: 2, 6: 2, 7: 2}
+FIRST_HALO = 3
+SECOND_HALO = 4
 
 VMEM_LIMIT = 16 * 1024 * 1024
 WHOLE_VMEM = 63 * 1024 * 1024
@@ -47,11 +48,12 @@
     return total
 
 
-def head_kernel(skeleton_hbm, density_hbm, compress_hbm, state, skeleton, density, compress, sems):
+def head_kernel(skeleton_hbm, density_hbm, compress_hbm, mix, state, first_mix, skeleton, density, compress, sems):
     copies = [
         pltpu.make_async_copy(skeleton_hbm, skeleton, sems.at[0]),
         pltpu.make_async_copy(density_hbm, density, sems.at[1]),
         pltpu.make_async_copy(compress_hbm, compress, sems.at[2]),
+        pltpu.make_async_copy(mix.at[0], first_mix, sems.at[3]),
     ]
     for copy in copies:
         copy.start()
@@ -68,8 +70,10 @@
     product = dot(d, compress[...], NT)
     real = product[:columns, :rank] - product[columns:, rank:] + picked[:columns]
     imag = product[:columns, rank:] + product[columns:, :rank] + picked[columns:]
-    state[0] = real.astype(state.dtype)
-    state[1] = imag.astype(state.dtype)
+    for i in range(state.shape[0]):
+        state[i, 0] = real.astype(state.dtype)
+        state[i, 1] = imag.astype(state.dtype)
+    copies[3].wait()
 
 
 def geometry_rows(coords, weights, count):
@@ -184,6 +188,28 @@
     return real.astype(jnp.bfloat16), imag.astype(jnp.bfloat16)
 
 
+def apply(states, matrices):
+    columns, rank = states[0].shape[0] // 2, states[0].shape[1]
+    total = dot(states[0], flatten(matrices[0]), NT)
+    for state, matrix in zip(states[1:], matrices[1:]):
+        total += dot(state, flatten(matrix), NT)
+    real = total[:columns, :rank] - total[columns:, rank:]
+    imag = total[:columns, rank:] + total[columns:, :rank]
+    return jnp.concatenate([real, imag], axis=0).astype(jnp.bfloat16)
+
+
+def two_level_kernel(gathered, far_mix, mix, *rest):
+    out = rest[-1]
+    me = lax.axis_index("sub")
+    states = [flatten(gathered[me ^ k]) for k in range(4)]
+    mine = apply(states[:2], [mix[0, 0], mix[0, 1]])
+    partner = apply(states[2:], [far_mix[0], far_mix[1]])
+    result = apply([mine, partner], [mix[1, 0], mix[1, 1]])
+    columns = out.shape[1]
+    out[0] = result[:columns]
+    out[1] = result[columns:]
+
+
 def level_kernel(level, own, other, mix, *rest):
     out = rest[-1]
     out[0], out[1] = add_level(level, own, other, mix)
@@ -257,21 +283,25 @@
     flat = density.reshape(rows, panels)
     basis = compress.reshape(2 * rank, panels)
 
-    state = pl.pallas_call(
+    mixes = mix[0]
+    copies, first_mix = pl.pallas_call(
         head_kernel,
-        out_shape=jax.ShapeDtypeStruct((2, columns, rank), jnp.bfloat16),
-        in_specs=[pl.BlockSpec(memory_space=pltpu.HBM)] * 3,
-        out_specs=in_vmem(),
+        out_shape=(
+            jax.ShapeDtypeStruct((4, 2, columns, rank), jnp.bfloat16),
+            jax.ShapeDtypeStruct(mixes.shape[1:], jnp.bfloat16),
+        ),
+        in_specs=[pl.BlockSpec(memory_space=pltpu.HBM)] * 4,
+        out_specs=(in_vmem(), in_vmem()),
         scratch_shapes=[
             pltpu.VMEM(skeleton.shape, skeleton.dtype),
             pltpu.VMEM(flat.shape, flat.dtype),
             pltpu.VMEM(basis.shape, basis.dtype),
-            pltpu.SemaphoreType.DMA((3,)),
+            pltpu.SemaphoreType.DMA((4,)),
         ],
         compiler_params=params(WHOLE_VMEM),
         cost_estimate=pl.CostEstimate(flops=2 * rows * panels * 3 * rank, bytes_accessed=2**20, transcendentals=0),
         name="compress_density",
-    )(skeleton, flat, basis)
+    )(skeleton, flat, basis, mixes)
 
     strip = jax.ShapeDtypeStruct((rows + PACK, halo), jnp.bfloat16)
     cheap = pl.CostEstimate(flops=2**20, bytes_accessed=2**18, transcendentals=0)
@@ -301,7 +331,6 @@
     sub_levels = lax.axis_size("sub").bit_length() - 1
     leaf_levels = lax.axis_size("leaf").bit_length() - 1
     steps = [("sub", i) for i in range(sub_levels)] + [("leaf", i) for i in range(leaf_levels)]
-    mixes = mix[0]
     wide = panels + 2 * halo
 
     def kernel(body, out_shape, operands, after=(), scratch=(), cost=cheap, name=None):
@@ -348,11 +377,19 @@
     near = []
     done = 0
     last = len(steps) - 1
-    for level, (axis, stride) in enumerate(steps):
+    far_mix = exchange(first_mix, *steps[1])
+    gathered = lax.all_to_all(copies, "sub", 0, 0)
+    state = kernel(
+        two_level_kernel,
+        jax.ShapeDtypeStruct((2, columns, rank), jnp.bfloat16),
+        [gathered, far_mix, mixes],
+        name="levels_0_1",
+    )
+    for level, (axis, stride) in list(enumerate(steps))[2:]:
         other = exchange(state, axis, stride)
         own = pair_product(state, mixes[level, 0])
         ties = []
-        if level == 1:
+        if level == min(FIRST_HALO, last):
             geometry, strip_out = tail_strip(state)
             left = shift(strip_out, 1)
         if level == min(SECOND_HALO, last):

time: 78.8 us -> 76.9 us (0.976)
  the two profiles are of different devices: /device:TPU:32 before, /device:TPU:16 now
where the time goes in v4:
time: 76.9 us; the launch traced here: 76.4 us
  starting transfers between devices  49.4 us (64%)
  Pallas kernels  13.5 us (18%)
  waiting for transfers between devices  10.4 us (14%)
  matrix products  1.27 us (2%)
  local copies, waits for them, and re-layouts  1.11 us (1%)
    ppermute x8, starting transfers between devices, exchange(): return lax.ppermute(value, axis, pairs)  37.9 us
    ppermute x8, waiting for transfers between devices, exchange(): return lax.ppermute(value, axis, pairs)  10.4 us
    pallas_call x11, Pallas kernels, kernel(): pl.pallas_call(body, out_shape=out_shape, in_specs=[in_vmem()] * len(oper...  8.89 us
    ppermute x2, starting transfers between devices, shift(): return lax.ppermute(value, axes, pairs)  7.02 us
    all_to_all x1, starting transfers between devices, per_device(): gathered = lax.all_to_all(copies, 'sub', 0, 0)  4.44 us
    pallas_call x1, Pallas kernels, per_device(): pl.pallas_call(head_kernel, out_shape=(jax.ShapeDtypeStruct((4, 2, column...  2.58 us
  transfers between devices with their start and end apart: 11, of which 6 were waited for; matrix products, arithmetic and copies ran while one was open for 3% of the time, Pallas kernels for 11%

profile of v4, /device:TPU:16, one launch (start us, length us, event | category | flops | bytes accessed | tf_op | source)
XLA Modules:
  0.0 76.4 jit_solution(2566213333482116111)
XLA Ops:
  0.0 2.6 %compress_density.1 = (bf16[4,2,128,128]{3,2,1,0:T(8,128)(2,1)}, bf16[2,2,128,128]{3,2,1,0:T(8,128)(2,1)}) custom-call(s32[1,128]{1,0:T(1,128)} %skeleton_hbm.1, bf16[256,1024]{1,0:T(8,128)(2,1)} %bitcast.69, bf16[256,1024]{1,0:T(8,128)(2,1)} %bitcast.83, bf16[9,2,2,128,128]{4,3,2,1,0:T(8,128)(2,1)} %bitcast.59), custom_call_target="tpu_custom_call" | custom-call | flops 201326592 | bytes 1048576 | tf_op jit(solution)/shard_map/compress_density/pallas_call | solution.py:287
  2.6 0.0 copy-start
  2.6 4.4 %all-to-all-start = ((bf16[4,2,128,128]{3,2,1,0:T(8,128)(2,1)}), bf16[4,2,128,128]{3,2,1,0:T(8,128)(2,1)S(1)}, u32[]{:S(2)}, u32[]{:S(2)}) async-start(bf16[4,2,128,128]{3,2,1,0:T(8,128)(2,1)} %get-tuple-element.12), calls=%async_computation | async-start | bytes 524288 | tf_op jit(solution)/shard_map/all_to_all | solution.py:381
  7.0 5.4 %collective-permute-start = (bf16[2,2,128,128]{3,2,1,0:T(8,128)(2,1)}, bf16[2,2,128,128]{3,2,1,0:T(8,128)(2,1)S(1)}, u32[]{:S(2)}, u32[]{:S(2)}) collective-permute-start(bf16[2,2,128,128]{3,2,1,0:T(8,128)(2,1)} %get-tuple-element.13), channel_id=1, source_target_pairs={{0,2},{1,3},{2,0},{3,1},{4,6},{5,7},{6,4},{7,5},{8,10},{9,11},{10,... | collective-permute-start | bytes 393224 | tf_op jit(solution)/shard_map/ppermute | solution.py:254
  12.5 1.1 %fusion.14 = (bf16[1,1,2,128,128]{4,3,2,1,0:T(8,128)(2,1)S(1)}, bf16[1,1,2,128,128]{4,3,2,1,0:T(8,128)(2,1)S(1)}, bf16[1,1,2,128,128]{4,3,2,1,0:T(8,128)(2,1)S(1...) fusion(bf16[9,2,2,128,128]{4,3,2,1,0:T(8,128)(2,1)} %bitcast.60), kind=kLoop, calls=%fused_computation.35 | loop fusion | bytes 917504 | tf_op jit(solution)/shard_map/slice | solution.py:390
  13.6 3.0 %collective-permute-done.far_mix = bf16[2,2,128,128]{3,2,1,0:T(8,128)(2,1)S(1)} collective-permute-done((bf16[2,2,128,128]{3,2,1,0:T(8,128)(2,1)}, bf16[2,2,128,128]{3,2,1,0:T(8,128)(2,1)S(1)}, u32[]{:S(2)}, u32[]{:S(2)}) %collective-permute-start) | collective-permute-done | bytes 131104 | tf_op jit(solution)/shard_map/ppermute | solution.py:254
  16.5 0.0 all-to-all-done.gathered
  16.5 0.6 levels_0_1.1
  17.1 1.9 %collective-permute-start.1 = (bf16[2,128,128]{2,1,0:T(8,128)(2,1)S(1)}, bf16[2,128,128]{2,1,0:T(8,128)(2,1)S(1)}, u32[]{:S(2)}, u32[]{:S(2)}) collective-permute-start(bf16[2,128,128]{2,1,0:T(8,128)(2,1)S(1)} %levels_0_1.1), channel_id=1, source_target_pairs={{0,4},{4,0},{8,12},{12,8},{16,20},{20,16},{24,28},{28,24},{32,36},... | collective-permute-start | bytes 196616 | tf_op jit(solution)/shard_map/ppermute | solution.py:254
  19.1 0.0 copy-start.1
  19.1 0.0 copy-start.3
  19.1 0.2 fusion.15
  19.3 1.0 %collective-permute-done.1.other = bf16[2,128,128]{2,1,0:T(8,128)(2,1)S(1)} collective-permute-done((bf16[2,128,128]{2,1,0:T(8,128)(2,1)S(1)}, bf16[2,128,128]{2,1,0:T(8,128)(2,1)S(1)}, u32[]{:S(2)}, u32[]{:S(2)}) %collective-permute-start.1) | collective-permute-done | bytes 65568 | tf_op jit(solution)/shard_map/ppermute | solution.py:254
  20.3 0.2 level_state.6.after
  20.5 3.5 %collective-permute-start.2 = (bf16[2,128,128]{2,1,0:T(8,128)(2,1)S(1)}, bf16[2,128,128]{2,1,0:T(8,128)(2,1)S(1)}, u32[]{:S(2)}, u32[]{:S(2)}) collective-permute-start(bf16[2,128,128]{2,1,0:T(8,128)(2,1)S(1)} %level_state.6.after), channel_id=1, source_target_pairs={{0,8},{4,12},{8,0},{12,4},{16,24},{20,28},{24,16},{28,20},{32,40},... | collective-permute-start | bytes 196616 | tf_op jit(solution)/shard_map/ppermute | solution.py:254
  24.0 3.0 %collective-permute-start.5 = (bf16[272,256]{1,0:T(8,128)(2,1)S(1)}, bf16[272,256]{1,0:T(8,128)(2,1)S(1)}, u32[]{:S(2)}, u32[]{:S(2)}) collective-permute-start(bf16[272,256]{1,0:T(8,128)(2,1)S(1)} %get-tuple-element.14), channel_id=1, source_target_pairs={{0,1},{1,2},{2,3},{3,4},{4,5},{5,6},{6,7},{7,8},{8,9},{9,10},{10,1... | collective-permute-start | bytes 417800 | tf_op jit(solution)/shard_map/ppermute | solution.py:264
  27.0 0.2 fusion.16
  27.3 0.0 collective-permute-done.2.other
  27.3 0.2 level_state.7.after
  27.5 5.2 %collective-permute-start.3 = (bf16[2,128,128]{2,1,0:T(8,128)(2,1)S(1)}, bf16[2,128,128]{2,1,0:T(8,128)(2,1)S(1)}, u32[]{:S(2)}, u32[]{:S(2)}) collective-permute-start(bf16[2,128,128]{2,1,0:T(8,128)(2,1)S(1)} %level_state.7.after), channel_id=1, source_target_pairs={{0,16},{4,20},{8,24},{12,28},{16,0},{20,4},{24,8},{28,12},{32,48},... | collective-permute-start | bytes 196616 | tf_op jit(solution)/shard_map/ppermute | solution.py:254
  32.7 4.0 %collective-permute-start.6 = (bf16[272,256]{1,0:T(8,128)(2,1)S(1)}, bf16[272,256]{1,0:T(8,128)(2,1)S(1)}, u32[]{:S(2)}, u32[]{:S(2)}) collective-permute-start(bf16[272,256]{1,0:T(8,128)(2,1)S(1)} %head_strip.1), channel_id=1, source_target_pairs={{1,0},{2,1},{3,2},{4,3},{5,4},{6,5},{7,6},{8,7},{9,8},{10,9},{11,1... | collective-permute-start | bytes 417800 | tf_op jit(solution)/shard_map/ppermute | solution.py:264
  36.7 0.2 fusion.17
  37.0 0.0 copy-start.4
  37.0 0.0 copy-start.5
  37.0 0.2 level_state.8.after
  37.2 4.7 %collective-permute-start.4 = (bf16[2,128,128]{2,1,0:T(8,128)(2,1)S(1)}, bf16[2,128,128]{2,1,0:T(8,128)(2,1)S(1)}, u32[]{:S(2)}, u32[]{:S(2)}) collective-permute-start(bf16[2,128,128]{2,1,0:T(8,128)(2,1)S(1)} %level_state.8.after), channel_id=1, source_target_pairs={{0,32},{4,36},{8,40},{12,44},{16,48},{20,52},{24,56},{28,60},{32,0... | collective-permute-start | bytes 196616 | tf_op jit(solution)/shard_map/ppermute | solution.py:254
  41.9 0.2 fusion.18
  42.1 0.0 collective-permute-done.5.left
  42.2 0.6 prepare_near.1
  42.8 1.8 %near_boxes.4.rest_0_ = f32[2,128,256]{2,1,0:T(8,128)S(1)} custom-call(bf16[256,1024]{1,0:T(8,128)(2,1)S(1)} %bitcast.72, bf16[272,256]{1,0:T(8,128)(2,1)S(1)} %collective-permute-done.5.left, bf16[272,256]{1,0:T(8,128)(2,1)S(1)} %collective-permute-done.6.right, bf16[16,1536]{1,0:T(8,128)(2,1)S(1)} %get-tuple-element.16.source, ...), custom_call_target="tpu_custom_call" | custom-call | flops 402653184 | bytes 2097152 | tf_op jit(solution)/shard_map/near_boxes/pallas_call | solution.py:338
  44.6 4.4 %collective-permute-done.4.other = bf16[2,128,128]{2,1,0:T(8,128)(2,1)S(1)} collective-permute-done((bf16[2,128,128]{2,1,0:T(8,128)(2,1)S(1)}, bf16[2,128,128]{2,1,0:T(8,128)(2,1)S(1)}, u32[]{:S(2)}, u32[]{:S(2)}) %collective-permute-start.4) | collective-permute-done | bytes 65568 | tf_op jit(solution)/shard_map/ppermute | solution.py:254
  49.0 0.2 level_state.9.after
  49.2 2.5 %collective-permute-start.7 = (bf16[2,128,128]{2,1,0:T(8,128)(2,1)S(1)}, bf16[2,128,128]{2,1,0:T(8,128)(2,1)S(1)}, u32[]{:S(2)}, u32[]{:S(2)}) collective-permute-start(bf16[2,128,128]{2,1,0:T(8,128)(2,1)S(1)} %level_state.9.after), channel_id=1, source_target_pairs={{0,64},{4,68},{8,72},{12,76},{16,80},{20,84},{24,88},{28,92},{32,9... | collective-permute-start | bytes 196616 | tf_op jit(solution)/shard_map/ppermute | solution.py:254
  51.8 0.2 fusion.19
  52.0 1.8 %near_boxes.5.rest_0_.rest_1_ = f32[2,128,256]{2,1,0:T(8,128)S(1)} custom-call(bf16[256,1024]{1,0:T(8,128)(2,1)S(1)} %bitcast.73, bf16[272,256]{1,0:T(8,128)(2,1)S(1)} %collective-permute-done.5.left, bf16[272,256]{1,0:T(8,128)(2,1)S(1)} %collective-permute-done.6.right, bf16[16,1536]{1,0:T(8,128)(2,1)S(1)} %get-tuple-element.16.source, ...), custom_call_target="tpu_custom_call" | custom-call | flops 402653184 | bytes 2097152 | tf_op jit(solution)/shard_map/near_boxes/pallas_call | solution.py:338
  53.8 1.6 %collective-permute-done.7.other = bf16[2,128,128]{2,1,0:T(8,128)(2,1)S(1)} collective-permute-done((bf16[2,128,128]{2,1,0:T(8,128)(2,1)S(1)}, bf16[2,128,128]{2,1,0:T(8,128)(2,1)S(1)}, u32[]{:S(2)}, u32[]{:S(2)}) %collective-permute-start.7) | collective-permute-done | bytes 65568 | tf_op jit(solution)/shard_map/ppermute | solution.py:254
  55.4 0.2 level_state.10.after
  55.6 4.7 %collective-permute-start.8 = (bf16[2,128,128]{2,1,0:T(8,128)(2,1)S(1)}, bf16[2,128,128]{2,1,0:T(8,128)(2,1)S(1)}, u32[]{:S(2)}, u32[]{:S(2)}) collective-permute-start(bf16[2,128,128]{2,1,0:T(8,128)(2,1)S(1)} %level_state.10.after), channel_id=1, source_target_pairs={{0,128},{4,132},{8,136},{12,140},{16,144},{20,148},{24,152},{28,15... | collective-permute-start | bytes 196616 | tf_op jit(solution)/shard_map/ppermute | solution.py:254
  60.3 0.2 fusion.20
  60.5 1.8 %near_boxes.6.rest_0_.rest_2_ = f32[2,128,256]{2,1,0:T(8,128)S(1)} custom-call(bf16[256,1024]{1,0:T(8,128)(2,1)S(1)} %bitcast.74, bf16[272,256]{1,0:T(8,128)(2,1)S(1)} %collective-permute-done.5.left, bf16[272,256]{1,0:T(8,128)(2,1)S(1)} %collective-permute-done.6.right, bf16[16,1536]{1,0:T(8,128)(2,1)S(1)} %get-tuple-element.16.source, ...), custom_call_target="tpu_custom_call" | custom-call | flops 402653184 | bytes 2097152 | tf_op jit(solution)/shard_map/near_boxes/pallas_call | solution.py:338
  62.3 0.3 collective-permute-done.8.other
  62.6 0.2 level_state.11.after
  62.8 10.0 %collective-permute-start.9 = (bf16[2,128,128]{2,1,0:T(8,128)(2,1)S(1)}, bf16[2,128,128]{2,1,0:T(8,128)(2,1)S(1)}, u32[]{:S(2)}, u32[]{:S(2)}) collective-permute-start(bf16[2,128,128]{2,1,0:T(8,128)(2,1)S(1)} %level_state.11.after), channel_id=1, source_target_pairs={{0,256},{4,260},{8,264},{12,268},{16,272},{20,276},{24,280},{28,28... | collective-permute-start | bytes 196616 | tf_op jit(solution)/shard_map/ppermute | solution.py:254
  72.8 0.0 copy-start.2
  72.8 0.2 fusion.21
  73.0 1.8 %near_boxes.7.rest_3_ = f32[2,128,256]{2,1,0:T(8,128)S(1)} custom-call(bf16[256,1024]{1,0:T(8,128)(2,1)S(1)} %bitcast.75, bf16[272,256]{1,0:T(8,128)(2,1)S(1)} %collective-permute-done.5.left, bf16[272,256]{1,0:T(8,128)(2,1)S(1)} %collective-permute-done.6.right, bf16[16,1536]{1,0:T(8,128)(2,1)S(1)} %get-tuple-element.16.source, ...), custom_call_target="tpu_custom_call" | custom-call | flops 402653184 | bytes 2097152 | tf_op jit(solution)/shard_map/near_boxes/pallas_call | solution.py:338
  74.8 0.2 collective-permute-done.9.other
  75.0 1.4 %expand_state.1 = bf16[2,128,1024]{2,1,0:T(8,128)(2,1)} custom-call(f32[2,128,128]{2,1,0:T(8,128)S(1)} %pad_maximum_fusion.6.own, bf16[2,128,128]{2,1,0:T(8,128)(2,1)S(1)} %collective-permute-done.9.other, bf16[9,2,2,128,128]{4,3,2,1,0:T(8,128)(2,1)S(1)} %bitcast.68, bf16[2,128,1024]{2,1,0:T(8,128)(2,1)S(1)} %copy-done.2, ...), custom_call_target="tpu_custom_call" | custom-call | flops 134217728 | bytes 2097152 | tf_op jit(solution)/shard_map/expand_state/pallas_call | solution.py:412
  (27 shorter events, 0.3 us)
Async XLA Ops:
  0.0 12.5 %copy-start.6 = (bf16[1024]{0:T(1024)(128)(2,1)S(1)}, bf16[1024]{0:T(1024)(128)(2,1)}, u32[]{:S(2)}) copy-start(bf16[1024]{0:T(1024)(128)(2,1)} %param.11) | copy-start | bytes 6148
  2.6 13.9 %copy-start = (bf16[1,9,2,2,128,128]{5,4,3,2,1,0:T(8,128)(2,1)S(1)}, bf16[1,9,2,2,128,128]{5,4,3,2,1,0:T(8,128)(2,1)}, u32[]{:S(2)}) copy-start(bf16[1,9,2,2,128,128]{5,4,3,2,1,0:T(8,128)(2,1)} %param.16) | copy-start | bytes 3538948
  2.6 13.9 %all-to-all-start = ((bf16[4,2,128,128]{3,2,1,0:T(8,128)(2,1)}), bf16[4,2,128,128]{3,2,1,0:T(8,128)(2,1)S(1)}, u32[]{:S(2)}, u32[]{:S(2)}) async-start(bf16[4,2,128,128]{3,2,1,0:T(8,128)(2,1)} %get-tuple-element.12), calls=%async_computation | async-start | bytes 524288 | tf_op jit(solution)/shard_map/all_to_all | solution.py:381
  7.0 9.5 %collective-permute-start = (bf16[2,2,128,128]{3,2,1,0:T(8,128)(2,1)}, bf16[2,2,128,128]{3,2,1,0:T(8,128)(2,1)S(1)}, u32[]{:S(2)}, u32[]{:S(2)}) collective-permute-start(bf16[2,2,128,128]{3,2,1,0:T(8,128)(2,1)} %get-tuple-element.13), channel_id=1, source_target_pairs={{0,2},{1,3},{2,0},{3,1},{4,6},{5,7},{6,4},{7,5},{8,10},{9,11},{10,... | collective-permute-start | bytes 393224 | tf_op jit(solution)/shard_map/ppermute | solution.py:254
  17.1 3.1 %collective-permute-start.1 = (bf16[2,128,128]{2,1,0:T(8,128)(2,1)S(1)}, bf16[2,128,128]{2,1,0:T(8,128)(2,1)S(1)}, u32[]{:S(2)}, u32[]{:S(2)}) collective-permute-start(bf16[2,128,128]{2,1,0:T(8,128)(2,1)S(1)} %levels_0_1.1), channel_id=1, source_target_pairs={{0,4},{4,0},{8,12},{12,8},{16,20},{20,16},{24,28},{28,24},{32,36},... | collective-permute-start | bytes 196616 | tf_op jit(solution)/shard_map/ppermute | solution.py:254
  19.1 4.9 %copy-start.1 = (bf16[2,128,1024]{2,1,0:T(8,128)(2,1)S(1)}, bf16[2,128,1024]{2,1,0:T(8,128)(2,1)}, u32[]{:S(2)}) copy-start(bf16[2,128,1024]{2,1,0:T(8,128)(2,1)} %param.9) | copy-start | bytes 1572868
  19.1 4.9 %copy-start.3 = (bf16[3,1024]{1,0:T(4,128)(2,1)S(1)}, bf16[3,1024]{1,0:T(4,128)(2,1)}, u32[]{:S(2)}) copy-start(bf16[3,1024]{1,0:T(4,128)(2,1)} %coords.1) | copy-start | bytes 18436
  20.5 6.8 %collective-permute-start.2 = (bf16[2,128,128]{2,1,0:T(8,128)(2,1)S(1)}, bf16[2,128,128]{2,1,0:T(8,128)(2,1)S(1)}, u32[]{:S(2)}, u32[]{:S(2)}) collective-permute-start(bf16[2,128,128]{2,1,0:T(8,128)(2,1)S(1)} %level_state.6.after), channel_id=1, source_target_pairs={{0,8},{4,12},{8,0},{12,4},{16,24},{20,28},{24,16},{28,20},{32,40},... | collective-permute-start | bytes 196616 | tf_op jit(solution)/shard_map/ppermute | solution.py:254
  24.0 18.1 %collective-permute-start.5 = (bf16[272,256]{1,0:T(8,128)(2,1)S(1)}, bf16[272,256]{1,0:T(8,128)(2,1)S(1)}, u32[]{:S(2)}, u32[]{:S(2)}) collective-permute-start(bf16[272,256]{1,0:T(8,128)(2,1)S(1)} %get-tuple-element.14), channel_id=1, source_target_pairs={{0,1},{1,2},{2,3},{3,4},{4,5},{5,6},{6,7},{7,8},{8,9},{9,10},{10,1... | collective-permute-start | bytes 417800 | tf_op jit(solution)/shard_map/ppermute | solution.py:264
  27.5 9.5 %collective-permute-start.3 = (bf16[2,128,128]{2,1,0:T(8,128)(2,1)S(1)}, bf16[2,128,128]{2,1,0:T(8,128)(2,1)S(1)}, u32[]{:S(2)}, u32[]{:S(2)}) collective-permute-start(bf16[2,128,128]{2,1,0:T(8,128)(2,1)S(1)} %level_state.7.after), channel_id=1, source_target_pairs={{0,16},{4,20},{8,24},{12,28},{16,0},{20,4},{24,8},{28,12},{32,48},... | collective-permute-start | bytes 196616 | tf_op jit(solution)/shard_map/ppermute | solution.py:254
  32.7 9.5 %collective-permute-start.6 = (bf16[272,256]{1,0:T(8,128)(2,1)S(1)}, bf16[272,256]{1,0:T(8,128)(2,1)S(1)}, u32[]{:S(2)}, u32[]{:S(2)}) collective-permute-start(bf16[272,256]{1,0:T(8,128)(2,1)S(1)} %head_strip.1), channel_id=1, source_target_pairs={{1,0},{2,1},{3,2},{4,3},{5,4},{6,5},{7,6},{8,7},{9,8},{10,9},{11,1... | collective-permute-start | bytes 417800 | tf_op jit(solution)/shard_map/ppermute | solution.py:264
  37.0 5.2 %copy-start.4 = (s32[8,27]{1,0:T(8,128)S(1)}, s32[8,27]{1,0:T(8,128)}, u32[]{:S(2)}) copy-start(s32[8,27]{1,0:T(8,128)} %neighbors.1) | copy-start | bytes 2596
  37.0 5.2 %copy-start.5 = (s32[8]{0:T(128)S(1)}, s32[8]{0:T(128)}, u32[]{:S(2)}) copy-start(s32[8]{0:T(128)} %counts.1) | copy-start | bytes 100
  37.2 11.8 %collective-permute-start.4 = (bf16[2,128,128]{2,1,0:T(8,128)(2,1)S(1)}, bf16[2,128,128]{2,1,0:T(8,128)(2,1)S(1)}, u32[]{:S(2)}, u32[]{:S(2)}) collective-permute-start(bf16[2,128,128]{2,1,0:T(8,128)(2,1)S(1)} %level_state.8.after), channel_id=1, source_target_pairs={{0,32},{4,36},{8,40},{12,44},{16,48},{20,52},{24,56},{28,60},{32,0... | collective-permute-start | bytes 196616 | tf_op jit(solution)/shard_map/ppermute | solution.py:254
  49.2 6.2 %collective-permute-start.7 = (bf16[2,128,128]{2,1,0:T(8,128)(2,1)S(1)}, bf16[2,128,128]{2,1,0:T(8,128)(2,1)S(1)}, u32[]{:S(2)}, u32[]{:S(2)}) collective-permute-start(bf16[2,128,128]{2,1,0:T(8,128)(2,1)S(1)} %level_state.9.after), channel_id=1, source_target_pairs={{0,64},{4,68},{8,72},{12,76},{16,80},{20,84},{24,88},{28,92},{32,9... | collective-permute-start | bytes 196616 | tf_op jit(solution)/shard_map/ppermute | solution.py:254
  55.6 7.1 %collective-permute-start.8 = (bf16[2,128,128]{2,1,0:T(8,128)(2,1)S(1)}, bf16[2,128,128]{2,1,0:T(8,128)(2,1)S(1)}, u32[]{:S(2)}, u32[]{:S(2)}) collective-permute-start(bf16[2,128,128]{2,1,0:T(8,128)(2,1)S(1)} %level_state.10.after), channel_id=1, source_target_pairs={{0,128},{4,132},{8,136},{12,140},{16,144},{20,148},{24,152},{28,15... | collective-permute-start | bytes 196616 | tf_op jit(solution)/shard_map/ppermute | solution.py:254
  62.8 12.2 %collective-permute-start.9 = (bf16[2,128,128]{2,1,0:T(8,128)(2,1)S(1)}, bf16[2,128,128]{2,1,0:T(8,128)(2,1)S(1)}, u32[]{:S(2)}, u32[]{:S(2)}) collective-permute-start(bf16[2,128,128]{2,1,0:T(8,128)(2,1)S(1)} %level_state.11.after), channel_id=1, source_target_pairs={{0,256},{4,260},{8,264},{12,268},{16,272},{20,276},{24,280},{28,28... | collective-permute-start | bytes 196616 | tf_op jit(solution)/shard_map/ppermute | solution.py:254
  72.8 2.2 %copy-start.2 = (bf16[2,128,1024]{2,1,0:T(8,128)(2,1)S(1)}, bf16[2,128,1024]{2,1,0:T(8,128)(2,1)}, u32[]{:S(2)}) copy-start(bf16[2,128,1024]{2,1,0:T(8,128)(2,1)} %expand.1) | copy-start | bytes 1572868

commit v5 on v4

--- a/solution.py
+++ b/solution.py
@@ -21,9 +21,9 @@
 NN = (((1,), (0,)), ((), ()))
 TN = (((0,), (0,)), ((), ()))
 
-NEAR_PLAN = {5: 2, 6: 2, 7: 2}
+NEAR_PLAN = {6: 2, 7: 3}
 FIRST_HALO = 3
-SECOND_HALO = 4
+SECOND_HALO = 5
 
 VMEM_LIMIT = 16 * 1024 * 1024
 WHOLE_VMEM = 63 * 1024 * 1024

time: 76.9 us -> 77.5 us (level)
  the two profiles are of different devices: /device:TPU:16 before, /device:TPU:6 now
where the time goes in v5:
time: 77.5 us; the launch traced here: 77 us
  starting transfers between devices  42.3 us (55%)
  waiting for transfers between devices  18 us (23%)
  Pallas kernels  13.6 us (18%)
  matrix products  1.28 us (2%)
  local copies, waits for them, and re-layouts  1.11 us (1%)
    ppermute x8, starting transfers between devices, exchange(): return lax.ppermute(value, axis, pairs)  29.1 us
    ppermute x8, waiting for transfers between devices, exchange(): return lax.ppermute(value, axis, pairs)  17.4 us
    all_to_all x1, starting transfers between devices, per_device(): gathered = lax.all_to_all(copies, 'sub', 0, 0)  9.37 us
    pallas_call x10, Pallas kernels, kernel(): pl.pallas_call(body, out_shape=out_shape, in_specs=[in_vmem()] * len(oper...  9.01 us
    ppermute x2, starting transfers between devices, shift(): return lax.ppermute(value, axes, pairs)  3.84 us
    pallas_call x1, Pallas kernels, per_device(): pl.pallas_call(head_kernel, out_shape=(jax.ShapeDtypeStruct((4, 2, column...  2.58 us
  transfers between devices with their start and end apart: 11, of which 7 were waited for; matrix products, arithmetic and copies ran while one was open for 3% of the time, Pallas kernels for 11%

profile of v5, /device:TPU:6, one launch (start us, length us, event | category | flops | bytes accessed | tf_op | source)
XLA Modules:
  0.0 77.0 jit_solution(9839784028876501061)
XLA Ops:
  0.0 2.6 %compress_density.1 = (bf16[4,2,128,128]{3,2,1,0:T(8,128)(2,1)}, bf16[2,2,128,128]{3,2,1,0:T(8,128)(2,1)}) custom-call(s32[1,128]{1,0:T(1,128)} %skeleton_hbm.1, bf16[256,1024]{1,0:T(8,128)(2,1)} %bitcast.69, bf16[256,1024]{1,0:T(8,128)(2,1)} %bitcast.82, bf16[9,2,2,128,128]{4,3,2,1,0:T(8,128)(2,1)} %bitcast.59), custom_call_target="tpu_custom_call" | custom-call | flops 201326592 | bytes 1048576 | tf_op jit(solution)/shard_map/compress_density/pallas_call | solution.py:287
  2.6 0.0 copy-start
  2.6 9.4 %all-to-all-start = ((bf16[4,2,128,128]{3,2,1,0:T(8,128)(2,1)}), bf16[4,2,128,128]{3,2,1,0:T(8,128)(2,1)S(1)}, u32[]{:S(2)}, u32[]{:S(2)}) async-start(bf16[4,2,128,128]{3,2,1,0:T(8,128)(2,1)} %get-tuple-element.12), calls=%async_computation | async-start | bytes 524288 | tf_op jit(solution)/shard_map/all_to_all | solution.py:381
  12.0 3.4 %collective-permute-start = (bf16[2,2,128,128]{3,2,1,0:T(8,128)(2,1)}, bf16[2,2,128,128]{3,2,1,0:T(8,128)(2,1)S(1)}, u32[]{:S(2)}, u32[]{:S(2)}) collective-permute-start(bf16[2,2,128,128]{3,2,1,0:T(8,128)(2,1)} %get-tuple-element.13), channel_id=1, source_target_pairs={{0,2},{1,3},{2,0},{3,1},{4,6},{5,7},{6,4},{7,5},{8,10},{9,11},{10,... | collective-permute-start | bytes 393224 | tf_op jit(solution)/shard_map/ppermute | solution.py:254
  15.4 1.1 %fusion.14 = (bf16[1,1,2,128,128]{4,3,2,1,0:T(8,128)(2,1)S(1)}, bf16[1,1,2,128,128]{4,3,2,1,0:T(8,128)(2,1)S(1)}, bf16[1,1,2,128,128]{4,3,2,1,0:T(8,128)(2,1)S(1...) fusion(bf16[9,2,2,128,128]{4,3,2,1,0:T(8,128)(2,1)} %bitcast.60), kind=kLoop, calls=%fused_computation.35 | loop fusion | bytes 917504 | tf_op jit(solution)/shard_map/slice | solution.py:390
  16.4 4.1 %collective-permute-done.far_mix = bf16[2,2,128,128]{3,2,1,0:T(8,128)(2,1)S(1)} collective-permute-done((bf16[2,2,128,128]{3,2,1,0:T(8,128)(2,1)}, bf16[2,2,128,128]{3,2,1,0:T(8,128)(2,1)S(1)}, u32[]{:S(2)}, u32[]{:S(2)}) %collective-permute-start) | collective-permute-done | bytes 131104 | tf_op jit(solution)/shard_map/ppermute | solution.py:254
  20.5 0.0 all-to-all-done.gathered
  20.5 0.6 levels_0_1.1
  21.1 1.9 %collective-permute-start.1 = (bf16[2,128,128]{2,1,0:T(8,128)(2,1)S(1)}, bf16[2,128,128]{2,1,0:T(8,128)(2,1)S(1)}, u32[]{:S(2)}, u32[]{:S(2)}) collective-permute-start(bf16[2,128,128]{2,1,0:T(8,128)(2,1)S(1)} %levels_0_1.1), channel_id=1, source_target_pairs={{0,4},{4,0},{8,12},{12,8},{16,20},{20,16},{24,28},{28,24},{32,36},... | collective-permute-start | bytes 196616 | tf_op jit(solution)/shard_map/ppermute | solution.py:254
  23.1 0.0 copy-start.1
  23.1 0.0 copy-start.3
  23.1 0.2 fusion.15
  23.3 1.0 %collective-permute-done.1.other = bf16[2,128,128]{2,1,0:T(8,128)(2,1)S(1)} collective-permute-done((bf16[2,128,128]{2,1,0:T(8,128)(2,1)S(1)}, bf16[2,128,128]{2,1,0:T(8,128)(2,1)S(1)}, u32[]{:S(2)}, u32[]{:S(2)}) %collective-permute-start.1) | collective-permute-done | bytes 65568 | tf_op jit(solution)/shard_map/ppermute | solution.py:254
  24.3 0.2 level_state.6.after
  24.5 1.9 %collective-permute-start.2 = (bf16[2,128,128]{2,1,0:T(8,128)(2,1)S(1)}, bf16[2,128,128]{2,1,0:T(8,128)(2,1)S(1)}, u32[]{:S(2)}, u32[]{:S(2)}) collective-permute-start(bf16[2,128,128]{2,1,0:T(8,128)(2,1)S(1)} %level_state.6.after), channel_id=1, source_target_pairs={{0,8},{4,12},{8,0},{12,4},{16,24},{20,28},{24,16},{28,20},{32,40},... | collective-permute-start | bytes 196616 | tf_op jit(solution)/shard_map/ppermute | solution.py:254
  26.5 1.9 %collective-permute-start.6 = (bf16[272,256]{1,0:T(8,128)(2,1)S(1)}, bf16[272,256]{1,0:T(8,128)(2,1)S(1)}, u32[]{:S(2)}, u32[]{:S(2)}) collective-permute-start(bf16[272,256]{1,0:T(8,128)(2,1)S(1)} %get-tuple-element.14), channel_id=1, source_target_pairs={{0,1},{1,2},{2,3},{3,4},{4,5},{5,6},{6,7},{7,8},{8,9},{9,10},{10,1... | collective-permute-start | bytes 417800 | tf_op jit(solution)/shard_map/ppermute | solution.py:264
  28.4 0.2 fusion.16
  28.6 2.0 %collective-permute-done.2.other = bf16[2,128,128]{2,1,0:T(8,128)(2,1)S(1)} collective-permute-done((bf16[2,128,128]{2,1,0:T(8,128)(2,1)S(1)}, bf16[2,128,128]{2,1,0:T(8,128)(2,1)S(1)}, u32[]{:S(2)}, u32[]{:S(2)}) %collective-permute-start.2) | collective-permute-done | bytes 65568 | tf_op jit(solution)/shard_map/ppermute | solution.py:254
  30.6 0.2 level_state.7
  30.8 1.9 %collective-permute-start.3 = (bf16[2,128,128]{2,1,0:T(8,128)(2,1)S(1)}, bf16[2,128,128]{2,1,0:T(8,128)(2,1)S(1)}, u32[]{:S(2)}, u32[]{:S(2)}) collective-permute-start(bf16[2,128,128]{2,1,0:T(8,128)(2,1)S(1)} %level_state.7), channel_id=1, source_target_pairs={{0,16},{4,20},{8,24},{12,28},{16,0},{20,4},{24,8},{28,12},{32,48},... | collective-permute-start | bytes 196616 | tf_op jit(solution)/shard_map/ppermute | solution.py:254
  32.8 0.2 fusion.17
  33.0 5.3 %collective-permute-done.3.other = bf16[2,128,128]{2,1,0:T(8,128)(2,1)S(1)} collective-permute-done((bf16[2,128,128]{2,1,0:T(8,128)(2,1)S(1)}, bf16[2,128,128]{2,1,0:T(8,128)(2,1)S(1)}, u32[]{:S(2)}, u32[]{:S(2)}) %collective-permute-start.3) | collective-permute-done | bytes 65568 | tf_op jit(solution)/shard_map/ppermute | solution.py:254
  38.4 0.2 level_state.8.after
  38.5 3.9 %collective-permute-start.4 = (bf16[2,128,128]{2,1,0:T(8,128)(2,1)S(1)}, bf16[2,128,128]{2,1,0:T(8,128)(2,1)S(1)}, u32[]{:S(2)}, u32[]{:S(2)}) collective-permute-start(bf16[2,128,128]{2,1,0:T(8,128)(2,1)S(1)} %level_state.8.after), channel_id=1, source_target_pairs={{0,32},{4,36},{8,40},{12,44},{16,48},{20,52},{24,56},{28,60},{32,0... | collective-permute-start | bytes 196616 | tf_op jit(solution)/shard_map/ppermute | solution.py:254
  42.5 1.9 %collective-permute-start.7 = (bf16[272,256]{1,0:T(8,128)(2,1)S(1)}, bf16[272,256]{1,0:T(8,128)(2,1)S(1)}, u32[]{:S(2)}, u32[]{:S(2)}) collective-permute-start(bf16[272,256]{1,0:T(8,128)(2,1)S(1)} %head_strip.1), channel_id=1, source_target_pairs={{1,0},{2,1},{3,2},{4,3},{5,4},{6,5},{7,6},{8,7},{9,8},{10,9},{11,1... | collective-permute-start | bytes 417800 | tf_op jit(solution)/shard_map/ppermute | solution.py:264
  44.4 0.2 fusion.18
  44.6 0.0 copy-start.4
  44.6 0.0 copy-start.5
  44.6 4.0 %collective-permute-done.4.other = bf16[2,128,128]{2,1,0:T(8,128)(2,1)S(1)} collective-permute-done((bf16[2,128,128]{2,1,0:T(8,128)(2,1)S(1)}, bf16[2,128,128]{2,1,0:T(8,128)(2,1)S(1)}, u32[]{:S(2)}, u32[]{:S(2)}) %collective-permute-start.4) | collective-permute-done | bytes 65568 | tf_op jit(solution)/shard_map/ppermute | solution.py:254
  48.6 0.2 level_state.9.after
  48.8 1.9 %collective-permute-start.5 = (bf16[2,128,128]{2,1,0:T(8,128)(2,1)S(1)}, bf16[2,128,128]{2,1,0:T(8,128)(2,1)S(1)}, u32[]{:S(2)}, u32[]{:S(2)}) collective-permute-start(bf16[2,128,128]{2,1,0:T(8,128)(2,1)S(1)} %level_state.9.after), channel_id=1, source_target_pairs={{0,64},{4,68},{8,72},{12,76},{16,80},{20,84},{24,88},{28,92},{32,9... | collective-permute-start | bytes 196616 | tf_op jit(solution)/shard_map/ppermute | solution.py:254
  50.7 0.2 fusion.19
  51.0 0.5 collective-permute-done.7.right
  51.5 0.6 prepare_near.1
  52.2 1.8 %near_boxes.3.rest_0_ = f32[2,128,256]{2,1,0:T(8,128)S(1)} custom-call(bf16[256,1024]{1,0:T(8,128)(2,1)S(1)} %bitcast.72, bf16[272,256]{1,0:T(8,128)(2,1)S(1)} %collective-permute-done.6.left, bf16[272,256]{1,0:T(8,128)(2,1)S(1)} %collective-permute-done.7.right, bf16[16,1536]{1,0:T(8,128)(2,1)S(1)} %get-tuple-element.16.source, ...), custom_call_target="tpu_custom_call" | custom-call | flops 402653184 | bytes 2097152 | tf_op jit(solution)/shard_map/near_boxes/pallas_call | solution.py:338
  54.0 1.0 %collective-permute-done.5.other = bf16[2,128,128]{2,1,0:T(8,128)(2,1)S(1)} collective-permute-done((bf16[2,128,128]{2,1,0:T(8,128)(2,1)S(1)}, bf16[2,128,128]{2,1,0:T(8,128)(2,1)S(1)}, u32[]{:S(2)}, u32[]{:S(2)}) %collective-permute-start.5) | collective-permute-done | bytes 65568 | tf_op jit(solution)/shard_map/ppermute | solution.py:254
  55.0 0.2 level_state.10.after
  55.2 5.1 %collective-permute-start.8 = (bf16[2,128,128]{2,1,0:T(8,128)(2,1)S(1)}, bf16[2,128,128]{2,1,0:T(8,128)(2,1)S(1)}, u32[]{:S(2)}, u32[]{:S(2)}) collective-permute-start(bf16[2,128,128]{2,1,0:T(8,128)(2,1)S(1)} %level_state.10.after), channel_id=1, source_target_pairs={{0,128},{4,132},{8,136},{12,140},{16,144},{20,148},{24,152},{28,15... | collective-permute-start | bytes 196616 | tf_op jit(solution)/shard_map/ppermute | solution.py:254
  60.3 0.2 fusion.20
  60.5 2.7 %near_boxes.4.rest_0_.rest_1_ = f32[2,128,384]{2,1,0:T(8,128)S(1)} custom-call(bf16[256,1024]{1,0:T(8,128)(2,1)S(1)} %bitcast.73, bf16[272,256]{1,0:T(8,128)(2,1)S(1)} %collective-permute-done.6.left, bf16[272,256]{1,0:T(8,128)(2,1)S(1)} %collective-permute-done.7.right, bf16[16,1536]{1,0:T(8,128)(2,1)S(1)} %get-tuple-element.16.source, ...), custom_call_target="tpu_custom_call" | custom-call | flops 603979776 | bytes 2097152 | tf_op jit(solution)/shard_map/near_boxes/pallas_call | solution.py:338
  63.3 0.0 collective-permute-done.8.other
  63.3 0.2 level_state.11.after
  63.5 9.1 %collective-permute-start.9 = (bf16[2,128,128]{2,1,0:T(8,128)(2,1)S(1)}, bf16[2,128,128]{2,1,0:T(8,128)(2,1)S(1)}, u32[]{:S(2)}, u32[]{:S(2)}) collective-permute-start(bf16[2,128,128]{2,1,0:T(8,128)(2,1)S(1)} %level_state.11.after), channel_id=1, source_target_pairs={{0,256},{4,260},{8,264},{12,268},{16,272},{20,276},{24,280},{28,28... | collective-permute-start | bytes 196616 | tf_op jit(solution)/shard_map/ppermute | solution.py:254
  72.6 0.2 fusion.21
  72.8 0.0 copy-start.2
  72.9 2.7 %near_boxes.5.rest_2_ = f32[2,128,384]{2,1,0:T(8,128)S(1)} custom-call(bf16[256,1024]{1,0:T(8,128)(2,1)S(1)} %bitcast.74, bf16[272,256]{1,0:T(8,128)(2,1)S(1)} %collective-permute-done.6.left, bf16[272,256]{1,0:T(8,128)(2,1)S(1)} %collective-permute-done.7.right, bf16[16,1536]{1,0:T(8,128)(2,1)S(1)} %get-tuple-element.16.source, ...), custom_call_target="tpu_custom_call" | custom-call | flops 603979776 | bytes 2097152 | tf_op jit(solution)/shard_map/near_boxes/pallas_call | solution.py:338
  75.6 0.0 collective-permute-done.9.other
  75.6 1.4 %expand_state.1 = bf16[2,128,1024]{2,1,0:T(8,128)(2,1)} custom-call(f32[2,128,128]{2,1,0:T(8,128)S(1)} %pad_maximum_fusion.6.own, bf16[2,128,128]{2,1,0:T(8,128)(2,1)S(1)} %collective-permute-done.9.other, bf16[9,2,2,128,128]{4,3,2,1,0:T(8,128)(2,1)S(1)} %bitcast.68, bf16[2,128,1024]{2,1,0:T(8,128)(2,1)S(1)} %copy-done.2, ...), custom_call_target="tpu_custom_call" | custom-call | flops 134217728 | bytes 2097152 | tf_op jit(solution)/shard_map/expand_state/pallas_call | solution.py:412
  (26 shorter events, 0.3 us)
Async XLA Ops:
  0.0 15.3 %copy-start.6 = (bf16[1024]{0:T(1024)(128)(2,1)S(1)}, bf16[1024]{0:T(1024)(128)(2,1)}, u32[]{:S(2)}) copy-start(bf16[1024]{0:T(1024)(128)(2,1)} %param.11) | copy-start | bytes 6148
  2.6 18.0 %copy-start = (bf16[1,9,2,2,128,128]{5,4,3,2,1,0:T(8,128)(2,1)S(1)}, bf16[1,9,2,2,128,128]{5,4,3,2,1,0:T(8,128)(2,1)}, u32[]{:S(2)}) copy-start(bf16[1,9,2,2,128,128]{5,4,3,2,1,0:T(8,128)(2,1)} %param.16) | copy-start | bytes 3538948
  2.6 17.9 %all-to-all-start = ((bf16[4,2,128,128]{3,2,1,0:T(8,128)(2,1)}), bf16[4,2,128,128]{3,2,1,0:T(8,128)(2,1)S(1)}, u32[]{:S(2)}, u32[]{:S(2)}) async-start(bf16[4,2,128,128]{3,2,1,0:T(8,128)(2,1)} %get-tuple-element.12), calls=%async_computation | async-start | bytes 524288 | tf_op jit(solution)/shard_map/all_to_all | solution.py:381
  12.0 8.6 %collective-permute-start = (bf16[2,2,128,128]{3,2,1,0:T(8,128)(2,1)}, bf16[2,2,128,128]{3,2,1,0:T(8,128)(2,1)S(1)}, u32[]{:S(2)}, u32[]{:S(2)}) collective-permute-start(bf16[2,2,128,128]{3,2,1,0:T(8,128)(2,1)} %get-tuple-element.13), channel_id=1, source_target_pairs={{0,2},{1,3},{2,0},{3,1},{4,6},{5,7},{6,4},{7,5},{8,10},{9,11},{10,... | collective-permute-start | bytes 393224 | tf_op jit(solution)/shard_map/ppermute | solution.py:254
  21.1 3.1 %collective-permute-start.1 = (bf16[2,128,128]{2,1,0:T(8,128)(2,1)S(1)}, bf16[2,128,128]{2,1,0:T(8,128)(2,1)S(1)}, u32[]{:S(2)}, u32[]{:S(2)}) collective-permute-start(bf16[2,128,128]{2,1,0:T(8,128)(2,1)S(1)} %levels_0_1.1), channel_id=1, source_target_pairs={{0,4},{4,0},{8,12},{12,8},{16,20},{20,16},{24,28},{28,24},{32,36},... | collective-permute-start | bytes 196616 | tf_op jit(solution)/shard_map/ppermute | solution.py:254
  23.1 3.3 %copy-start.1 = (bf16[2,128,1024]{2,1,0:T(8,128)(2,1)S(1)}, bf16[2,128,1024]{2,1,0:T(8,128)(2,1)}, u32[]{:S(2)}) copy-start(bf16[2,128,1024]{2,1,0:T(8,128)(2,1)} %param.9) | copy-start | bytes 1572868
  23.1 3.3 %copy-start.3 = (bf16[3,1024]{1,0:T(4,128)(2,1)S(1)}, bf16[3,1024]{1,0:T(4,128)(2,1)}, u32[]{:S(2)}) copy-start(bf16[3,1024]{1,0:T(4,128)(2,1)} %coords.1) | copy-start | bytes 18436
  24.5 6.2 %collective-permute-start.2 = (bf16[2,128,128]{2,1,0:T(8,128)(2,1)S(1)}, bf16[2,128,128]{2,1,0:T(8,128)(2,1)S(1)}, u32[]{:S(2)}, u32[]{:S(2)}) collective-permute-start(bf16[2,128,128]{2,1,0:T(8,128)(2,1)S(1)} %level_state.6.after), channel_id=1, source_target_pairs={{0,8},{4,12},{8,0},{12,4},{16,24},{20,28},{24,16},{28,20},{32,40},... | collective-permute-start | bytes 196616 | tf_op jit(solution)/shard_map/ppermute | solution.py:254
  26.5 24.5 %collective-permute-start.6 = (bf16[272,256]{1,0:T(8,128)(2,1)S(1)}, bf16[272,256]{1,0:T(8,128)(2,1)S(1)}, u32[]{:S(2)}, u32[]{:S(2)}) collective-permute-start(bf16[272,256]{1,0:T(8,128)(2,1)S(1)} %get-tuple-element.14), channel_id=1, source_target_pairs={{0,1},{1,2},{2,3},{3,4},{4,5},{5,6},{6,7},{7,8},{8,9},{9,10},{10,1... | collective-permute-start | bytes 417800 | tf_op jit(solution)/shard_map/ppermute | solution.py:264
  30.8 7.5 %collective-permute-start.3 = (bf16[2,128,128]{2,1,0:T(8,128)(2,1)S(1)}, bf16[2,128,128]{2,1,0:T(8,128)(2,1)S(1)}, u32[]{:S(2)}, u32[]{:S(2)}) collective-permute-start(bf16[2,128,128]{2,1,0:T(8,128)(2,1)S(1)} %level_state.7), channel_id=1, source_target_pairs={{0,16},{4,20},{8,24},{12,28},{16,0},{20,4},{24,8},{28,12},{32,48},... | collective-permute-start | bytes 196616 | tf_op jit(solution)/shard_map/ppermute | solution.py:254
  38.5 10.1 %collective-permute-start.4 = (bf16[2,128,128]{2,1,0:T(8,128)(2,1)S(1)}, bf16[2,128,128]{2,1,0:T(8,128)(2,1)S(1)}, u32[]{:S(2)}, u32[]{:S(2)}) collective-permute-start(bf16[2,128,128]{2,1,0:T(8,128)(2,1)S(1)} %level_state.8.after), channel_id=1, source_target_pairs={{0,32},{4,36},{8,40},{12,44},{16,48},{20,52},{24,56},{28,60},{32,0... | collective-permute-start | bytes 196616 | tf_op jit(solution)/shard_map/ppermute | solution.py:254
  42.5 9.1 %collective-permute-start.7 = (bf16[272,256]{1,0:T(8,128)(2,1)S(1)}, bf16[272,256]{1,0:T(8,128)(2,1)S(1)}, u32[]{:S(2)}, u32[]{:S(2)}) collective-permute-start(bf16[272,256]{1,0:T(8,128)(2,1)S(1)} %head_strip.1), channel_id=1, source_target_pairs={{1,0},{2,1},{3,2},{4,3},{5,4},{6,5},{7,6},{8,7},{9,8},{10,9},{11,1... | collective-permute-start | bytes 417800 | tf_op jit(solution)/shard_map/ppermute | solution.py:264
  44.6 6.9 %copy-start.4 = (s32[8,27]{1,0:T(8,128)S(1)}, s32[8,27]{1,0:T(8,128)}, u32[]{:S(2)}) copy-start(s32[8,27]{1,0:T(8,128)} %neighbors.1) | copy-start | bytes 2596
  44.6 6.9 %copy-start.5 = (s32[8]{0:T(128)S(1)}, s32[8]{0:T(128)}, u32[]{:S(2)}) copy-start(s32[8]{0:T(128)} %counts.1) | copy-start | bytes 100
  48.8 6.2 %collective-permute-start.5 = (bf16[2,128,128]{2,1,0:T(8,128)(2,1)S(1)}, bf16[2,128,128]{2,1,0:T(8,128)(2,1)S(1)}, u32[]{:S(2)}, u32[]{:S(2)}) collective-permute-start(bf16[2,128,128]{2,1,0:T(8,128)(2,1)S(1)} %level_state.9.after), channel_id=1, source_target_pairs={{0,64},{4,68},{8,72},{12,76},{16,80},{20,84},{24,88},{28,92},{32,9... | collective-permute-start | bytes 196616 | tf_op jit(solution)/shard_map/ppermute | solution.py:254
  55.2 8.1 %collective-permute-start.8 = (bf16[2,128,128]{2,1,0:T(8,128)(2,1)S(1)}, bf16[2,128,128]{2,1,0:T(8,128)(2,1)S(1)}, u32[]{:S(2)}, u32[]{:S(2)}) collective-permute-start(bf16[2,128,128]{2,1,0:T(8,128)(2,1)S(1)} %level_state.10.after), channel_id=1, source_target_pairs={{0,128},{4,132},{8,136},{12,140},{16,144},{20,148},{24,152},{28,15... | collective-permute-start | bytes 196616 | tf_op jit(solution)/shard_map/ppermute | solution.py:254
  63.5 12.1 %collective-permute-start.9 = (bf16[2,128,128]{2,1,0:T(8,128)(2,1)S(1)}, bf16[2,128,128]{2,1,0:T(8,128)(2,1)S(1)}, u32[]{:S(2)}, u32[]{:S(2)}) collective-permute-start(bf16[2,128,128]{2,1,0:T(8,128)(2,1)S(1)} %level_state.11.after), channel_id=1, source_target_pairs={{0,256},{4,260},{8,264},{12,268},{16,272},{20,276},{24,280},{28,28... | collective-permute-start | bytes 196616 | tf_op jit(solution)/shard_map/ppermute | solution.py:254
  72.8 2.8 %copy-start.2 = (bf16[2,128,1024]{2,1,0:T(8,128)(2,1)S(1)}, bf16[2,128,1024]{2,1,0:T(8,128)(2,1)}, u32[]{:S(2)}) copy-start(bf16[2,128,1024]{2,1,0:T(8,128)(2,1)} %expand.1) | copy-start | bytes 1572868
